TPU v7x, 128 devices: a whole 4x4x4 slice. The times are simulated.
128 devices in a mesh: sample: 32 (over x, z, core), feature: 4 (over y).
Axes of the slice: x: 4, y: 4, z: 4, core: 2. Of those that a mesh axis runs over, the one named last changes fastest.
Arguments:
- feat_values: float32 [65536, 2048], P('sample', 'feature'), may hold values from -0.6 to 0.6
- block_ids: int32 [512, 16], P('sample', 'feature'), may hold values from 0 to 8191
- fixed_weights: float32 [32768, 128], P('feature'), may hold values from -1.5 to 1.5
- labels: float32 [65536], P('sample'), may hold values from 0 to 1
- prior_scores: float32 [65536], P('sample'), may hold values from -3 to 3
- member_feats: float32 [65536, 128], P(('sample', 'feature')), may hold values from -1.8 to 1.8
- member_ids: int32 [65536], P(('sample', 'feature')), may hold values from 0 to 4095, as said below
- member_coefs: float32 [4096, 128], P(('sample', 'feature')), may hold values from -1.5 to 1.5
Outputs:
- new_weights: float32 [32768, 128], P('feature')
- new_coefs: float32 [4096, 128], P(('sample', 'feature'))
- total_scores: float32 [65536, 1], P(('sample', 'feature'))
Inputs may be any that keep to these rules, and one draw needn't show every extreme that they name: member_ids // 32 is the index along sample+feature of the device that owns the member; no member has more than 32 rows, and every member of some owner has exactly 32; at most 8 rows of one device belong to members of one owner, and every device has exactly 8 rows for some owner.
All inputs are finite; a program needn't handle non-finite values.
Results may differ from a plain program's by a relative error of at most 0.0003.
Values sent between devices are 32-bit elements; how exact they have to be, the bound alone decides.
No kernel may reach another device: no remote copies, remote signals or barrier semaphores. Data moves between devices by JAX's collectives and lax.ppermute only.
A program may use at most 128 MiB of HBM per device.

v0:
```python
import jax
import jax.numpy as jnp
from jax import lax
from jax.sharding import PartitionSpec as P

NEWTON = 2


STEP_SIZE = 0.5
FIXED_RIDGE = 0.1
MEMBER_RIDGE = 1.0
MEMBER_STEP = 0.5
HIGH = lax.Precision.HIGHEST


def partial_margin(tiled, block_ids, weights):
    chosen = weights[block_ids]
    local = jnp.einsum("trkb,tkb->tr", tiled, chosen, precision=HIGH).reshape(-1)
    return lax.psum(local, "feature")


def newton_update(weights, gradient, hessian):
    return weights - STEP_SIZE * (gradient + FIXED_RIDGE * weights) / (hessian + 1.0)


def member_solve(group_feats, weight, gradient_re):
    group = group_feats.shape[1]
    feat_width = group_feats.shape[2]
    scaled = group_feats * jnp.sqrt(weight)[:, :, None]
    small = (
        jnp.einsum("mgf,mhf->mgh", scaled, scaled, precision=HIGH)
        + MEMBER_RIDGE * jnp.eye(group, dtype=jnp.float32)[None]
    )
    projected = jnp.einsum("mgf,mf->mg", scaled, gradient_re, precision=HIGH)
    factor = jnp.linalg.cholesky(small)
    middle = lax.linalg.triangular_solve(factor, projected[:, :, None], left_side=True, lower=True)
    inner = lax.linalg.triangular_solve(
        factor, middle, left_side=True, lower=True, transpose_a=True
    )
    return gradient_re - jnp.einsum("mgf,mg->mf", scaled, inner[:, :, 0], precision=HIGH)


def shards(
    feat_values,
    block_ids,
    fixed_weights,
    labels,
    prior_scores,
    member_feats,
    member_ids,
    member_coefs,
):
    tile_count = block_ids.shape[0]
    slots_tile = block_ids.shape[1]
    block_width = fixed_weights.shape[1]
    shard_blocks = fixed_weights.shape[0]
    tiled = feat_values.reshape(tile_count, -1, slots_tile, block_width)
    margin = partial_margin(tiled, block_ids, fixed_weights)
    probs = jax.nn.sigmoid(margin + prior_scores)
    residual = (probs - labels).reshape(tile_count, -1)
    curvature = (probs * (1.0 - probs)).reshape(tile_count, -1)
    grad_tiles = jnp.einsum("trkb,tr->tkb", tiled, residual, precision=HIGH)
    hess_tiles = jnp.einsum("trkb,tr->tkb", tiled * tiled, curvature, precision=HIGH)
    stacked = jnp.stack([grad_tiles, hess_tiles]).reshape(2, -1, block_width)
    flat_ids = block_ids.reshape(-1)
    stats = jnp.zeros((2, shard_blocks, block_width), jnp.float32).at[:, flat_ids].add(stacked)
    totals = lax.psum(stats, "sample")
    new_weights = newton_update(fixed_weights, totals[0], totals[1])
    fixed_score = partial_margin(tiled, block_ids, new_weights)
    sample_count = lax.axis_size("sample")
    feature_count = lax.axis_size("feature")
    device_count = sample_count * feature_count
    rows_sample = labels.shape[0]
    send_rows = member_feats.shape[0]
    feat_width = member_feats.shape[1]
    member_count = member_coefs.shape[0]
    capacity = max(2, 2 * rows_sample // (feature_count * device_count))
    slot_total = device_count * capacity
    group = slot_total // member_count
    start_row = lax.axis_index("feature") * send_rows
    own_fixed = lax.dynamic_slice_in_dim(fixed_score, start_row, send_rows, 0)
    own_labels = lax.dynamic_slice_in_dim(labels, start_row, send_rows, 0)
    owner_of = member_ids // member_count
    row_range = jnp.arange(send_rows, dtype=jnp.int32)
    earlier = (owner_of[None, :] == owner_of[:, None]) & (row_range[None, :] < row_range[:, None])
    rank_owner = jnp.sum(earlier.astype(jnp.int32), axis=1)
    send_slots = owner_of * capacity + rank_owner
    local_member = jnp.remainder(member_ids, member_count).astype(jnp.float32)
    extras = jnp.stack([own_fixed, own_labels, local_member], axis=1)
    feat_buffer = jnp.zeros((slot_total, feat_width), jnp.float32).at[send_slots].set(member_feats)
    extra_buffer = (
        jnp.zeros((slot_total, 3), jnp.float32).at[:, 2].set(-1.0).at[send_slots].set(extras)
    )
    got_feats, got_extras = (
        lax.all_to_all(
            feat_buffer.reshape(device_count, capacity, feat_width),
            ("sample", "feature"),
            split_axis=0,
            concat_axis=0,
            tiled=True,
        ),
        lax.all_to_all(
            extra_buffer.reshape(device_count, capacity, 3),
            ("sample", "feature"),
            split_axis=0,
            concat_axis=0,
            tiled=True,
        ),
    )
    rows_feats = got_feats.reshape(slot_total, feat_width)
    rows_extra = got_extras.reshape(slot_total, 3)
    member_local = rows_extra[:, 2].astype(jnp.int32)
    sort_key = jnp.where(member_local >= 0, member_local, member_count)
    positions = jnp.arange(slot_total, dtype=jnp.int32)
    order = jnp.argsort(sort_key * slot_total + positions)
    sorted_member = sort_key[order]
    member_range = jnp.arange(member_count, dtype=jnp.int32)
    counts = jnp.sum((sort_key[:, None] == member_range[None, :]).astype(jnp.int32), axis=0)
    offsets = jnp.cumsum(counts) - counts
    clipped = jnp.minimum(sorted_member, member_count - 1)
    rank_in = positions - offsets[clipped]
    target = jnp.where(
        sorted_member < member_count, sorted_member * group + rank_in, member_count * group
    )
    grouped_rows = (
        jnp.full((member_count * group,), slot_total, jnp.int32).at[target].set(order, mode="drop")
    )
    padded_feats = jnp.concatenate([rows_feats, jnp.zeros((1, feat_width), jnp.float32)], axis=0)
    padded_extra = jnp.concatenate([rows_extra, jnp.zeros((1, 3), jnp.float32)], axis=0)
    group_feats = padded_feats[grouped_rows].reshape(member_count, group, feat_width)
    group_extra = padded_extra[grouped_rows].reshape(member_count, group, 3)
    live = (grouped_rows < slot_total).astype(jnp.float32).reshape(member_count, group)
    coefs = member_coefs
    for sweep in range(NEWTON):
        score = jnp.einsum("mgf,mf->mg", group_feats, coefs, precision=HIGH) + group_extra[:, :, 0]
        prob_now = jax.nn.sigmoid(score)
        error = (prob_now - group_extra[:, :, 1]) * live
        weight = prob_now * (1.0 - prob_now) * live
        gradient_re = (
            jnp.einsum("mgf,mg->mf", group_feats, error, precision=HIGH) + MEMBER_RIDGE * coefs
        )
        coefs = coefs - MEMBER_STEP * member_solve(group_feats, weight, gradient_re)
    group_final = jnp.einsum("mgf,mf->mg", group_feats, coefs, precision=HIGH) * live
    final = (
        jnp.zeros((slot_total + 1,), jnp.float32)
        .at[grouped_rows]
        .set(group_final.reshape(-1))[:slot_total]
    )
    returned = lax.all_to_all(
        final.reshape(device_count, capacity),
        ("sample", "feature"),
        split_axis=0,
        concat_axis=0,
        tiled=True,
    )
    member_score = returned.reshape(-1)[send_slots]
    total = own_fixed + member_score
    return (new_weights, coefs, total[:, None])


def solution(mesh):
    in_specs = (
        P("sample", "feature"),
        P("sample", "feature"),
        P("feature", None),
        P("sample"),
        P("sample"),
        P(("sample", "feature"), None),
        P(("sample", "feature")),
        P(("sample", "feature"), None),
    )
    out_specs = (P("feature", None), P(("sample", "feature"), None), P(("sample", "feature"), None))
    return jax.shard_map(shards, mesh=mesh, in_specs=in_specs, out_specs=out_specs, check_vma=False)
```

profile of v0, /device:TPU:1, one launch (start us, length us, event | category | flops | bytes accessed | tf_op | source)
XLA Modules:
  0.0 548.3 jit_solution(9729989409527750932)
XLA Ops:
  8.7 5.2 reshape.245
  14.1 6.7 %mul.86 = f32[16,128,4,128]{3,2,1,0:T(4,128)} multiply(f32[16,128,4,128]{3,2,1,0:T(4,128)} %reshape.245, f32[16,128,4,128]{3,2,1,0:T(4,128)} %reshape.245) | non-fusion elementwise | flops 1048576 | bytes 12582912 | tf_op jit(solution)/shard_map/mul | solution.py:63
  23.6 5.7 %fusion.6 = f32[16,1,128,1]{2,1,3,0:T(1,128)S(1)} fusion(f32[16,4,128,1]{2,3,1,0:T(1,128)S(1)} %bitcast.279, f32[16,128,4,128]{3,2,1,0:T(4,128)} %reshape.245), kind=kOutput, calls=%fused_computation.19 | convolution fusion | flops 12582912 | bytes 4235264 | tf_op jit(solution)/shard_map/trkb,tkb->tr/dot_general | solution.py:18
  29.3 9.7 %psum.21 = f32[2048]{0:T(1024)S(1)} all-reduce(f32[2048]{0:T(1024)S(1)} %bitcast.295), channel_id=1, replica_groups=mesh['sample'=32,'feature'=4] {'feature'}, use_global_device_ids=true, to_apply=%region_0.0 | all-reduce | flops 2048 | bytes 16384 | tf_op jit(solution)/shard_map/psum | solution.py:19
  39.0 4.3 fusion.2
  43.4 4.4 fusion
  47.9 5.5 %broadcast_in_dim.31 = f32[2,8192,128]{2,0,1:T(2,128)} broadcast(f32[]{:T(128)} %constant.124.clone.1), dimensions={} | broadcast | bytes 8388612 | tf_op jit(solution)/shard_map/broadcast_in_dim | solution.py:66
  53.4 6.7 %scatter_fusion = f32[2,8192,128]{2,0,1:T(2,128)} fusion(f32[2,8192,128]{2,0,1:T(2,128)} %broadcast_in_dim.31, s32[64]{0:T(128)S(1)} %fusion.52, f32[64,2,128]{2,1,0:T(2,128)S(1)} %maximum_bitcast_fusion), kind=kCustom, calls=%fused_computation.6 | custom fusion | flops 16384 | bytes 196864 | tf_op jit(solution)/shard_map/scatter-add | solution.py:66
  61.1 2.9 scatter_custom_fusion.1
  64.0 10.3 %all-to-all-start = ((f32[128,8,128]{2,1,0:T(8,128)}), f32[128,8,128]{2,1,0:T(8,128)S(1)}, u32[]{:S(2)}, u32[]{:S(2)}) async-start(f32[128,8,128]{2,1,0:T(8,128)} %bitcast.22), calls=%async_computation | async-start | bytes 1048576 | tf_op jit(solution)/shard_map/all_to_all | solution.py:95
  74.3 113.9 %all-reduce.4.cloned.1.call-done = f32[2,8192,128]{2,0,1:T(2,128)} async-done(((f32[2,8192,128]{2,0,1:T(2,128)}), f32[2,8192,128]{2,0,1:T(2,128)}) %all-reduce.4.cloned.1.call-update) | async-done | bytes 8388624 | tf_op jit(solution)/shard_map/psum | solution.py:67
  188.2 10.6 %fusion.54 = (f32[1,8192,128]{2,0,1:T(1,128)S(1)}, f32[1,8192,128]{2,0,1:T(1,128)S(1)}) fusion(f32[2,8192,128]{2,0,1:T(2,128)} %all-reduce.4.cloned.1.call-done), kind=kLoop, calls=%fused_computation.155 | loop fusion | flops 1048576 | bytes 16777216 | tf_op jit(solution)/shard_map/slice | solution.py:68
  198.8 2.8 divide_subtract_fusion
  204.5 5.7 %fusion.4 = f32[16,1,128,1]{2,1,3,0:T(1,128)S(1)} fusion(f32[16,4,128,1]{2,3,1,0:T(1,128)S(1)} %bitcast.278, f32[16,128,4,128]{3,2,1,0:T(4,128)} %reshape.245), kind=kOutput, calls=%fused_computation.17 | convolution fusion | flops 12582912 | bytes 4235264 | tf_op jit(solution)/shard_map/trkb,tkb->tr/dot_general | solution.py:18
  210.2 8.6 %psum.23 = f32[2048]{0:T(1024)S(1)} all-reduce(f32[2048]{0:T(1024)S(1)} %bitcast.294), channel_id=1, replica_groups=mesh['sample'=32,'feature'=4] {'feature'}, use_global_device_ids=true, to_apply=%region_5.6 | all-reduce | flops 2048 | bytes 16384 | tf_op jit(solution)/shard_map/psum | solution.py:19
  222.5 7.5 %all-to-all-start.1 = ((f32[128,8,3]{1,2,0:T(4,128)}), f32[128,8,3]{1,2,0:T(4,128)S(1)}, u32[]{:S(2)}, u32[]{:S(2)}) async-start(f32[128,8,3]{1,2,0:T(4,128)} %copy.93), calls=%async_computation.1 | async-start | bytes 524288 | tf_op jit(solution)/shard_map/all_to_all | solution.py:102
  230.0 11.3 %all-to-all-done.1 = f32[128,8,3]{1,2,0:T(4,128)S(1)} async-done(((f32[128,8,3]{1,2,0:T(4,128)}), f32[128,8,3]{1,2,0:T(4,128)S(1)}, u32[]{:S(2)}, u32[]{:S(2)}) %all-to-all-start.1) | async-done | bytes 12320 | tf_op jit(solution)/shard_map/all_to_all | solution.py:102
  244.5 4.4 sort.17
  248.8 4.5 gather_fusion.2
  253.7 3.5 compare_reduce_fusion.24
  257.2 4.7 select_reduce_fusion.2
  261.9 15.7 %select_select_fusion = s32[1024]{0:T(1024)S(1)} fusion(pred[1024]{0:T(1024)(128)(4,1)S(1)} %get-tuple-element.46, pred[1024]{0:T(1024)(128)(4,1)S(1)} %get-tuple-element.23, pred[1024]{0:T(1024)(128)(4,1)S(1)} %get-tuple-element.28, pred[1024]{0:T(1024)(128)(4,1)S(1)} %get-tuple-element.27, pred[1024]{0:T(1024)(128)(4,1)S(1)} %get-tuple-element.26, ...), kind=kLoop, calls=%fused_computation.132 | loop fusion | flops 25600 | bytes 33892 | tf_op jit(solution)/shard_map/gather | solution.py:121
  278.4 4.5 scatter_custom_fusion.3
  282.9 2.8 gather_fusion.4
  286.5 2.8 gather_fusion.3
  293.5 93.8 %custom-call.12 = f32[32,32,32]{2,1,0:T(8,128)S(1)} custom-call(f32[32,32,32]{2,1,0:T(8,128)S(1)} %fusion.12), custom_call_target="Cholesky" | custom-call | tf_op jit(solution)/shard_map/jit(cholesky)/cholesky | solution.py:35
  388.0 12.5 %custom-call.14 = f32[32,1,32,32]{0,2,3,1:T(8,128)S(1)} custom-call(f32[32,1,32,32]{0,3,2,1:T(8,128)S(1)} %select_bitcast_fusion.1), custom_call_target="InvertDiagBlocksLowerTriangular" | custom-call | tf_op jit(solution)/shard_map/triangular_solve/custom-call.2 | solution.py:37
  407.1 93.8 %custom-call.15 = f32[32,32,32]{2,1,0:T(8,128)S(1)} custom-call(f32[32,32,32]{2,1,0:T(8,128)S(1)} %fusion.11), custom_call_target="Cholesky" | custom-call | tf_op jit(solution)/shard_map/jit(cholesky)/cholesky | solution.py:35
  501.7 12.7 %custom-call.17 = f32[32,1,32,32]{0,2,3,1:T(8,128)S(1)} custom-call(f32[32,1,32,32]{0,3,2,1:T(8,128)S(1)} %select_bitcast_fusion), custom_call_target="InvertDiagBlocksLowerTriangular" | custom-call | tf_op jit(solution)/shard_map/triangular_solve/custom-call.2 | solution.py:37
  518.0 4.3 scatter_custom_fusion.4
  523.1 3.9 all-to-all-start.2
  527.0 9.9 %all-to-all-done.2 = f32[128,1,8]{2,1,0:T(1,128)S(1)} async-done(((f32[128,1,8]{2,1,0:T(1,128)}), f32[128,1,8]{2,1,0:T(1,128)S(1)}, u32[]{:S(2)}, u32[]{:S(2)}) %all-to-all-start.2) | async-done | bytes 4128 | tf_op jit(solution)/shard_map/all_to_all | solution.py:149
  (112 shorter events, 38.1 us)
Async XLA Ops:
  7.2 181.0 %all-reduce.4.cloned.1.call-start = ((), (), s32[]{:S(2)}) async-start(), calls=%async_computation.3 | async-start | bytes 16777216 | tf_op jit(solution)/shard_map/psum | solution.py:67
  20.8 18.2 %copy-start.3 = (f32[2048]{0:T(1024)S(1)}, f32[2048]{0:T(1024)}, u32[]{:S(2)}) copy-start(f32[2048]{0:T(1024)} %param.18) | copy-start | bytes 24580
  20.8 18.2 %copy-start.4 = (f32[2048]{0:T(1024)S(1)}, f32[2048]{0:T(1024)}, u32[]{:S(2)}) copy-start(f32[2048]{0:T(1024)} %param.19) | copy-start | bytes 24580
  60.1 0.7 copy-start.5
  64.0 158.5 %all-to-all-start = ((f32[128,8,128]{2,1,0:T(8,128)}), f32[128,8,128]{2,1,0:T(8,128)S(1)}, u32[]{:S(2)}, u32[]{:S(2)}) async-start(f32[128,8,128]{2,1,0:T(8,128)} %bitcast.22), calls=%async_computation | async-start | bytes 1048576 | tf_op jit(solution)/shard_map/all_to_all | solution.py:95
  188.2 10.6 %copy-start = (f32[8192,128]{1,0:T(8,128)S(1)}, f32[8192,128]{1,0:T(8,128)}, u32[]{:S(2)}) copy-start(f32[8192,128]{1,0:T(8,128)} %param.17) | copy-start | bytes 12582916
  201.7 17.3 %copy-start.6 = (f32[3]{0:T(128)S(1)}, f32[3]{0:T(128)}, u32[]{:S(2)}) copy-start(f32[3]{0:T(128)} %constant.136.clone.1) | copy-start | bytes 40
  222.5 18.8 %all-to-all-start.1 = ((f32[128,8,3]{1,2,0:T(4,128)}), f32[128,8,3]{1,2,0:T(4,128)S(1)}, u32[]{:S(2)}, u32[]{:S(2)}) async-start(f32[128,8,3]{1,2,0:T(4,128)} %copy.93), calls=%async_computation.1 | async-start | bytes 524288 | tf_op jit(solution)/shard_map/all_to_all | solution.py:102
  285.8 3.6 copy-start.1
  517.0 24.2 %copy-start.2 = (f32[32,128]{1,0:T(8,128)}, f32[32,128]{1,0:T(8,128)S(1)}, u32[]{:S(2)}) copy-start(f32[32,128]{1,0:T(8,128)S(1)} %multiply_subtract_fusion) | copy-start | bytes 49156
  523.1 13.8 %all-to-all-start.2 = ((f32[128,1,8]{2,1,0:T(1,128)}), f32[128,1,8]{2,1,0:T(1,128)S(1)}, u32[]{:S(2)}, u32[]{:S(2)}) async-start(f32[128,1,8]{2,1,0:T(1,128)} %bitcast.149), calls=%async_computation.2 | async-start | bytes 131072 | tf_op jit(solution)/shard_map/all_to_all | solution.py:149
Sparse Core Ops, SparseCore 0:
  60.3 127.8 all-reduce.3
where the time goes:
time: 558 us; the launch traced here: 548 us
  other arithmetic  273 us (49%)
  waiting for transfers between devices  135 us (24%)
  local copies, waits for them, and re-layouts  53.2 us (10%)
  matrix products  32.7 us (6%)
  starting transfers between devices  21.6 us (4%)
  blocking collectives  18.2 us (3%)
  between operations  14.8 us (3%)
    another operation x7, other arithmetic, member_solve(): factor = jnp.linalg.cholesky(small)  188 us
    psum x1, waiting for transfers between devices, shards(): totals = lax.psum(stats, 'sample')  114 us
    another operation x5, other arithmetic, member_solve(): lax.linalg.triangular_solve(factor, middle, left_side=True, lower=True, t...  25.6 us
    gather x3, other arithmetic, shards(): rank_in = positions - offsets[clipped]  23.9 us
    psum x2, blocking collectives, partial_margin(): return lax.psum(local, 'feature')  18.2 us
    dot_general x2, matrix products, partial_margin(): jnp.einsum('trkb,tkb->tr', tiled, chosen, precision=HIGH).reshape(-1)  11.4 us
    all_to_all x1, waiting for transfers between devices, shards(): lax.all_to_all(extra_buffer.reshape(device_count, capacity, 3), ('sample'...  11.3 us
  transfers between devices with their start and end apart: 4, of which 3 were waited for; matrix products, arithmetic and copies ran while one was open for 5% of the time, Pallas kernels for 0%

commit v1 on v0

v1 whole, which is shorter than its diff:
```python
import functools

import jax
import jax.numpy as jnp
from jax import lax
from jax.experimental import pallas as pl
from jax.experimental.pallas import tpu as pltpu
from jax.sharding import PartitionSpec as P

STEP_SIZE = 0.5
FIXED_RIDGE = 0.1
MEMBER_RIDGE = 1.0
MEMBER_STEP = 0.5

F32 = jnp.float32
BF16 = jnp.bfloat16
I32 = jnp.int32

TILES = 16
SLOTS = 4
TILE = 128
BLK = 128
ENTRIES = TILES * SLOTS
PACKET = ENTRIES + 8
DEVICES = 128
SAMPLES = 32
FEATURES = 4
CAP = 8
OWN = 512
POS = DEVICES * CAP
MEM = 32
GROUP = 32

NN = (((1,), (0,)), ((), ()))
NT = (((1,), (1,)), ((), ()))


def split(x, parts):
    out = []
    for _ in range(parts - 1):
        top = x.astype(BF16)
        out.append(top)
        x = x - top.astype(F32)
    out.append(x.astype(BF16))
    return out


def dot(a, b, dims=NN):
    return lax.dot_general(a, b, dims, preferred_element_type=F32)


def dot_right(mask, x, parts, dims=NN):
    return functools.reduce(jnp.add, [dot(mask, piece, dims) for piece in split(x, parts)])


def dot_left(x, mask, parts, dims=NN):
    return functools.reduce(jnp.add, [dot(piece, mask, dims) for piece in split(x, parts)])


def iota(shape, dim):
    return lax.broadcasted_iota(I32, shape, dim)


def onehot(cond):
    return jnp.where(cond, 1.0, 0.0).astype(F32)


def params(mib):
    return pltpu.CompilerParams(vmem_limit_bytes=mib << 20)


def full(shape):
    return pl.BlockSpec(shape, lambda *_: (0,) * len(shape))


def margin_kernel(ids, feats, weights, out, chosen, sems):
    step = pl.program_id(0)

    @pl.when(step == 0)
    def _():
        copies = [
            pltpu.make_async_copy(
                weights.at[pl.ds(ids[j], 1)], chosen.at[pl.ds(j, 1)], sems.at[j]
            )
            for j in range(ENTRIES)
        ]
        for copy in copies:
            copy.start()
        for copy in copies:
            copy.wait()

    tiles = feats.shape[0] // TILE
    rows = []
    for t in range(tiles):
        w = chosen[pl.ds((step * tiles + t) * SLOTS, SLOTS), :]
        total = None
        for k in range(SLOTS):
            term = feats[t * TILE : (t + 1) * TILE, k * BLK : (k + 1) * BLK] * w[k : k + 1, :]
            total = term if total is None else total + term
        rows.append(jnp.sum(total.T, axis=0, keepdims=True))
    out[...] = jnp.concatenate(rows, axis=0)


def first_margin(ids, feats, weights):
    steps = 2
    return pl.pallas_call(
        margin_kernel,
        grid_spec=pltpu.PrefetchScalarGridSpec(
            num_scalar_prefetch=1,
            grid=(steps,),
            in_specs=[
                pl.BlockSpec((TILES * TILE // steps, SLOTS * BLK), lambda i, s: (i, 0)),
                pl.BlockSpec(memory_space=pl.ANY),
            ],
            out_specs=[
                pl.BlockSpec((TILES // steps, TILE), lambda i, s: (i, 0)),
                full((ENTRIES, BLK)),
            ],
            scratch_shapes=[pltpu.SemaphoreType.DMA((ENTRIES,))],
        ),
        out_shape=[
            jax.ShapeDtypeStruct((TILES, TILE), F32),
            jax.ShapeDtypeStruct((ENTRIES, BLK), F32),
        ],
        compiler_params=params(16),
        name="first_margin",
    )(ids, feats, weights)


def stats_kernel(m0, m1, m2, m3, prior, labels, ids, feats, out):
    step = pl.program_id(0)
    tiles = feats.shape[0] // TILE
    at = pl.ds(step * tiles, tiles)
    margin = (m0[at, :] + m1[at, :]) + (m2[at, :] + m3[at, :])
    probs = jax.nn.sigmoid(margin + prior[at, :])
    residual = (probs - labels[at, :]).T
    curvature = (probs * (1.0 - probs)).T
    rows = []
    for t in range(tiles):
        r = jnp.broadcast_to(residual[:, t : t + 1], (TILE, BLK))
        c = jnp.broadcast_to(curvature[:, t : t + 1], (TILE, BLK))
        for k in range(SLOTS):
            x = feats[t * TILE : (t + 1) * TILE, k * BLK : (k + 1) * BLK]
            grad = jnp.sum(x * r, axis=0, keepdims=True)
            hess = jnp.sum(x * x * c, axis=0, keepdims=True)
            rows.append(jnp.concatenate([grad, hess], axis=1))
    out[pl.ds(step * tiles * SLOTS, tiles * SLOTS), :] = jnp.concatenate(rows, axis=0)

    @pl.when(step == 0)
    def _():
        out[ENTRIES:PACKET, :] = ids[...]


def own_stats(margins, prior, labels, ids, feats):
    steps = 2
    small = full((TILES, TILE))
    return pl.pallas_call(
        stats_kernel,
        grid=(steps,),
        in_specs=[small] * 6
        + [
            full((8, 2 * BLK)),
            pl.BlockSpec((TILES * TILE // steps, SLOTS * BLK), lambda i: (i, 0)),
        ],
        out_specs=full((PACKET, 2 * BLK)),
        out_shape=jax.ShapeDtypeStruct((PACKET, 2 * BLK), F32),
        compiler_params=params(16),
        name="own_stats",
    )(*margins, prior, labels, ids, feats)


def second_kernel(packets, own_ids, chosen, feats, place, owners, out):
    lane = iota((1, 128), 1)
    acc = None
    for pair in range(SAMPLES // 2):
        a, b = 2 * pair, 2 * pair + 1
        ids = jnp.where(
            lane < ENTRIES,
            packets[a, ENTRIES : ENTRIES + 1, 0:128],
            packets[b, ENTRIES : ENTRIES + 1, 0:128],
        )
        mask = onehot(own_ids[...] == ids).astype(BF16)
        both = jnp.concatenate([packets[a, 0:ENTRIES, :], packets[b, 0:ENTRIES, :]], axis=0)
        term = dot_right(mask, both, 2)
        acc = term if acc is None else acc + term
    w = chosen[...]
    w = w - STEP_SIZE * (acc[:, :BLK] + FIXED_RIDGE * w) / (acc[:, BLK:] + 1.0)
    ones = jnp.ones((BLK, 128), BF16)
    result = None
    pair = 2 * TILE
    for step in range(TILES // 2):
        parts = []
        for t in (2 * step, 2 * step + 1):
            total = None
            for k in range(SLOTS):
                x = feats[t * TILE : (t + 1) * TILE, k * BLK : (k + 1) * BLK]
                term = x * w[t * SLOTS + k : t * SLOTS + k + 1, :]
                total = term if total is None else total + term
            parts.append(total)
        margin = dot_left(jnp.concatenate(parts, axis=0), ones, 2)
        placed = margin * place[step * pair : (step + 1) * pair, :]
        mask = onehot(
            iota((DEVICES, pair), 0) == owners[0:1, step * pair : (step + 1) * pair]
        ).astype(BF16)
        term = dot_right(mask, placed, 2)
        result = term if result is None else result + term
    out[...] = result


def second_margin(packets, own_ids, chosen, feats, place, owners):
    return pl.pallas_call(
        second_kernel,
        out_shape=jax.ShapeDtypeStruct((DEVICES, 128), F32),
        compiler_params=params(24),
        name="second_margin",
    )(packets, own_ids, chosen, feats, place, owners)


def weights_kernel(ids, order, packets, weights, out, grad, hess):
    step = pl.program_id(0)

    @pl.when(step == 0)
    def _():
        grad[...] = jnp.zeros_like(grad)
        hess[...] = jnp.zeros_like(hess)

        def source(s, carry):
            at = order[s]
            for j in range(ENTRIES):
                row = pl.ds(ids[at * ENTRIES + j], 1)
                grad[row, :] += packets[at, j : j + 1, 0:BLK]
                hess[row, :] += packets[at, j : j + 1, BLK : 2 * BLK]
            return carry

        lax.fori_loop(0, SAMPLES, source, 0)

    rows = weights.shape[0]
    at = pl.ds(step * rows, rows)
    w = weights[...]
    out[...] = w - STEP_SIZE * (grad[at, :] + FIXED_RIDGE * w) / (hess[at, :] + 1.0)


def all_weights(ids, order, packets, weights):
    blocks = weights.shape[0]
    steps = 8
    piece = pl.BlockSpec((blocks // steps, BLK), lambda i, *_: (i, 0))
    return pl.pallas_call(
        weights_kernel,
        grid_spec=pltpu.PrefetchScalarGridSpec(
            num_scalar_prefetch=2,
            grid=(steps,),
            in_specs=[full((SAMPLES, PACKET, 2 * BLK)), piece],
            out_specs=piece,
            scratch_shapes=[pltpu.VMEM((blocks, BLK), F32), pltpu.VMEM((blocks, BLK), F32)],
        ),
        out_shape=jax.ShapeDtypeStruct((blocks, BLK), F32),
        compiler_params=params(24),
        name="all_weights",
    )(ids, order, packets, weights)


def pack_kernel(slots, feats, labels, members, out):
    at = iota((POS, OWN), 0)
    slot = slots[...]
    rows = dot_right(onehot(at == slot).astype(BF16), feats[...], 3)
    out[:, 0:CAP, :] = rows.reshape(DEVICES, CAP, 128)
    owner = slot // CAP
    extra = dot_right(onehot(at == owner * CAP).astype(BF16), labels[...], 3)
    extra += dot_right(onehot(at == owner * CAP + 1).astype(BF16), members[...], 1)
    out[:, CAP : 2 * CAP, :] = extra.reshape(DEVICES, CAP, 128)


def pack_rows(slots, feats, labels, members):
    return pl.pallas_call(
        pack_kernel,
        out_shape=jax.ShapeDtypeStruct((DEVICES, 2 * CAP, 128), F32),
        compiler_params=params(24),
        name="pack_rows",
    )(slots, feats, labels, members)


def spread(block, source):
    group = iota(block.shape, 1) // MEM
    out = None
    for g in range(4):
        shift = (g - source) % 4
        moved = pltpu.roll(block, MEM * shift, 1) if shift else block
        out = moved if out is None else jnp.where(group == g, moved, out)
    return out


def group_kernel(rows, coefs, gram, score, label, live, member, rank, turned, diag):
    lab_parts, mem_parts = [], []
    sub, lane = iota((128, 128), 0), iota((128, 128), 1)
    for b in range(8):
        extra = rows[16 * b : 16 * (b + 1), CAP : 2 * CAP, :].reshape(128, 128)
        first = (lane // CAP) * CAP
        lab_parts.append(jnp.sum(jnp.where(sub == first, extra, 0.0), axis=0, keepdims=True))
        mem_parts.append(jnp.sum(jnp.where(sub == first + 1, extra, 0.0), axis=0, keepdims=True))
    lab = jnp.concatenate(lab_parts, axis=1)
    mem = jnp.concatenate(mem_parts, axis=1).astype(I32) - 1
    member[...] = mem
    few = onehot(iota((MEM, POS), 0) == mem)
    before = onehot(sub < lane).astype(BF16)
    ones = jnp.ones((128, 128), BF16)
    carry = jnp.zeros((MEM, 128), F32)
    ranks = []
    for b in range(8):
        part = few[:, 128 * b : 128 * (b + 1)]
        half = part.astype(BF16)
        count = dot(half, before) + carry
        carry = carry + dot(half, ones)
        ranks.append(jnp.sum(part * count, axis=0, keepdims=True))
    rnk = jnp.concatenate(ranks, axis=1).astype(I32)
    rank[...] = rnk
    by_rank = onehot((iota((GROUP, POS), 0) == rnk) & (mem >= 0))
    by_member = onehot((iota((128, POS), 0) % MEM) == mem).astype(BF16)
    label[...] = dot_left(by_rank * lab, by_member, 3, NT)
    live[...] = dot(by_rank.astype(BF16), by_member, NT)
    target = jnp.where(mem >= 0, rnk * MEM + mem, -1)
    feats = rows[:, 0:CAP, :].reshape(POS, 128).T
    pieces = split(feats, 3)
    for b in range(4):
        goal = onehot(iota((256, POS), 0) + 256 * b == target).astype(BF16)
        moved = dot(pieces[0], goal, NT) + dot(pieces[1], goal, NT) + dot(pieces[2], goal, NT)
        turned[0, :, 256 * b : 256 * (b + 1)] = moved
    x = turned[0]
    for p in range(1, 4):
        turned[p] = pltpu.roll(x, POS - MEM * p, 1)
    c = coefs[...].T
    own = jnp.sum(x * jnp.concatenate([c] * 8, axis=1), axis=0, keepdims=True)
    own = jnp.where(iota((GROUP, POS), 1) // MEM == iota((GROUP, POS), 0), own, 0.0)
    folded = own[:, 0:128]
    for b in range(1, 8):
        folded = folded + own[:, 128 * b : 128 * (b + 1)]
    folded = folded + pltpu.roll(folded, 64, 1)
    score[...] = folded + pltpu.roll(folded, 32, 1)
    for delta in range(GROUP // 2 + 1):
        p, q = delta % 4, delta // 4
        for b in range(8):
            o = (b + q) % 8
            prod = turned[0, :, 128 * b : 128 * (b + 1)] * turned[p, :, 128 * o : 128 * (o + 1)]
            diag[delta : delta + 1, 128 * b : 128 * (b + 1)] = jnp.sum(prod, axis=0, keepdims=True)
    for delta in range(GROUP // 2 + 1, GROUP):
        diag[delta : delta + 1, :] = pltpu.roll(
            jnp.broadcast_to(diag[GROUP - delta : GROUP - delta + 1, :], (8, POS)), POS - MEM * delta, 1
        )[0:1, :]
    for b in range(8):
        block = diag[:, 128 * b : 128 * (b + 1)]
        for p in range(4):
            i = 4 * b + p
            wide = spread(block, p)
            gram[i] = pltpu.roll(wide, i, 0) if i else wide


def group_rows(rows, coefs):
    small = jax.ShapeDtypeStruct((GROUP, 128), F32)
    line = jax.ShapeDtypeStruct((1, POS), I32)
    return pl.pallas_call(
        group_kernel,
        out_shape=[
            jax.ShapeDtypeStruct((GROUP, GROUP, 128), F32),
            small,
            small,
            small,
            line,
            line,
        ],
        scratch_shapes=[pltpu.VMEM((4, 128, POS), F32), pltpu.VMEM((GROUP, POS), F32)],
        compiler_params=params(32),
        name="group_rows",
    )(rows, coefs)


def gram_times(gram, v):
    out = None
    for i in range(GROUP):
        term = gram[i] * v[i : i + 1, :]
        out = term if out is None else out + term
    return out


def solve_kernel(parts, gram, score, label, live, member, rank, back, steps, work):
    sub, lane = iota((128, 128), 0), iota((128, 128), 1)
    got = parts[...]
    fixed = []
    for b in range(8):
        keep = sub // FEATURES == 4 * b + lane // 32
        fixed.append(jnp.sum(jnp.where(keep, got, 0.0), axis=0, keepdims=True))
    fixed = jnp.concatenate(fixed, axis=1)
    mem = member[...]
    by_rank = onehot((iota((GROUP, POS), 0) == rank[...]) & (mem >= 0))
    by_member = onehot((iota((128, POS), 0) % MEM) == mem).astype(BF16)
    offset = dot_left(by_rank * fixed, by_member, 2, NT)
    alive = live[...]
    y = label[...]
    s = score[...]
    at = iota((GROUP, 128), 0)
    steps_total = None
    for sweep in range(2):
        p = jax.nn.sigmoid(s + offset)
        error = (p - y) * alive
        d = jnp.sqrt(p * (1.0 - p) * alive)
        b = d * (gram_times(gram, error) + s)
        for i in range(GROUP):
            row = gram[i] * (d * d[i : i + 1, :])
            work[i] = row + onehot(at == i)
        for k in range(GROUP):
            row = work[k]
            inverse = 1.0 / row[k : k + 1, :]
            scaled = jnp.where(at == k, 1.0 - inverse, row * inverse)
            b = b - b[k : k + 1, :] * scaled
            for i in range(k + 1, GROUP):
                work[i] = work[i] - row[i : i + 1, :] * scaled
        u = error - d * b
        s = s - MEMBER_STEP * (gram_times(gram, u) + MEMBER_RIDGE * s)
        steps_total = u * 0.25 if sweep == 0 else steps_total + u * 0.5
    steps[...] = steps_total
    final = (s + offset) * 0.25
    scores = jnp.sum(by_rank * dot_left(final, by_member, 2), axis=0, keepdims=True)
    for b in range(8):
        line = jnp.broadcast_to(scores[:, 128 * b : 128 * (b + 1)], (16, 128))
        back[16 * b : 16 * (b + 1), :] = jnp.where(
            iota((16, 128), 1) // CAP == iota((16, 128), 0), line, 0.0
        )


def solve_members(parts, gram, score, label, live, member, rank):
    return pl.pallas_call(
        solve_kernel,
        out_shape=[
            jax.ShapeDtypeStruct((DEVICES, 128), F32),
            jax.ShapeDtypeStruct((GROUP, 128), F32),
        ],
        scratch_shapes=[pltpu.VMEM((GROUP, GROUP, 128), F32)],
        compiler_params=params(16),
        name="solve_members",
    )(parts, gram, score, label, live, member, rank)


def coefs_kernel(rows, coefs, steps, member, rank, out):
    mem = member[...]
    by_rank = onehot((iota((GROUP, POS), 0) == rank[...]) & (mem >= 0))
    by_member = onehot((iota((128, POS), 0) % MEM) == mem)
    line = jnp.sum(
        by_rank * dot_left(steps[...] * 0.25, by_member.astype(BF16), 2), axis=0, keepdims=True
    )
    weighted = split(by_member[0:MEM, :] * line, 2)
    feats = split(rows[:, 0:CAP, :].reshape(POS, 128), 2)
    moved = dot(weighted[0], feats[0]) + dot(weighted[0], feats[1]) + dot(weighted[1], feats[0])
    out[...] = 0.25 * coefs[...] - moved


def new_coefs(rows, coefs, steps, member, rank):
    return pl.pallas_call(
        coefs_kernel,
        out_shape=jax.ShapeDtypeStruct((MEM, 128), F32),
        compiler_params=params(16),
        name="new_coefs",
    )(rows, coefs, steps, member, rank)


def total_kernel(back, slots, out):
    slot = slots[...]
    mask = onehot(iota((DEVICES, OWN), 0) == slot // CAP).astype(BF16)
    moved = dot_left(back[...].T, mask, 2)
    keep = (iota((128, OWN), 0) % CAP) == slot % CAP
    out[...] = jnp.sum(jnp.where(keep, moved, 0.0), axis=0, keepdims=True)


def total_rows(back, slots):
    return pl.pallas_call(
        total_kernel,
        out_shape=jax.ShapeDtypeStruct((1, OWN), F32),
        compiler_params=params(16),
        name="total_rows",
    )(back, slots)


def ring_feature(value):
    pairs = [[(i, (i + k) % FEATURES) for i in range(FEATURES)] for k in range(FEATURES)]
    return [value] + [lax.ppermute(value, "feature", pairs[k]) for k in (1, 3, 2)]


def sample_pairs(shift, first):
    pairs = []
    for i in range(SAMPLES):
        x, z, core = i // 8, (i // 2) % 4, i % 2
        if (core == 0) == first:
            z = (z + shift) % 4
        else:
            x = (x + shift) % 4
        pairs.append((i, (x * 4 + z) * 2 + core))
    return pairs


def gather_sample(value):
    for first in (True, False):
        value = jnp.concatenate(
            [value]
            + [lax.ppermute(value, "sample", sample_pairs(k, first)) for k in (1, 2, 3)],
            axis=0,
        )
    other = lax.ppermute(value, "sample", [(i, i ^ 1) for i in range(SAMPLES)])
    return jnp.concatenate([value, other], axis=0)


def gathered_order():
    me = lax.axis_index("sample")
    x, z, core = me // 8, (me // 2) % 4, me % 2
    source = jnp.arange(SAMPLES, dtype=I32)
    xs, zs, cs = source // 8, (source // 2) % 4, source % 2
    along_x, along_z = (x - xs) % 4, (z - zs) % 4
    late = jnp.where(cs == 0, along_x, along_z)
    early = jnp.where(cs == 0, along_z, along_x)
    return (jnp.where(cs == core, 0, 16) + late * 4 + early).astype(I32)


def exchange(value):
    return lax.all_to_all(value, ("sample", "feature"), split_axis=0, concat_axis=0, tiled=True)


def shards(
    feat_values,
    block_ids,
    fixed_weights,
    labels,
    prior_scores,
    member_feats,
    member_ids,
    member_coefs,
):
    flat_ids = block_ids.reshape(-1)
    float_ids = flat_ids.astype(F32)
    feature = lax.axis_index("feature")

    owner = member_ids // MEM
    span = jnp.arange(OWN, dtype=I32)
    earlier = (owner[None, :] == owner[:, None]) & (span[None, :] < span[:, None])
    rank = jnp.sum(earlier.astype(I32), axis=1)
    slots = owner * CAP + rank

    margin, chosen = first_margin(flat_ids, feat_values, fixed_weights)
    margins = ring_feature(margin)

    ring = ring_feature(slots)
    shift = (0, 1, 3, 2)
    quarter = jnp.arange(FEATURES, dtype=I32)
    every = functools.reduce(
        jnp.add,
        [
            jnp.where((quarter == (feature - k) % FEATURES)[:, None], r[None, :], 0)
            for k, r in zip(shift, ring)
        ],
    )
    lanes = jnp.arange(128, dtype=I32)
    column = (quarter[:, None] * CAP + every % CAP).reshape(-1)
    place = (lanes[None, :] % 32 == column[:, None]).astype(F32)
    owners = (every // CAP).reshape(1, -1)

    id_rows = jnp.tile(float_ids[None, :], (8, 4))
    packet = own_stats(
        margins, prior_scores.reshape(TILES, TILE), labels.reshape(TILES, TILE), id_rows, feat_values
    )

    own_labels = lax.dynamic_slice_in_dim(labels, feature * OWN, OWN, 0)
    mine = lanes[None, :] % CAP == rank[:, None]
    label_rows = jnp.where(mine, own_labels[:, None], 0.0)
    member_rows = jnp.where(mine, (member_ids % MEM + 1).astype(F32)[:, None], 0.0)
    packed = pack_rows(slots[None, :], member_feats, label_rows, member_rows)
    packed, packet = lax.optimization_barrier((packed, packet))
    rows = exchange(packed)
    packets = gather_sample(packet[None])

    gram, score, label, live, member, rank_in = group_rows(rows, jnp.tile(member_coefs, (4, 1)))

    own_ids = jnp.broadcast_to(float_ids[:, None], (ENTRIES, 128))
    partial = second_margin(packets, own_ids, chosen, feat_values, place, owners)
    parts = exchange(partial[:, None, :])[:, 0, :]

    all_ids = packets[:, ENTRIES, :ENTRIES].astype(I32).reshape(-1)
    weights = all_weights(all_ids, gathered_order(), packets, fixed_weights)

    back, steps = solve_members(parts, gram, score, label, live, member, rank_in)
    returned = exchange(back[:, None, :])[:, 0, :]
    coefs = new_coefs(rows, member_coefs, steps, member, rank_in)
    total = total_rows(returned, slots[None, :])
    return (weights, coefs, total.reshape(OWN, 1))


def solution(mesh):
    both = ("sample", "feature")
    in_specs = (
        P("sample", "feature"),
        P("sample", "feature"),
        P("feature", None),
        P("sample"),
        P("sample"),
        P(both, None),
        P(both),
        P(both, None),
    )
    out_specs = (P("feature", None), P(both, None), P(both, None))
    return jax.shard_map(shards, mesh=mesh, in_specs=in_specs, out_specs=out_specs, check_vma=False)
```

time: 558 us -> 121 us (0.22); the launches traced: 548 us -> 120 us
  other arithmetic: 273 us -> 1.12 us
  waiting for transfers between devices: 135 us -> 22.6 us
  matrix products: 32.7 us -> 0 us
  Pallas kernels: 0 us -> 32.7 us
  local copies, waits for them, and re-layouts: 53.2 us -> 23.2 us
  blocking collectives: 18.2 us -> 0 us
  starting transfers between devices: 21.6 us -> 39.6 us
  between operations: 14.8 us -> 0.96 us
    another operation x16 -> x0, other arithmetic: 214 us -> none  [the longest x7 188 us: member_solve(): factor = jnp.linalg.cholesky(small)]
    psum x1 -> x0, waiting for transfers between devices: 114 us -> none  [shards(): totals = lax.psum(stats, 'sample')]
    pallas_call x0 -> x9, Pallas kernels: none -> 32.7 us  [the longest x1 15.7 us: all_weights(): pl.pallas_call(weights_kernel, grid_spec=pltpu.PrefetchScalarGridSpec(num...]
    dot_general x15 -> x0, matrix products: 29.7 us -> none  [the longest x2 11.4 us: partial_margin(): jnp.einsum('trkb,tkb->tr', tiled, chosen, precision=HIGH).reshape(-1)]
    gather x6 -> x0, other arithmetic: 23.9 us -> none  [the longest x3 23.9 us: shards(): rank_in = positions - offsets[clipped]]
    ppermute x0 -> x13, starting transfers between devices: none -> 23.5 us  [the longest x6 10.6 us: gather_sample(): lax.ppermute(value, 'sample', sample_pairs(k, first))]
    gather x9 -> x0, local copies, waits for them, and re-layouts: 19.7 us -> none  [the longest x2 5.61 us: partial_margin(): chosen = weights[block_ids]]
    unnamed x17 -> x45, local copies, waits for them, and re-layouts: 1.96 us -> 20.7 us
  transfers between devices with their start and end apart: 4 -> 16, of which waited for: 3 -> 6; matrix products, arithmetic and copies ran while one was open for 5% -> 6% of each run, Pallas kernels for 0% -> 22%
where the time goes in v1:
time: 121 us; the launch traced here: 120 us
  starting transfers between devices  39.6 us (33%)
  Pallas kernels  32.7 us (27%)
  local copies, waits for them, and re-layouts  23.2 us (19%)
  waiting for transfers between devices  22.6 us (19%)
    unnamed x45, local copies, waits for them, and re-layouts  20.7 us
    all_to_all x3, waiting for transfers between devices, exchange(): lax.all_to_all(value, ('sample', 'feature'), split_axis=0, concat_axis=0,...  17.2 us
    all_to_all x3, starting transfers between devices, exchange(): lax.all_to_all(value, ('sample', 'feature'), split_axis=0, concat_axis=0,...  16.2 us
    pallas_call x1, Pallas kernels, all_weights(): pl.pallas_call(weights_kernel, grid_spec=pltpu.PrefetchScalarGridSpec(num...  15.7 us
    ppermute x6, starting transfers between devices, gather_sample(): lax.ppermute(value, 'sample', sample_pairs(k, first))  10.6 us
    ppermute x6, starting transfers between devices, ring_feature(): lax.ppermute(value, 'feature', pairs[k])  8.22 us
    ppermute x6, waiting for transfers between devices, gather_sample(): lax.ppermute(value, 'sample', sample_pairs(k, first))  5.35 us
    ppermute x1, starting transfers between devices, gather_sample(): other = lax.ppermute(value, 'sample', [(i, i ^ 1) for i in range(SAMPLES)])  4.64 us
  transfers between devices with their start and end apart: 16, of which 6 were waited for; matrix products, arithmetic and copies ran while one was open for 6% of the time, Pallas kernels for 22%

profile of v1, /device:TPU:1, one launch (start us, length us, event | category | flops | bytes accessed | tf_op | source)
XLA Modules:
  0.0 120.3 jit_solution(13560933507504486141)
XLA Ops:
  1.5 2.2 %copy-done = f32[2048,512]{1,0:T(8,128)S(1)} copy-done((f32[2048,512]{1,0:T(8,128)S(1)}, f32[2048,512]{1,0:T(8,128)}, u32[]{:S(2)}) %copy-start) | copy-done | bytes 4194328
  3.7 2.2 %copy-done.3 = f32[8192,128]{1,0:T(8,128)S(1)} copy-done((f32[8192,128]{1,0:T(8,128)S(1)}, f32[8192,128]{1,0:T(8,128)}, u32[]{:S(2)}) %copy-start.3) | copy-done | bytes 4194328
  5.9 2.0 %first_margin.1 = (f32[16,128]{1,0:T(8,128)S(1)}, f32[64,128]{1,0:T(8,128)S(1)}) custom-call(s32[64]{0:T(128)S(1)} %reshape.332.ids, f32[2048,512]{1,0:T(8,128)S(1)} %copy-done, f32[8192,128]{1,0:T(8,128)S(1)} %copy-done.3), custom_call_target="tpu_custom_call" | custom-call | tf_op jit(solution)/shard_map/first_margin/pallas_call | solution.py:106
  7.9 2.2 %collective-permute-start = (f32[16,128]{1,0:T(8,128)S(1)}, f32[16,128]{1,0:T(8,128)S(1)}, u32[]{:S(2)}, u32[]{:S(2)}) collective-permute-start(f32[16,128]{1,0:T(8,128)S(1)} %get-tuple-element.15.m0), channel_id=1, source_target_pairs={{0,1},{1,2},{2,3},{3,0},{4,5},{5,6},{6,7},{7,4},{8,9},{9,10},{10,1... | collective-permute-start | bytes 24584 | tf_op jit(solution)/shard_map/ppermute | solution.py:482
  10.1 1.5 %collective-permute-start.1 = (f32[16,128]{1,0:T(8,128)S(1)}, f32[16,128]{1,0:T(8,128)S(1)}, u32[]{:S(2)}, u32[]{:S(2)}) collective-permute-start(f32[16,128]{1,0:T(8,128)S(1)} %get-tuple-element.15.m0), channel_id=1, source_target_pairs={{0,3},{1,0},{2,1},{3,2},{4,7},{5,4},{6,5},{7,6},{8,11},{9,8},{10,9... | collective-permute-start | bytes 24584 | tf_op jit(solution)/shard_map/ppermute | solution.py:482
  11.6 1.6 %collective-permute-start.2 = (f32[16,128]{1,0:T(8,128)S(1)}, f32[16,128]{1,0:T(8,128)S(1)}, u32[]{:S(2)}, u32[]{:S(2)}) collective-permute-start(f32[16,128]{1,0:T(8,128)S(1)} %get-tuple-element.15.m0), channel_id=1, source_target_pairs={{0,2},{1,3},{2,0},{3,1},{4,6},{5,7},{6,4},{7,5},{8,10},{9,11},{10,... | collective-permute-start | bytes 24584 | tf_op jit(solution)/shard_map/ppermute | solution.py:482
  13.9 2.3 %collective-permute-start.11 = (s32[512]{0:T(512)S(1)}, s32[512]{0:T(512)S(1)}, u32[]{:S(2)}, u32[]{:S(2)}) collective-permute-start(s32[512]{0:T(512)S(1)} %multiply_add_fusion), channel_id=1, source_target_pairs={{0,3},{1,0},{2,1},{3,2},{4,7},{5,4},{6,5},{7,6},{8,11},{9,8},{10,9... | collective-permute-start | bytes 6152 | tf_op jit(solution)/shard_map/ppermute | solution.py:482
  16.8 2.1 %pack_rows.1 = f32[128,16,128]{2,1,0:T(8,128)S(1)} custom-call(s32[1,512]{1,0:T(1,128)S(1)} %bitcast.33, f32[512,128]{1,0:T(8,128)S(1)} %copy-done.8, f32[512,128]{1,0:T(8,128)S(1)} %get-tuple-element.44.labels, f32[512,128]{1,0:T(8,128)S(1)} %get-tuple-element.43.members), custom_call_target="tpu_custom_call" | custom-call | tf_op jit(solution)/shard_map/pack_rows/pallas_call | solution.py:274
  18.9 2.5 %copy-done.1 = f32[2048,512]{1,0:T(8,128)S(1)} copy-done((f32[2048,512]{1,0:T(8,128)S(1)}, f32[2048,512]{1,0:T(8,128)}, u32[]{:S(2)}) %copy-start.1) | copy-done | bytes 4194328
  21.4 1.3 %own_stats.1 = f32[72,256]{1,0:T(8,128)S(1)} custom-call(f32[16,128]{1,0:T(8,128)S(1)} %get-tuple-element.15.m0, f32[16,128]{1,0:T(8,128)S(1)} %collective-permute-done.m1, f32[16,128]{1,0:T(8,128)S(1)} %collective-permute-done.1.m2, f32[16,128]{1,0:T(8,128)S(1)} %collective-permute-done.2.m3, f32[16,128]{1,0:T(8,128)S(1)} %bitcast.36, ...), custom_call_target="tpu_custom_call" | custom-call | tf_op jit(solution)/shard_map/own_stats/pallas_call | solution.py:157
  22.8 1.3 %collective-permute-start.3 = (f32[1,72,256]{2,1,0:T(8,128)S(1)}, f32[1,72,256]{2,1,0:T(8,128)S(1)}, u32[]{:S(2)}, u32[]{:S(2)}) collective-permute-start(f32[1,72,256]{2,1,0:T(8,128)S(1)} %bitcast.26), channel_id=1, source_target_pairs={{0,8},{4,36},{8,16},{12,44},{16,24},{20,52},{24,0},{28,60},{32,40}... | collective-permute-start | bytes 221192 | tf_op jit(solution)/shard_map/ppermute | solution.py:501
  24.1 2.5 %collective-permute-start.4 = (f32[1,72,256]{2,1,0:T(8,128)S(1)}, f32[1,72,256]{2,1,0:T(8,128)S(1)}, u32[]{:S(2)}, u32[]{:S(2)}) collective-permute-start(f32[1,72,256]{2,1,0:T(8,128)S(1)} %bitcast.27), channel_id=1, source_target_pairs={{0,16},{4,68},{8,24},{12,76},{16,0},{20,84},{24,8},{28,92},{32,48}... | collective-permute-start | bytes 221192 | tf_op jit(solution)/shard_map/ppermute | solution.py:501
  26.5 1.2 collective-permute-start.5
  29.7 1.7 %collective-permute-start.6 = (f32[4,72,256]{2,1,0:T(8,128)S(1)}, f32[4,72,256]{2,1,0:T(8,128)S(1)}, u32[]{:S(2)}, u32[]{:S(2)}) collective-permute-start(f32[4,72,256]{2,1,0:T(8,128)S(1)} %pad_maximum_fusion), channel_id=1, source_target_pairs={{0,32},{4,12},{8,40},{12,20},{16,48},{20,28},{24,56},{28,4},{32,64... | collective-permute-start | bytes 884744 | tf_op jit(solution)/shard_map/ppermute | solution.py:501
  31.5 3.6 %collective-permute-start.7 = (f32[4,72,256]{2,1,0:T(8,128)S(1)}, f32[4,72,256]{2,1,0:T(8,128)S(1)}, u32[]{:S(2)}, u32[]{:S(2)}) collective-permute-start(f32[4,72,256]{2,1,0:T(8,128)S(1)} %pad_maximum_fusion), channel_id=1, source_target_pairs={{0,64},{4,20},{8,72},{12,28},{16,80},{20,4},{24,88},{28,12},{32,96... | collective-permute-start | bytes 884744 | tf_op jit(solution)/shard_map/ppermute | solution.py:501
  38.9 3.4 %collective-permute-done.7 = f32[4,72,256]{2,1,0:T(8,128)S(1)} collective-permute-done((f32[4,72,256]{2,1,0:T(8,128)S(1)}, f32[4,72,256]{2,1,0:T(8,128)S(1)}, u32[]{:S(2)}, u32[]{:S(2)}) %collective-permute-start.7) | collective-permute-done | bytes 294944 | tf_op jit(solution)/shard_map/ppermute | solution.py:501
  43.8 4.6 %collective-permute-start.9 = (f32[16,72,256]{2,1,0:T(8,128)}, f32[16,72,256]{2,1,0:T(8,128)}, u32[]{:S(2)}, u32[]{:S(2)}) collective-permute-start(f32[16,72,256]{2,1,0:T(8,128)} %get-tuple-element.27), channel_id=1, source_target_pairs={{0,4},{4,0},{8,12},{12,8},{16,20},{20,16},{24,28},{28,24},{32,36},... | collective-permute-start | bytes 3538952 | tf_op jit(solution)/shard_map/ppermute | solution.py:504
  48.6 6.7 %all-to-all-start = ((f32[128,16,128]{2,1,0:T(8,128)}), f32[128,16,128]{2,1,0:T(8,128)S(1)}, u32[]{:S(2)}, u32[]{:S(2)}) async-start(f32[128,16,128]{2,1,0:T(8,128)} %copy-done.5), calls=%async_computation | async-start | bytes 2097152 | tf_op jit(solution)/shard_map/all_to_all | solution.py:520
  55.8 1.4 %constant_dynamic-update-slice_fusion.7.packets = f32[32,72,256]{2,1,0:T(8,128)S(1)} fusion(f32[32,72,256]{2,1,0:T(8,128)S(1)} %get-tuple-element.28, f32[16,72,256]{2,1,0:T(8,128)} %collective-permute-done.9), kind=kLoop, calls=%fused_computation.14 | loop fusion | bytes 2359296 | tf_op jit(solution)/shard_map/concatenate | solution.py:505
  57.2 2.2 %copy-done.2 = f32[2048,512]{1,0:T(8,128)S(1)} copy-done((f32[2048,512]{1,0:T(8,128)S(1)}, f32[2048,512]{1,0:T(8,128)}, u32[]{:S(2)}) %copy-start.2) | copy-done | bytes 4194328
  59.4 2.8 %second_margin.1 = f32[128,128]{1,0:T(8,128)} custom-call(f32[32,72,256]{2,1,0:T(8,128)S(1)} %constant_dynamic-update-slice_fusion.7.packets, f32[64,128]{1,0:T(8,128)S(1)} %broadcast_in_dim.124.own_ids, f32[64,128]{1,0:T(8,128)S(1)} %get-tuple-element.18.chosen, f32[2048,512]{1,0:T(8,128)S(1)} %copy-done.2, f32[2048,128]{1,0:T(8,128)S(1)} %compare_convert_fusion.place, ...), custom_call_target="tpu_custom_call" | custom-call | tf_op jit(solution)/shard_map/second_margin/pallas_call | solution.py:211
  62.2 12.9 %all-to-all-done.rows = f32[128,16,128]{2,1,0:T(8,128)S(1)} async-done(((f32[128,16,128]{2,1,0:T(8,128)}), f32[128,16,128]{2,1,0:T(8,128)S(1)}, u32[]{:S(2)}, u32[]{:S(2)}) %all-to-all-start) | async-done | bytes 1048608 | tf_op jit(solution)/shard_map/all_to_all | solution.py:520
  75.1 3.8 %all-to-all-start.1 = ((f32[128,1,128]{2,1,0:T(1,128)}), f32[128,1,128]{2,1,0:T(1,128)S(1)}, u32[]{:S(2)}, u32[]{:S(2)}) async-start(f32[128,1,128]{2,1,0:T(1,128)} %bitcast.5), calls=%async_computation.1 | async-start | bytes 131072 | tf_op jit(solution)/shard_map/all_to_all | solution.py:520
  79.0 3.7 %group_rows.1 = (f32[32,32,128]{2,1,0:T(8,128)S(1)}, f32[32,128]{1,0:T(8,128)S(1)}, f32[32,128]{1,0:T(8,128)S(1)}, f32[32,128]{1,0:T(8,128)S(1)}, s32[1,1024]{1,0:T(1,128)S(1)}, /*index=5*/s32[1,1024]{1,0:T(1,128)S(1)}) custom-call(f32[128,16,128]{2,1,0:T(8,128)S(1)} %all-to-all-done.rows, f32[128,128]{1,0:T(8,128)S(1)} %bitcast.30), custom_call_target="tpu_custom_call" | custom-call | tf_op jit(solution)/shard_map/group_rows/pallas_call | solution.py:359
  84.7 4.3 %all-to-all-done.1 = f32[128,1,128]{2,1,0:T(1,128)S(1)} async-done(((f32[128,1,128]{2,1,0:T(1,128)}), f32[128,1,128]{2,1,0:T(1,128)S(1)}, u32[]{:S(2)}, u32[]{:S(2)}) %all-to-all-start.1) | async-done | bytes 65568 | tf_op jit(solution)/shard_map/all_to_all | solution.py:520
  89.0 1.0 copy-done.7
  91.4 3.2 %solve_members.1 = (f32[128,128]{1,0:T(8,128)}, f32[32,128]{1,0:T(8,128)S(1)}) custom-call(f32[128,128]{1,0:T(8,128)S(1)} %bitcast.31, f32[32,32,128]{2,1,0:T(8,128)S(1)} %copy-done.7, f32[32,128]{1,0:T(8,128)S(1)} %get-tuple-element.20.score, f32[32,128]{1,0:T(8,128)S(1)} %copy-done.11, f32[32,128]{1,0:T(8,128)S(1)} %copy-done.13, ...), custom_call_target="tpu_custom_call" | custom-call | tf_op jit(solution)/shard_map/solve_members/pallas_call | solution.py:429
  94.7 5.6 %all-to-all-start.2 = ((f32[128,1,128]{2,1,0:T(1,128)}), f32[128,1,128]{2,1,0:T(1,128)S(1)}, u32[]{:S(2)}, u32[]{:S(2)}) async-start(f32[128,1,128]{2,1,0:T(1,128)} %bitcast.9), calls=%async_computation.2 | async-start | bytes 131072 | tf_op jit(solution)/shard_map/all_to_all | solution.py:520
  100.5 2.2 %copy-done.4 = f32[8192,128]{1,0:T(8,128)S(1)} copy-done((f32[8192,128]{1,0:T(8,128)S(1)}, f32[8192,128]{1,0:T(8,128)}, u32[]{:S(2)}) %copy-start.4) | copy-done | bytes 4194328
  102.6 15.7 %all_weights.1 = f32[8192,128]{1,0:T(8,128)} custom-call(s32[2048]{0:T(1024)S(1)} %convert_element_type.31.ids, s32[32]{0:T(128)S(1)} %fusion.12.order, f32[32,72,256]{2,1,0:T(8,128)S(1)} %constant_dynamic-update-slice_fusion.7.packets, f32[8192,128]{1,0:T(8,128)S(1)} %copy-done.4), custom_call_target="tpu_custom_call" | custom-call | tf_op jit(solution)/shard_map/all_weights/pallas_call | solution.py:247
  118.3 1.0 new_coefs.1
  119.4 0.9 total_rows.1
  (81 shorter events, 13.8 us)
Async XLA Ops:
  1.5 2.2 %copy-start = (f32[2048,512]{1,0:T(8,128)S(1)}, f32[2048,512]{1,0:T(8,128)}, u32[]{:S(2)}) copy-start(f32[2048,512]{1,0:T(8,128)} %feats.7) | copy-start | bytes 12582916
  3.7 2.2 %copy-start.3 = (f32[8192,128]{1,0:T(8,128)S(1)}, f32[8192,128]{1,0:T(8,128)}, u32[]{:S(2)}) copy-start(f32[8192,128]{1,0:T(8,128)} %weights.3) | copy-start | bytes 12582916
  5.9 7.3 %copy-start.16 = (s32[512]{0:T(512)S(1)}, s32[512]{0:T(512)}, u32[]{:S(2)}) copy-start(s32[512]{0:T(512)} %param.14) | copy-start | bytes 6148
  5.9 10.4 %copy-start.14 = (f32[2048]{0:T(1024)S(1)}, f32[2048]{0:T(1024)}, u32[]{:S(2)}) copy-start(f32[2048]{0:T(1024)} %param.11) | copy-start | bytes 24580
  5.9 10.9 %copy-start.8 = (f32[512,128]{1,0:T(8,128)S(1)}, f32[512,128]{1,0:T(8,128)}, u32[]{:S(2)}) copy-start(f32[512,128]{1,0:T(8,128)} %feats.4) | copy-start | bytes 786436
  7.8 11.1 %copy-start.15 = (f32[2048]{0:T(1024)S(1)}, f32[2048]{0:T(1024)}, u32[]{:S(2)}) copy-start(f32[2048]{0:T(1024)} %param.12) | copy-start | bytes 24580
  7.9 11.0 %collective-permute-start = (f32[16,128]{1,0:T(8,128)S(1)}, f32[16,128]{1,0:T(8,128)S(1)}, u32[]{:S(2)}, u32[]{:S(2)}) collective-permute-start(f32[16,128]{1,0:T(8,128)S(1)} %get-tuple-element.15.m0), channel_id=1, source_target_pairs={{0,1},{1,2},{2,3},{3,0},{4,5},{5,6},{6,7},{7,4},{8,9},{9,10},{10,1... | collective-permute-start | bytes 24584 | tf_op jit(solution)/shard_map/ppermute | solution.py:482
  10.1 8.8 %collective-permute-start.1 = (f32[16,128]{1,0:T(8,128)S(1)}, f32[16,128]{1,0:T(8,128)S(1)}, u32[]{:S(2)}, u32[]{:S(2)}) collective-permute-start(f32[16,128]{1,0:T(8,128)S(1)} %get-tuple-element.15.m0), channel_id=1, source_target_pairs={{0,3},{1,0},{2,1},{3,2},{4,7},{5,4},{6,5},{7,6},{8,11},{9,8},{10,9... | collective-permute-start | bytes 24584 | tf_op jit(solution)/shard_map/ppermute | solution.py:482
  11.6 7.3 %collective-permute-start.2 = (f32[16,128]{1,0:T(8,128)S(1)}, f32[16,128]{1,0:T(8,128)S(1)}, u32[]{:S(2)}, u32[]{:S(2)}) collective-permute-start(f32[16,128]{1,0:T(8,128)S(1)} %get-tuple-element.15.m0), channel_id=1, source_target_pairs={{0,2},{1,3},{2,0},{3,1},{4,6},{5,7},{6,4},{7,5},{8,10},{9,11},{10,... | collective-permute-start | bytes 24584 | tf_op jit(solution)/shard_map/ppermute | solution.py:482
  13.4 35.1 %collective-permute-start.10 = (s32[512]{0:T(512)S(1)}, s32[512]{0:T(512)S(1)}, u32[]{:S(2)}, u32[]{:S(2)}) collective-permute-start(s32[512]{0:T(512)S(1)} %multiply_add_fusion), channel_id=1, source_target_pairs={{0,1},{1,2},{2,3},{3,0},{4,5},{5,6},{6,7},{7,4},{8,9},{9,10},{10,1... | collective-permute-start | bytes 6152 | tf_op jit(solution)/shard_map/ppermute | solution.py:482
  13.9 34.6 %collective-permute-start.11 = (s32[512]{0:T(512)S(1)}, s32[512]{0:T(512)S(1)}, u32[]{:S(2)}, u32[]{:S(2)}) collective-permute-start(s32[512]{0:T(512)S(1)} %multiply_add_fusion), channel_id=1, source_target_pairs={{0,3},{1,0},{2,1},{3,2},{4,7},{5,4},{6,5},{7,6},{8,11},{9,8},{10,9... | collective-permute-start | bytes 6152 | tf_op jit(solution)/shard_map/ppermute | solution.py:482
  18.8 10.9 %copy-start.5 = (f32[128,16,128]{2,1,0:T(8,128)}, f32[128,16,128]{2,1,0:T(8,128)S(1)}, u32[]{:S(2)}) copy-start(f32[128,16,128]{2,1,0:T(8,128)S(1)} %pack_rows.1) | copy-start | bytes 3145732
  18.9 2.5 %copy-start.1 = (f32[2048,512]{1,0:T(8,128)S(1)}, f32[2048,512]{1,0:T(8,128)}, u32[]{:S(2)}) copy-start(f32[2048,512]{1,0:T(8,128)} %feats.7) | copy-start | bytes 12582916
  22.8 5.5 %collective-permute-start.3 = (f32[1,72,256]{2,1,0:T(8,128)S(1)}, f32[1,72,256]{2,1,0:T(8,128)S(1)}, u32[]{:S(2)}, u32[]{:S(2)}) collective-permute-start(f32[1,72,256]{2,1,0:T(8,128)S(1)} %bitcast.26), channel_id=1, source_target_pairs={{0,8},{4,36},{8,16},{12,44},{16,24},{20,52},{24,0},{28,60},{32,40}... | collective-permute-start | bytes 221192 | tf_op jit(solution)/shard_map/ppermute | solution.py:501
  24.1 5.0 %collective-permute-start.4 = (f32[1,72,256]{2,1,0:T(8,128)S(1)}, f32[1,72,256]{2,1,0:T(8,128)S(1)}, u32[]{:S(2)}, u32[]{:S(2)}) collective-permute-start(f32[1,72,256]{2,1,0:T(8,128)S(1)} %bitcast.27), channel_id=1, source_target_pairs={{0,16},{4,68},{8,24},{12,76},{16,0},{20,84},{24,8},{28,92},{32,48}... | collective-permute-start | bytes 221192 | tf_op jit(solution)/shard_map/ppermute | solution.py:501
  26.5 3.2 %collective-permute-start.5 = (f32[1,72,256]{2,1,0:T(8,128)S(1)}, f32[1,72,256]{2,1,0:T(8,128)S(1)}, u32[]{:S(2)}, u32[]{:S(2)}) collective-permute-start(f32[1,72,256]{2,1,0:T(8,128)S(1)} %bitcast.28), channel_id=1, source_target_pairs={{0,24},{4,100},{8,0},{12,108},{16,8},{20,116},{24,16},{28,124},{32... | collective-permute-start | bytes 221192 | tf_op jit(solution)/shard_map/ppermute | solution.py:501
  29.7 8.2 %collective-permute-start.6 = (f32[4,72,256]{2,1,0:T(8,128)S(1)}, f32[4,72,256]{2,1,0:T(8,128)S(1)}, u32[]{:S(2)}, u32[]{:S(2)}) collective-permute-start(f32[4,72,256]{2,1,0:T(8,128)S(1)} %pad_maximum_fusion), channel_id=1, source_target_pairs={{0,32},{4,12},{8,40},{12,20},{16,48},{20,28},{24,56},{28,4},{32,64... | collective-permute-start | bytes 884744 | tf_op jit(solution)/shard_map/ppermute | solution.py:501
  31.5 10.9 %collective-permute-start.7 = (f32[4,72,256]{2,1,0:T(8,128)S(1)}, f32[4,72,256]{2,1,0:T(8,128)S(1)}, u32[]{:S(2)}, u32[]{:S(2)}) collective-permute-start(f32[4,72,256]{2,1,0:T(8,128)S(1)} %pad_maximum_fusion), channel_id=1, source_target_pairs={{0,64},{4,20},{8,72},{12,28},{16,80},{20,4},{24,88},{28,12},{32,96... | collective-permute-start | bytes 884744 | tf_op jit(solution)/shard_map/ppermute | solution.py:501
  35.1 8.0 %collective-permute-start.8 = (f32[4,72,256]{2,1,0:T(8,128)S(1)}, f32[4,72,256]{2,1,0:T(8,128)S(1)}, u32[]{:S(2)}, u32[]{:S(2)}) collective-permute-start(f32[4,72,256]{2,1,0:T(8,128)S(1)} %pad_maximum_fusion), channel_id=1, source_target_pairs={{0,96},{4,28},{8,104},{12,4},{16,112},{20,12},{24,120},{28,20},{32... | collective-permute-start | bytes 884744 | tf_op jit(solution)/shard_map/ppermute | solution.py:501
  38.0 10.5 %collective-permute-start.12 = (s32[512]{0:T(512)S(1)}, s32[512]{0:T(512)S(1)}, u32[]{:S(2)}, u32[]{:S(2)}) collective-permute-start(s32[512]{0:T(512)S(1)} %multiply_add_fusion), channel_id=1, source_target_pairs={{0,2},{1,3},{2,0},{3,1},{4,6},{5,7},{6,4},{7,5},{8,10},{9,11},{10,... | collective-permute-start | bytes 6152 | tf_op jit(solution)/shard_map/ppermute | solution.py:482
  43.8 11.9 %collective-permute-start.9 = (f32[16,72,256]{2,1,0:T(8,128)}, f32[16,72,256]{2,1,0:T(8,128)}, u32[]{:S(2)}, u32[]{:S(2)}) collective-permute-start(f32[16,72,256]{2,1,0:T(8,128)} %get-tuple-element.27), channel_id=1, source_target_pairs={{0,4},{4,0},{8,12},{12,8},{16,20},{20,16},{24,28},{28,24},{32,36},... | collective-permute-start | bytes 3538952 | tf_op jit(solution)/shard_map/ppermute | solution.py:504
  48.6 26.5 %all-to-all-start = ((f32[128,16,128]{2,1,0:T(8,128)}), f32[128,16,128]{2,1,0:T(8,128)S(1)}, u32[]{:S(2)}, u32[]{:S(2)}) async-start(f32[128,16,128]{2,1,0:T(8,128)} %copy-done.5), calls=%async_computation | async-start | bytes 2097152 | tf_op jit(solution)/shard_map/all_to_all | solution.py:520
  57.2 2.2 %copy-start.2 = (f32[2048,512]{1,0:T(8,128)S(1)}, f32[2048,512]{1,0:T(8,128)}, u32[]{:S(2)}) copy-start(f32[2048,512]{1,0:T(8,128)} %feats.7) | copy-start | bytes 12582916
  59.4 19.6 %copy-start.9 = (f32[32,128]{1,0:T(8,128)S(1)}, f32[32,128]{1,0:T(8,128)}, u32[]{:S(2)}) copy-start(f32[32,128]{1,0:T(8,128)} %coefs.1) | copy-start | bytes 49156
  75.1 13.8 %all-to-all-start.1 = ((f32[128,1,128]{2,1,0:T(1,128)}), f32[128,1,128]{2,1,0:T(1,128)S(1)}, u32[]{:S(2)}, u32[]{:S(2)}) async-start(f32[128,1,128]{2,1,0:T(1,128)} %bitcast.5), calls=%async_computation.1 | async-start | bytes 131072 | tf_op jit(solution)/shard_map/all_to_all | solution.py:520
  82.7 0.8 copy-start.6
  83.5 0.6 copy-start.10
  89.0 1.0 copy-start.7
  90.0 0.7 copy-start.11
  90.7 0.7 copy-start.13
  94.7 24.7 %all-to-all-start.2 = ((f32[128,1,128]{2,1,0:T(1,128)}), f32[128,1,128]{2,1,0:T(1,128)S(1)}, u32[]{:S(2)}, u32[]{:S(2)}) async-start(f32[128,1,128]{2,1,0:T(1,128)} %bitcast.9), calls=%async_computation.2 | async-start | bytes 131072 | tf_op jit(solution)/shard_map/all_to_all | solution.py:520
  100.5 2.2 %copy-start.4 = (f32[8192,128]{1,0:T(8,128)S(1)}, f32[8192,128]{1,0:T(8,128)}, u32[]{:S(2)}) copy-start(f32[8192,128]{1,0:T(8,128)} %weights.3) | copy-start | bytes 12582916
  (1 other events, 0.6 us)

commit v2 on v1

v2 whole, which is shorter than its diff:
```python
import functools

import jax
import jax.numpy as jnp
from jax import lax
from jax.experimental import pallas as pl
from jax.experimental.pallas import tpu as pltpu
from jax.sharding import PartitionSpec as P

STEP_SIZE = 0.5
FIXED_RIDGE = 0.1
MEMBER_RIDGE = 1.0
MEMBER_STEP = 0.5

F32 = jnp.float32
BF16 = jnp.bfloat16
I32 = jnp.int32

TILES = 16
SLOTS = 4
TILE = 128
BLK = 128
ENTRIES = TILES * SLOTS
PACKET = ENTRIES + 8
DEVICES = 128
SAMPLES = 32
FEATURES = 4
CAP = 8
OWN = 512
POS = DEVICES * CAP
NOTE = CAP + 1
MEM = 32
GROUP = 32
RING = (0, 1, 3, 2)

NN = (((1,), (0,)), ((), ()))
NT = (((1,), (1,)), ((), ()))


def split(x, parts):
    out = []
    for _ in range(parts - 1):
        top = x.astype(BF16)
        out.append(top)
        x = x - top.astype(F32)
    out.append(x.astype(BF16))
    return out


def dot(a, b, dims=NN):
    return lax.dot_general(a, b, dims, preferred_element_type=F32)


def dot_right(mask, x, parts, dims=NN):
    return functools.reduce(jnp.add, [dot(mask, piece, dims) for piece in split(x, parts)])


def dot_left(x, mask, parts, dims=NN):
    return functools.reduce(jnp.add, [dot(piece, mask, dims) for piece in split(x, parts)])


def iota(shape, dim):
    return lax.broadcasted_iota(I32, shape, dim)


def onehot(cond):
    return jnp.where(cond, 1.0, 0.0).astype(F32)


def params(mib):
    return pltpu.CompilerParams(vmem_limit_bytes=mib << 20)


HBM = pl.BlockSpec(memory_space=pltpu.HBM)
ANY = pl.BlockSpec(memory_space=pl.ANY)
VMEM = pl.BlockSpec(memory_space=pltpu.VMEM)
SMEM = pl.BlockSpec(memory_space=pltpu.SMEM)
CHUNKS = 8
WIDE = 50


def fetch(source, target, sems, chunks=CHUNKS):
    rows = source.shape[0] // chunks
    copies = [
        pltpu.make_async_copy(
            source.at[pl.ds(i * rows, rows)], target.at[pl.ds(i * rows, rows)], sems.at[i]
        )
        for i in range(chunks)
    ]
    for copy in copies:
        copy.start()
    return copies


def tile_margin(feats, weights, t):
    total = None
    for k in range(SLOTS):
        x = feats[t * TILE : (t + 1) * TILE, k * BLK : (k + 1) * BLK]
        e = t * SLOTS + k
        term = x * weights[e : e + 1, :]
        total = term if total is None else total + term
    return total


def margin_kernel(
    ids, members, feats, weights, out, chosen, own, sent, merge, held, row_sems, sems
):
    copies = fetch(feats, held, sems)
    picked = [
        pltpu.make_async_copy(
            weights.at[pl.ds(ids[e % SLOTS, e // SLOTS], 1)], chosen.at[pl.ds(e, 1)], row_sems.at[e]
        )
        for e in range(ENTRIES)
    ]
    for copy in picked:
        copy.start()

    owner = members[...] // MEM
    column = owner.astype(F32).T.astype(I32)
    sub, lane = iota((TILE, TILE), 0), iota((TILE, TILE), 1)
    for a in range(4):
        rank = None
        for b in range(a + 1):
            same = jnp.broadcast_to(column[:, b : b + 1], (TILE, TILE)) == owner[a : a + 1, :]
            if a == b:
                same = same & (sub < lane)
            term = jnp.sum(onehot(same), axis=0, keepdims=True)
            rank = term if rank is None else rank + term
        out[TILES + a : TILES + a + 1, :] = owner[a : a + 1, :].astype(F32) * CAP + rank
    out[TILES + 4 :, :] = jnp.zeros((4, TILE), F32)

    at, of = iota((ENTRIES, 128), 0), iota((ENTRIES, 128), 1) % ENTRIES
    rows = jnp.zeros((ENTRIES, 128), I32)
    line = jnp.zeros((8, 128), I32)
    for e in range(ENTRIES):
        block = ids[e % SLOTS, e // SLOTS]
        rows = jnp.where(at == e, block, rows)
        line = jnp.where(of[0:8, :] == e, block, line)
    same = rows == line[0:1, :]
    repeat = jnp.sum(onehot(same & (at < of)), axis=0, keepdims=True)
    own[...] = rows.astype(F32)
    kept = jnp.where(repeat > 0.0, weights.shape[0], line[0:1, :]).astype(F32)
    sent[...] = jnp.broadcast_to(jnp.concatenate([kept, kept], axis=1), (8, 256))
    earlier = jnp.sum(onehot(same & (of < at)), axis=1, keepdims=True)
    merge[...] = jnp.where(earlier > 0.0, 0.0, onehot(same))

    for copy in picked:
        copy.wait()
    each = TILES // CHUNKS
    for c in range(CHUNKS):
        copies[c].wait()
        for t in range(c * each, (c + 1) * each):
            out[t : t + 1, :] = jnp.sum(tile_margin(held, chosen, t).T, axis=0, keepdims=True)


def first_margin(ids, members, feats, weights):
    table = jax.ShapeDtypeStruct((ENTRIES, BLK), F32)
    return pl.pallas_call(
        margin_kernel,
        in_specs=[SMEM, VMEM, HBM, HBM],
        out_shape=[
            jax.ShapeDtypeStruct((TILES + 8, TILE), F32),
            table,
            table,
            jax.ShapeDtypeStruct((8, 2 * BLK), F32),
            table,
        ],
        scratch_shapes=[
            pltpu.VMEM((TILES * TILE, SLOTS * BLK), F32),
            pltpu.SemaphoreType.DMA((ENTRIES,)),
            pltpu.SemaphoreType.DMA((CHUNKS,)),
        ],
        compiler_params=params(WIDE),
        name="first_margin",
    )(ids, members, feats, weights)


def stats_kernel(m0, m1, m2, m3, prior, labels, ids, merge, feats, out, held, raw, sems):
    copies = fetch(feats, held, sems)
    margin = (m0[0:TILES, :] + m1[0:TILES, :]) + (m2[0:TILES, :] + m3[0:TILES, :])
    probs = jax.nn.sigmoid(margin + prior[...])
    residual = (probs - labels[...]).T
    curvature = (probs * (1.0 - probs)).T
    each = TILES // CHUNKS
    for t in range(TILES):
        if t % each == 0:
            copies[t // each].wait()
        r = jnp.broadcast_to(residual[:, t : t + 1], (TILE, BLK))
        c = jnp.broadcast_to(curvature[:, t : t + 1], (TILE, BLK))
        for k in range(SLOTS):
            x = held[t * TILE : (t + 1) * TILE, k * BLK : (k + 1) * BLK]
            e = t * SLOTS + k
            raw[e : e + 1, 0:BLK] = jnp.sum(x * r, axis=0, keepdims=True)
            raw[e : e + 1, BLK : 2 * BLK] = jnp.sum(x * x * c, axis=0, keepdims=True)
    out[0:ENTRIES, :] = dot_right(merge[:, 0:ENTRIES].astype(BF16), raw[...], 3)
    out[ENTRIES:PACKET, :] = ids[...]


def own_stats(margins, prior, labels, ids, merge, feats):
    return pl.pallas_call(
        stats_kernel,
        in_specs=[VMEM] * 8 + [HBM],
        out_shape=jax.ShapeDtypeStruct((PACKET, 2 * BLK), F32),
        scratch_shapes=[
            pltpu.VMEM((TILES * TILE, SLOTS * BLK), F32),
            pltpu.VMEM((ENTRIES, 2 * BLK), F32),
            pltpu.SemaphoreType.DMA((CHUNKS,)),
        ],
        compiler_params=params(WIDE),
        name="own_stats",
    )(*margins, prior, labels, ids, merge, feats)


def second_kernel(own_ids, chosen, packed, feats, *rest):
    margins, pieces, (out, held, sent, slots, sems, piece_sems) = rest[:4], rest[4:12], rest[12:]
    arrivals = [
        pltpu.make_async_copy(piece, sent.at[pl.ds(4 * PACKET * i, 4 * PACKET)], piece_sems.at[i])
        for i, piece in enumerate(pieces)
    ]
    for copy in arrivals:
        copy.start()
    copies = fetch(feats, held, sems)
    lane = iota((1, 128), 1)
    acc = None
    for pair in range(SAMPLES // 2):
        a, b = 2 * pair, 2 * pair + 1
        if a % 4 == 0:
            arrivals[a // 4].wait()
        a, b = a * PACKET, b * PACKET
        ids = jnp.where(
            lane < ENTRIES,
            sent[a + ENTRIES : a + ENTRIES + 1, 0:128],
            sent[b + ENTRIES : b + ENTRIES + 1, 0:128],
        )
        mask = onehot(own_ids[...] == ids).astype(BF16)
        both = jnp.concatenate([sent[a : a + ENTRIES, :], sent[b : b + ENTRIES, :]], axis=0)
        term = dot_right(mask, both, 2)
        acc = term if acc is None else acc + term
    w = chosen[...]
    w = w - STEP_SIZE * (acc[:, :BLK] + FIXED_RIDGE * w) / (acc[:, BLK:] + 1.0)
    ones = jnp.ones((BLK, 128), BF16)
    feature = lax.axis_index("feature")
    for shift, margin in zip(RING, margins):
        source = lax.rem(feature + FEATURES - shift, FEATURES)
        slots[pl.ds(source * 4, 4), :] = margin[TILES : TILES + 4, :]
    slot = slots[...].astype(I32)
    column = (slot % CAP + CAP * (iota((TILES, TILE), 0) // 4)).astype(F32).T
    owner = slot // CAP
    result = None
    lanes = (iota((TILE, 128), 1) % 32).astype(F32)
    for t in range(0, TILES, 2):
        copies[t // 2].wait()
        both = [tile_margin(held, w, t), tile_margin(held, w, t + 1)]
        margin = dot_left(jnp.concatenate(both, axis=0), ones, 2)
        place = [
            lanes == jnp.broadcast_to(column[:, q : q + 1], (TILE, 128)) for q in (t, t + 1)
        ]
        placed = jnp.where(jnp.concatenate(place, axis=0), margin, 0.0)
        owners = jnp.concatenate([owner[t : t + 1, :], owner[t + 1 : t + 2, :]], axis=1)
        mask = onehot(iota((DEVICES, 2 * TILE), 0) == owners).astype(BF16)
        term = dot_right(mask, placed, 2)
        result = term if result is None else result + term
    out[...] = packed[...]
    result = jnp.where(iota((DEVICES, 128), 1) < 32, result, 0.0)
    for d in range(DEVICES):
        at = NOTE * d + CAP
        out[at : at + 1, :] = packed[at : at + 1, :] + result[d : d + 1, :]


def second_margin(pieces, own_ids, chosen, margins, packed, feats):
    return pl.pallas_call(
        second_kernel,
        in_specs=[VMEM] * 3 + [HBM] + [VMEM] * 4 + [ANY] * 8,
        out_shape=jax.ShapeDtypeStruct((DEVICES * NOTE, 128), F32),
        scratch_shapes=[
            pltpu.VMEM((TILES * TILE, SLOTS * BLK), F32),
            pltpu.VMEM((SAMPLES * PACKET, 2 * BLK), F32),
            pltpu.VMEM((TILES, TILE), F32),
            pltpu.SemaphoreType.DMA((CHUNKS,)),
            pltpu.SemaphoreType.DMA((8,)),
        ],
        compiler_params=params(WIDE),
        name="second_margin",
    )(own_ids, chosen, packed, feats, *margins, *pieces)


def gathered_place(source):
    me = lax.axis_index("sample")
    x, z, core = me // 8, (me // 2) % 4, me % 2
    xs, zs, cs = source // 8, (source // 2) % 4, source % 2
    along_x, along_z = (x - xs + 4) % 4, (z - zs + 4) % 4
    late = jnp.where(cs == 0, along_x, along_z)
    early = jnp.where(cs == 0, along_z, along_x)
    return jnp.where(cs == core, 0, 16) + late * 4 + early


def weights_kernel(weights, *rest):
    pieces, rest = rest[:8], rest[8:]
    out, held, grad, hess, sent, table, ids, in_sems, out_sems, piece_sems, id_sem = rest
    blocks = weights.shape[0]
    arrivals = [
        pltpu.make_async_copy(piece, sent.at[pl.ds(4 * PACKET * i, 4 * PACKET)], piece_sems.at[i])
        for i, piece in enumerate(pieces)
    ]
    for copy in arrivals:
        copy.start()
    copies = fetch(weights, held, in_sems)

    def clear(i, carry):
        at = pl.ds(pl.multiple_of(i * 256, 256), 256)
        grad[at, :] = jnp.zeros((256, BLK), F32)
        hess[at, :] = jnp.zeros((256, BLK), F32)
        return carry

    lax.fori_loop(0, blocks // 256, clear, 0)
    for copy in arrivals:
        copy.wait()

    lines = [sent[i * PACKET + ENTRIES : i * PACKET + ENTRIES + 1, 0:128] for i in range(SAMPLES)]
    table[...] = jnp.concatenate(lines, axis=0).astype(I32)
    copy = pltpu.make_async_copy(table, ids, id_sem)
    copy.start()
    copy.wait()

    def source(s, carry):
        at = gathered_place(s)
        packet = sent.at[pl.ds(pl.multiple_of(at * PACKET, 8), PACKET)]
        for first in range(0, ENTRIES, 16):
            span = range(first, first + 16)
            rows = [pl.ds(ids[at, j], 1) for j in span]
            old = [(grad[r, :], hess[r, :]) for r in rows]
            new = [
                (g + packet[j : j + 1, 0:BLK], h + packet[j : j + 1, BLK : 2 * BLK])
                for j, (g, h) in zip(span, old)
            ]
            for r, (g, h) in zip(rows, new):
                grad[r, :] = g
                hess[r, :] = h
        return carry

    lax.fori_loop(0, SAMPLES, source, 0)
    size = blocks // CHUNKS
    done = []
    for c in range(CHUNKS):
        copies[c].wait()

        def update(i, carry, c=c):
            at = pl.ds(pl.multiple_of(c * size + i * 256, 256), 256)
            w = held[at, :]
            held[at, :] = w - STEP_SIZE * (grad[at, :] + FIXED_RIDGE * w) / (hess[at, :] + 1.0)
            return carry

        lax.fori_loop(0, size // 256, update, 0)
        at = pl.ds(c * size, size)
        copy = pltpu.make_async_copy(held.at[at], out.at[at], out_sems.at[c])
        copy.start()
        done.append(copy)
    for copy in done:
        copy.wait()


def all_weights(pieces, weights):
    blocks = weights.shape[0]
    return pl.pallas_call(
        weights_kernel,
        in_specs=[HBM] + [ANY] * 8,
        out_specs=HBM,
        out_shape=jax.ShapeDtypeStruct((blocks, BLK), F32),
        scratch_shapes=[
            pltpu.VMEM((blocks, BLK), F32),
            pltpu.VMEM((blocks + 8, BLK), F32),
            pltpu.VMEM((blocks + 8, BLK), F32),
            pltpu.VMEM((SAMPLES * PACKET, 2 * BLK), F32),
            pltpu.VMEM((SAMPLES, 128), I32),
            pltpu.SMEM((SAMPLES, 128), I32),
            pltpu.SemaphoreType.DMA((CHUNKS,)),
            pltpu.SemaphoreType.DMA((CHUNKS,)),
            pltpu.SemaphoreType.DMA((8,)),
            pltpu.SemaphoreType.DMA,
        ],
        compiler_params=params(WIDE),
        name="all_weights",
    )(weights, *pieces)


def pack_kernel(margin, members, labels, feats, out, slot, placed):
    feature = lax.axis_index("feature")
    slots = margin[TILES : TILES + 4, :].astype(I32)
    own = labels[pl.ds(feature * 4, 4), :]
    local = (members[...] % MEM + 1).astype(F32)
    columns = jnp.concatenate([(slots % CAP).astype(F32), own, local], axis=0).T
    lane = iota((TILE, 128), 1)
    within = (lane % CAP).astype(F32)
    for a in range(4):
        slot[:, a * TILE : (a + 1) * TILE] = slots[a : a + 1, :]
        rank, label, member = (
            jnp.broadcast_to(columns[:, 4 * q + a : 4 * q + a + 1], (TILE, 128)) for q in range(3)
        )
        value = jnp.where(lane // CAP == 4, label, jnp.where(lane // CAP == 5, member, 0.0))
        placed[a * TILE : (a + 1) * TILE, :] = jnp.where(within == rank, value, 0.0)
    line = slot[...]
    rows = dot_right(onehot(iota((POS, OWN), 0) == line).astype(BF16), feats[...], 3)
    notes = dot_right(onehot(iota((DEVICES, OWN), 0) == line // CAP).astype(BF16), placed[...], 3)
    for d in range(DEVICES):
        out[NOTE * d : NOTE * d + CAP, :] = rows[CAP * d : CAP * (d + 1), :]
        out[NOTE * d + CAP : NOTE * (d + 1), :] = notes[d : d + 1, :]


def pack_rows(margin, members, labels, feats):
    return pl.pallas_call(
        pack_kernel,
        out_shape=[
            jax.ShapeDtypeStruct((DEVICES * NOTE, 128), F32),
            jax.ShapeDtypeStruct((1, OWN), I32),
        ],
        scratch_shapes=[pltpu.VMEM((OWN, 128), F32)],
        compiler_params=params(WIDE),
        name="pack_rows",
    )(margin, members, labels, feats)


def gram_times(gram, v):
    out = None
    for i in range(GROUP):
        term = gram[i] * v[i : i + 1, :]
        out = term if out is None else out + term
    return out


def spread(block, source):
    group = iota(block.shape, 1) // MEM
    out = None
    for g in range(4):
        shift = (g - source) % 4
        moved = pltpu.roll(block, MEM * shift, 1) if shift else block
        out = moved if out is None else jnp.where(group == g, moved, out)
    return out


def unpack(rows, feats, notes=None):
    for d in range(DEVICES):
        feats[CAP * d : CAP * (d + 1), :] = rows[NOTE * d : NOTE * d + CAP, :]
        if notes is not None:
            notes[d : d + 1, :] = rows[NOTE * d + CAP : NOTE * (d + 1), :]


def repeat_lanes(x, first, size):
    lane = iota(x.shape, 1)
    x = jnp.where((lane >= first) & (lane < first + size), x, 0.0)
    while size < 128:
        x = x + pltpu.roll(x, size, 1)
        size *= 2
    return x


def owner_kernel(rows, coefs, back, steps, lines, turned, diag, gram, work, held, notes):
    unpack(rows, held, notes)
    sub, lane = iota((128, 128), 0), iota((128, 128), 1)
    lab_parts, mem_parts, fixed_parts = [], [], []
    labs = repeat_lanes(notes[...], 4 * CAP, CAP)
    mems = repeat_lanes(notes[...], 5 * CAP, CAP)
    got = repeat_lanes(notes[...], 0, 32)
    for b in range(8):
        at = slice(16 * b, 16 * (b + 1))
        keep = iota((16, 128), 0) == iota((16, 128), 1) // CAP
        lab_parts.append(jnp.sum(jnp.where(keep, labs[at, :], 0.0), axis=0, keepdims=True))
        mem_parts.append(jnp.sum(jnp.where(keep, mems[at, :], 0.0), axis=0, keepdims=True))
        keep = iota((16, 128), 0) // FEATURES == iota((16, 128), 1) // 32
        fixed_parts.append(jnp.sum(jnp.where(keep, got[at, :], 0.0), axis=0, keepdims=True))
    lab = jnp.concatenate(lab_parts, axis=1)
    fixed = jnp.concatenate(fixed_parts, axis=1)
    mem = jnp.concatenate(mem_parts, axis=1).astype(I32) - 1
    few = onehot(iota((MEM, POS), 0) == mem)
    before = onehot(sub < lane).astype(BF16)
    ones = jnp.ones((128, 128), BF16)
    carry = jnp.zeros((MEM, 128), F32)
    ranks = []
    for b in range(8):
        part = few[:, 128 * b : 128 * (b + 1)]
        half = part.astype(BF16)
        count = dot(half, before) + carry
        carry = carry + dot(half, ones)
        ranks.append(jnp.sum(part * count, axis=0, keepdims=True))
    rnk = jnp.concatenate(ranks, axis=1).astype(I32)
    lines[0:8, :] = jnp.broadcast_to(mem, (8, POS))
    lines[8:16, :] = jnp.broadcast_to(rnk, (8, POS))
    by_rank = onehot((iota((GROUP, POS), 0) == rnk) & (mem >= 0))
    by_member = onehot((iota((128, POS), 0) % MEM) == mem).astype(BF16)
    y = dot_left(by_rank * lab, by_member, 3, NT)
    offset = dot_left(by_rank * fixed, by_member, 2, NT)
    alive = dot(by_rank.astype(BF16), by_member, NT)
    target = jnp.where(mem >= 0, rnk * MEM + mem, -1)
    feats = held[...].T
    pieces = split(feats, 3)
    for b in range(4):
        goal = onehot(iota((256, POS), 0) + 256 * b == target).astype(BF16)
        moved = dot(pieces[0], goal, NT) + dot(pieces[1], goal, NT) + dot(pieces[2], goal, NT)
        turned[0, :, 256 * b : 256 * (b + 1)] = moved
    x = turned[0]
    for p in range(1, 4):
        turned[p] = pltpu.roll(x, POS - MEM * p, 1)
    c = jnp.concatenate([coefs[...]] * 4, axis=0).T
    own = jnp.sum(x * jnp.concatenate([c] * 8, axis=1), axis=0, keepdims=True)
    own = jnp.where(iota((GROUP, POS), 1) // MEM == iota((GROUP, POS), 0), own, 0.0)
    folded = own[:, 0:128]
    for b in range(1, 8):
        folded = folded + own[:, 128 * b : 128 * (b + 1)]
    folded = folded + pltpu.roll(folded, 64, 1)
    s = folded + pltpu.roll(folded, 32, 1)
    for delta in range(GROUP // 2 + 1):
        p, q = delta % 4, delta // 4
        for b in range(8):
            o = (b + q) % 8
            prod = turned[0, :, 128 * b : 128 * (b + 1)] * turned[p, :, 128 * o : 128 * (o + 1)]
            diag[delta : delta + 1, 128 * b : 128 * (b + 1)] = jnp.sum(prod, axis=0, keepdims=True)
    for delta in range(GROUP // 2 + 1, GROUP):
        diag[delta : delta + 1, :] = pltpu.roll(
            jnp.broadcast_to(diag[GROUP - delta : GROUP - delta + 1, :], (8, POS)), POS - MEM * delta, 1
        )[0:1, :]
    for b in range(8):
        block = diag[:, 128 * b : 128 * (b + 1)]
        for p in range(4):
            i = 4 * b + p
            wide = spread(block, p)
            gram[i] = pltpu.roll(wide, i, 0) if i else wide
    at = iota((GROUP, 128), 0)
    steps_total = None
    for sweep in range(2):
        p = jax.nn.sigmoid(s + offset)
        error = (p - y) * alive
        d = jnp.sqrt(p * (1.0 - p) * alive)
        b = d * (gram_times(gram, error) + s)
        for i in range(GROUP):
            row = gram[i] * (d * d[i : i + 1, :])
            work[i] = row + onehot(at == i)
        for k in range(GROUP):
            row = work[k]
            inverse = 1.0 / row[k : k + 1, :]
            scaled = jnp.where(at == k, 1.0 - inverse, row * inverse)
            b = b - b[k : k + 1, :] * scaled
            for i in range(k + 1, GROUP):
                work[i] = work[i] - row[i : i + 1, :] * scaled
        u = error - d * b
        s = s - MEMBER_STEP * (gram_times(gram, u) + MEMBER_RIDGE * s)
        steps_total = u * 0.25 if sweep == 0 else steps_total + u * 0.5
    steps[...] = steps_total
    final = (s + offset) * 0.25
    scores = jnp.sum(by_rank * dot_left(final, by_member, 2), axis=0, keepdims=True)
    for b in range(8):
        line = jnp.broadcast_to(scores[:, 128 * b : 128 * (b + 1)], (16, 128))
        back[16 * b : 16 * (b + 1), :] = jnp.where(
            iota((16, 128), 1) // CAP == iota((16, 128), 0), line, 0.0
        )


def owner_work(rows, coefs):
    return pl.pallas_call(
        owner_kernel,
        out_shape=[
            jax.ShapeDtypeStruct((DEVICES, 128), F32),
            jax.ShapeDtypeStruct((GROUP, 128), F32),
            jax.ShapeDtypeStruct((16, POS), I32),
        ],
        scratch_shapes=[
            pltpu.VMEM((4, 128, POS), F32),
            pltpu.VMEM((GROUP, POS), F32),
            pltpu.VMEM((GROUP, GROUP, 128), F32),
            pltpu.VMEM((GROUP, GROUP, 128), F32),
            pltpu.VMEM((POS, 128), F32),
            pltpu.VMEM((DEVICES, 128), F32),
        ],
        compiler_params=params(WIDE),
        name="owner_work",
    )(rows, coefs)


def coefs_kernel(rows, coefs, steps, lines, out, held):
    unpack(rows, held)
    mem = lines[0:1, :]
    by_rank = onehot((iota((GROUP, POS), 0) == lines[8:9, :]) & (mem >= 0))
    by_member = onehot((iota((128, POS), 0) % MEM) == mem)
    line = jnp.sum(
        by_rank * dot_left(steps[...] * 0.25, by_member.astype(BF16), 2), axis=0, keepdims=True
    )
    weighted = split(by_member[0:MEM, :] * line, 2)
    feats = split(held[...], 2)
    moved = dot(weighted[0], feats[0]) + dot(weighted[0], feats[1]) + dot(weighted[1], feats[0])
    out[...] = 0.25 * coefs[...] - moved


def new_coefs(rows, coefs, steps, lines):
    return pl.pallas_call(
        coefs_kernel,
        out_shape=jax.ShapeDtypeStruct((MEM, 128), F32),
        scratch_shapes=[pltpu.VMEM((POS, 128), F32)],
        compiler_params=params(16),
        name="new_coefs",
    )(rows, coefs, steps, lines)


def total_kernel(back, slots, out):
    slot = slots[...]
    mask = onehot(iota((DEVICES, OWN), 0) == slot // CAP).astype(BF16)
    moved = dot_left(back[...].T, mask, 2)
    keep = (iota((128, OWN), 0) % CAP) == slot % CAP
    out[...] = jnp.sum(jnp.where(keep, moved, 0.0), axis=0, keepdims=True)


def total_rows(back, slots):
    return pl.pallas_call(
        total_kernel,
        out_shape=jax.ShapeDtypeStruct((1, OWN), F32),
        compiler_params=params(16),
        name="total_rows",
    )(back, slots)


def ring_feature(value):
    pairs = [[(i, (i + k) % FEATURES) for i in range(FEATURES)] for k in range(FEATURES)]
    return [value] + [lax.ppermute(value, "feature", pairs[k]) for k in RING[1:]]


def sample_pairs(shift, first):
    pairs = []
    for i in range(SAMPLES):
        x, z, core = i // 8, (i // 2) % 4, i % 2
        if (core == 0) == first:
            z = (z + shift) % 4
        else:
            x = (x + shift) % 4
        pairs.append((i, (x * 4 + z) * 2 + core))
    return pairs


def gather_sample(value):
    early = jnp.concatenate(
        [value] + [lax.ppermute(value, "sample", sample_pairs(k, True)) for k in (1, 2, 3)], axis=0
    )
    late = [early] + [lax.ppermute(early, "sample", sample_pairs(k, False)) for k in (1, 2, 3)]
    return late + [lax.ppermute(v, "sample", [(i, i ^ 1) for i in range(SAMPLES)]) for v in late]


def exchange(value):
    return lax.all_to_all(value, ("sample", "feature"), split_axis=0, concat_axis=0, tiled=True)


def shards(
    feat_values,
    block_ids,
    fixed_weights,
    labels,
    prior_scores,
    member_feats,
    member_ids,
    member_coefs,
):
    members = member_ids.reshape(4, TILE)
    label_tiles = labels.reshape(TILES, TILE)
    prior_tiles = prior_scores.reshape(TILES, TILE)
    margin, chosen, own_ids, sent_ids, merge = first_margin(
        block_ids.T, members, feat_values, fixed_weights
    )
    margins = ring_feature(margin)
    packet = own_stats(margins, prior_tiles, label_tiles, sent_ids, merge, feat_values)
    margin, packet = lax.optimization_barrier((margin, packet))
    packed, slot_row = pack_rows(margin, members, label_tiles, member_feats)
    pieces = gather_sample(packet)
    message = second_margin(pieces, own_ids, chosen, margins, packed, feat_values)
    rows = exchange(message.reshape(DEVICES, 1, NOTE * 128)).reshape(DEVICES * NOTE, 128)
    weights = all_weights(pieces, fixed_weights)
    rows, weights = lax.optimization_barrier((rows, weights))
    back, steps, lines = owner_work(rows, member_coefs)
    returned = exchange(back[:, None, :])[:, 0, :]
    coefs = new_coefs(rows, member_coefs, steps, lines)
    total = total_rows(returned, slot_row)
    return (weights, coefs, total.reshape(OWN, 1))


def solution(mesh):
    both = ("sample", "feature")
    in_specs = (
        P("sample", "feature"),
        P("sample", "feature"),
        P("feature", None),
        P("sample"),
        P("sample"),
        P(both, None),
        P(both),
        P(both, None),
    )
    out_specs = (P("feature", None), P(both, None), P(both, None))
    return jax.shard_map(shards, mesh=mesh, in_specs=in_specs, out_specs=out_specs, check_vma=False)
```

time: 121 us -> 92.8 us (0.77)
  local copies, waits for them, and re-layouts: 23.2 us -> 1.4 us
  starting transfers between devices: 39.6 us -> 34.6 us
    unnamed x45 -> x15, local copies, waits for them, and re-layouts: 20.7 us -> 1.4 us
    all_to_all x3 -> x2, starting transfers between devices: 16.2 us -> 8.27 us  [exchange(): lax.all_to_all(value, ('sample', 'feature'), split_axis=0, concat_axis=0,...]
    ppermute x7 -> x10, starting transfers between devices: 15.3 us -> 21.1 us  [the longest x4 12.6 us: gather_sample(): lax.ppermute(v, 'sample', [(i, i ^ 1) for i in range(SAMPLES)])]
    ppermute x6 -> x3, waiting for transfers between devices: 0.02 us -> 3.06 us  [ring_feature(): lax.ppermute(value, 'feature', pairs[k])]
    ppermute x6 -> x3, starting transfers between devices: 8.22 us -> 5.29 us  [ring_feature(): lax.ppermute(value, 'feature', pairs[k])]
    all_to_all x3 -> x2, waiting for transfers between devices: 17.2 us -> 14.3 us  [exchange(): lax.all_to_all(value, ('sample', 'feature'), split_axis=0, concat_axis=0,...]
    concatenate x1 -> x0, local copies, waits for them, and re-layouts: 1.35 us -> none  [gather_sample(): return jnp.concatenate([value, other], axis=0)]
    ppermute x7 -> x10, waiting for transfers between devices: 5.35 us -> 6.04 us  [the longest x3 4.37 us: gather_sample(): lax.ppermute(value, 'sample', sample_pairs(k, True))]
  transfers between devices with their start and end apart: 16 -> 15, of which waited for: 6 -> 6; matrix products, arithmetic and copies ran while one was open for 6% -> 0% of each run, Pallas kernels for 22% -> 13%
where the time goes in v2:
time: 92.8 us; the launch traced here: 92.5 us
  starting transfers between devices  34.6 us (37%)
  Pallas kernels  32.3 us (35%)
  waiting for transfers between devices  23.4 us (25%)
  local copies, waits for them, and re-layouts  1.4 us (2%)
    all_to_all x2, waiting for transfers between devices, exchange(): lax.all_to_all(value, ('sample', 'feature'), split_axis=0, concat_axis=0,...  14.3 us
    ppermute x4, starting transfers between devices, gather_sample(): lax.ppermute(v, 'sample', [(i, i ^ 1) for i in range(SAMPLES)])  12.6 us
    pallas_call x1, Pallas kernels, all_weights(): pl.pallas_call(weights_kernel, in_specs=[HBM] + [ANY] * 8, out_specs=HBM,...  9.48 us
    all_to_all x2, starting transfers between devices, exchange(): lax.all_to_all(value, ('sample', 'feature'), split_axis=0, concat_axis=0,...  8.27 us
    pallas_call x1, Pallas kernels, owner_work(): pl.pallas_call(owner_kernel, out_shape=[jax.ShapeDtypeStruct((DEVICES, 12...  6.94 us
    pallas_call x1, Pallas kernels, second_margin(): pl.pallas_call(second_kernel, in_specs=[VMEM] * 3 + [HBM] + [VMEM] * 4 +...  5.71 us
    ppermute x3, starting transfers between devices, ring_feature(): lax.ppermute(value, 'feature', pairs[k])  5.29 us
    ppermute x3, starting transfers between devices, gather_sample(): lax.ppermute(early, 'sample', sample_pairs(k, False))  4.77 us
  transfers between devices with their start and end apart: 15, of which 6 were waited for; matrix products, arithmetic and copies ran while one was open for 0% of the time, Pallas kernels for 13%

profile of v2, /device:TPU:1, one launch (start us, length us, event | category | flops | bytes accessed | tf_op | source)
XLA Modules:
  0.0 92.5 jit_solution(6152535128018941390)
XLA Ops:
  0.6 0.7 copy-done.4
  1.3 0.7 copy-done.5
  2.0 4.6 %first_margin.1 = (f32[24,128]{1,0:T(8,128)S(1)}, f32[64,128]{1,0:T(8,128)S(1)}, f32[64,128]{1,0:T(8,128)S(1)}, f32[8,256]{1,0:T(8,128)S(1)}, f32[64,128]{1,0:T(8,128)S(1)}) custom-call(s32[4,16]{1,0:T(4,128)S(1)} %bitcast.19, s32[4,128]{1,0:T(4,128)S(1)} %bitcast.17, f32[2048,512]{1,0:T(8,128)} %feats.7, f32[8192,128]{1,0:T(8,128)} %weights.3), custom_call_target="tpu_custom_call" | custom-call | tf_op jit(solution)/shard_map/first_margin/pallas_call | solution.py:158
  6.6 3.8 %collective-permute-start.2 = (f32[24,128]{1,0:T(8,128)S(1)}, f32[24,128]{1,0:T(8,128)S(1)}, u32[]{:S(2)}, u32[]{:S(2)}) collective-permute-start(f32[24,128]{1,0:T(8,128)S(1)} %get-tuple-element.22.m0.margin.rest_0_), channel_id=1, source_target_pairs={{0,2},{1,3},{2,0},{3,1},{4,6},{5,7},{6,4},{7,5},{8,10},{9,11},{10,... | collective-permute-start | bytes 36872 | tf_op jit(solution)/shard_map/ppermute | solution.py:620
  10.4 0.8 collective-permute-start.1
  11.2 0.7 collective-permute-start
  11.9 1.1 %collective-permute-done.1.m2.rest_2_ = f32[24,128]{1,0:T(8,128)S(1)} collective-permute-done((f32[24,128]{1,0:T(8,128)S(1)}, f32[24,128]{1,0:T(8,128)S(1)}, u32[]{:S(2)}, u32[]{:S(2)}) %collective-permute-start.1) | collective-permute-done | bytes 12320 | tf_op jit(solution)/shard_map/ppermute | solution.py:620
  13.0 1.9 %collective-permute-done.m1.rest_1_ = f32[24,128]{1,0:T(8,128)S(1)} collective-permute-done((f32[24,128]{1,0:T(8,128)S(1)}, f32[24,128]{1,0:T(8,128)S(1)}, u32[]{:S(2)}, u32[]{:S(2)}) %collective-permute-start) | collective-permute-done | bytes 12320 | tf_op jit(solution)/shard_map/ppermute | solution.py:620
  15.0 2.6 %own_stats.1 = f32[72,256]{1,0:T(8,128)S(1)} custom-call(f32[24,128]{1,0:T(8,128)S(1)} %get-tuple-element.22.m0.margin.rest_0_, f32[24,128]{1,0:T(8,128)S(1)} %collective-permute-done.m1.rest_1_, f32[24,128]{1,0:T(8,128)S(1)} %collective-permute-done.1.m2.rest_2_, f32[24,128]{1,0:T(8,128)S(1)} %collective-permute-done.2.m3.rest_3_, f32[16,128]{1,0:T(8,128)S(1)} %bitcast.16, ...), custom_call_target="tpu_custom_call" | custom-call | tf_op jit(solution)/shard_map/own_stats/pallas_call | solution.py:200
  17.5 2.5 %collective-permute-start.5 = (f32[72,256]{1,0:T(8,128)S(1)}, f32[72,256]{1,0:T(8,128)S(1)}, u32[]{:S(2)}, u32[]{:S(2)}) collective-permute-start(f32[72,256]{1,0:T(8,128)S(1)} %own_stats.1), channel_id=1, source_target_pairs={{0,24},{4,100},{8,0},{12,108},{16,8},{20,116},{24,16},{28,124},{32... | collective-permute-start | bytes 221192 | tf_op jit(solution)/shard_map/ppermute | solution.py:637
  20.1 0.5 collective-permute-start.4
  20.6 0.6 collective-permute-start.3
  21.2 4.4 %collective-permute-done.3 = f32[72,256]{1,0:T(8,128)S(1)} collective-permute-done((f32[72,256]{1,0:T(8,128)S(1)}, f32[72,256]{1,0:T(8,128)S(1)}, u32[]{:S(2)}, u32[]{:S(2)}) %collective-permute-start.3) | collective-permute-done | bytes 73760 | tf_op jit(solution)/shard_map/ppermute | solution.py:637
  25.6 4.1 %collective-permute-start.8 = (f32[288,256]{1,0:T(8,128)S(1)}, f32[288,256]{1,0:T(8,128)S(1)}, u32[]{:S(2)}, u32[]{:S(2)}) collective-permute-start(f32[288,256]{1,0:T(8,128)S(1)} %constant_dynamic-update-slice_fusion.rest_4_.rest_0_), channel_id=1, source_target_pairs={{0,96},{4,28},{8,104},{12,4},{16,112},{20,12},{24,120},{28,20},{32... | collective-permute-start | bytes 884744 | tf_op jit(solution)/shard_map/ppermute | solution.py:639
  29.8 0.7 collective-permute-start.6
  30.4 4.5 %collective-permute-start.9 = (f32[288,256]{1,0:T(8,128)S(1)}, f32[288,256]{1,0:T(8,128)S(1)}, u32[]{:S(2)}, u32[]{:S(2)}) collective-permute-start(f32[288,256]{1,0:T(8,128)S(1)} %constant_dynamic-update-slice_fusion.rest_4_.rest_0_), channel_id=1, source_target_pairs={{0,4},{4,0},{8,12},{12,8},{16,20},{20,16},{24,28},{28,24},{32,36},... | collective-permute-start | bytes 884744 | tf_op jit(solution)/shard_map/ppermute | solution.py:640
  35.0 1.6 %collective-permute-done.8.rest_7_.rest_3_ = f32[288,256]{1,0:T(8,128)S(1)} collective-permute-done((f32[288,256]{1,0:T(8,128)S(1)}, f32[288,256]{1,0:T(8,128)S(1)}, u32[]{:S(2)}, u32[]{:S(2)}) %collective-permute-start.8) | collective-permute-done | bytes 294944 | tf_op jit(solution)/shard_map/ppermute | solution.py:639
  36.6 4.1 %collective-permute-start.12 = (f32[288,256]{1,0:T(8,128)S(1)}, f32[288,256]{1,0:T(8,128)S(1)}, u32[]{:S(2)}, u32[]{:S(2)}) collective-permute-start(f32[288,256]{1,0:T(8,128)S(1)} %collective-permute-done.8.rest_7_.rest_3_), channel_id=1, source_target_pairs={{0,4},{4,0},{8,12},{12,8},{16,20},{20,16},{24,28},{28,24},{32,36},... | collective-permute-start | bytes 884744 | tf_op jit(solution)/shard_map/ppermute | solution.py:640
  40.7 0.9 collective-permute-start.11
  41.6 3.1 %collective-permute-start.10 = (f32[288,256]{1,0:T(8,128)S(1)}, f32[288,256]{1,0:T(8,128)S(1)}, u32[]{:S(2)}, u32[]{:S(2)}) collective-permute-start(f32[288,256]{1,0:T(8,128)S(1)} %collective-permute-done.6.rest_5_.rest_1_), channel_id=1, source_target_pairs={{0,4},{4,0},{8,12},{12,8},{16,20},{20,16},{24,28},{28,24},{32,36},... | collective-permute-start | bytes 884744 | tf_op jit(solution)/shard_map/ppermute | solution.py:640
  44.7 1.1 %pack_rows.1 = (f32[1152,128]{1,0:T(8,128)S(1)}, s32[1,512]{1,0:T(1,128)S(1)}) custom-call(f32[24,128]{1,0:T(8,128)S(1)} %get-tuple-element.22.m0.margin.rest_0_, s32[4,128]{1,0:T(4,128)S(1)} %bitcast.18, f32[16,128]{1,0:T(8,128)S(1)} %bitcast.15, f32[512,128]{1,0:T(8,128)S(1)} %copy-done), custom_call_target="tpu_custom_call" | custom-call | tf_op jit(solution)/shard_map/pack_rows/pallas_call | solution.py:410
  45.8 0.0 collective-permute-done.10.rest_9_.rest_5_
  45.9 5.7 %second_margin.1 = f32[1152,128]{1,0:T(8,128)} custom-call(f32[64,128]{1,0:T(8,128)S(1)} %get-tuple-element.17.own_ids, f32[64,128]{1,0:T(8,128)S(1)} %get-tuple-element.18.chosen, f32[1152,128]{1,0:T(8,128)S(1)} %get-tuple-element.23.packed, f32[2048,512]{1,0:T(8,128)} %feats.7, f32[24,128]{1,0:T(8,128)S(1)} %get-tuple-element.22.m0.margin.rest_0_, ...), custom_call_target="tpu_custom_call" | custom-call | tf_op jit(solution)/shard_map/second_margin/pallas_call | solution.py:271
  51.6 3.8 %all-to-all-start = ((f32[128,1,1152]{2,1,0:T(1,128)}), f32[128,1,1152]{2,1,0:T(1,128)S(1)}, u32[]{:S(2)}, u32[]{:S(2)}) async-start(f32[128,1,1152]{2,1,0:T(1,128)} %bitcast.4), calls=%async_computation | async-start | bytes 1179648 | tf_op jit(solution)/shard_map/all_to_all | solution.py:644
  55.4 0.0 copy-start.1
  55.4 9.5 %all_weights.1 = f32[8192,128]{1,0:T(8,128)} custom-call(f32[8192,128]{1,0:T(8,128)} %weights.3, f32[288,256]{1,0:T(8,128)S(1)} %constant_dynamic-update-slice_fusion.rest_4_.rest_0_, f32[288,256]{1,0:T(8,128)S(1)} %collective-permute-done.6.rest_5_.rest_1_, f32[288,256]{1,0:T(8,128)S(1)} %collective-permute-done.7.rest_6_.rest_2_, ...), custom_call_target="tpu_custom_call" | custom-call | tf_op jit(solution)/shard_map/all_weights/pallas_call | solution.py:364
  64.9 5.5 %all-to-all-done = f32[128,1,1152]{2,1,0:T(1,128)S(1)} async-done(((f32[128,1,1152]{2,1,0:T(1,128)}), f32[128,1,1152]{2,1,0:T(1,128)S(1)}, u32[]{:S(2)}, u32[]{:S(2)}) %all-to-all-start) | async-done | bytes 589856 | tf_op jit(solution)/shard_map/all_to_all | solution.py:644
  70.4 6.9 %owner_work.1 = (f32[128,128]{1,0:T(8,128)}, f32[32,128]{1,0:T(8,128)S(1)}, s32[16,1024]{1,0:T(8,128)S(1)}) custom-call(f32[1152,128]{1,0:T(8,128)S(1)} %bitcast.11, f32[32,128]{1,0:T(8,128)S(1)} %copy-done.1), custom_call_target="tpu_custom_call" | custom-call | tf_op jit(solution)/shard_map/owner_work/pallas_call | solution.py:557
  77.3 4.4 %all-to-all-start.1 = ((f32[128,1,128]{2,1,0:T(1,128)}), f32[128,1,128]{2,1,0:T(1,128)S(1)}, u32[]{:S(2)}, u32[]{:S(2)}) async-start(f32[128,1,128]{2,1,0:T(1,128)} %bitcast.7), calls=%async_computation.1 | async-start | bytes 131072 | tf_op jit(solution)/shard_map/all_to_all | solution.py:644
  81.8 1.0 %new_coefs.1 = f32[32,128]{1,0:T(8,128)} custom-call(f32[1152,128]{1,0:T(8,128)S(1)} %bitcast.12, f32[32,128]{1,0:T(8,128)S(1)} %copy-done.1, f32[32,128]{1,0:T(8,128)S(1)} %get-tuple-element.27.steps, s32[16,1024]{1,0:T(8,128)S(1)} %get-tuple-element.28.lines), custom_call_target="tpu_custom_call" | custom-call | tf_op jit(solution)/shard_map/new_coefs/pallas_call | solution.py:592
  82.8 8.8 %all-to-all-done.1 = f32[128,1,128]{2,1,0:T(1,128)S(1)} async-done(((f32[128,1,128]{2,1,0:T(1,128)}), f32[128,1,128]{2,1,0:T(1,128)S(1)}, u32[]{:S(2)}, u32[]{:S(2)}) %all-to-all-start.1) | async-done | bytes 65568 | tf_op jit(solution)/shard_map/all_to_all | solution.py:644
  91.7 0.9 total_rows.1
  (22 shorter events, 0.1 us)
Async XLA Ops:
  0.6 0.7 copy-start.4
  1.3 0.7 copy-start.5
  2.0 13.0 %copy-start.2 = (f32[2048]{0:T(1024)S(1)}, f32[2048]{0:T(1024)}, u32[]{:S(2)}) copy-start(f32[2048]{0:T(1024)} %param.11) | copy-start | bytes 24580
  2.0 13.0 %copy-start.3 = (f32[2048]{0:T(1024)S(1)}, f32[2048]{0:T(1024)}, u32[]{:S(2)}) copy-start(f32[2048]{0:T(1024)} %param.12) | copy-start | bytes 24580
  6.6 38.1 %copy-start = (f32[512,128]{1,0:T(8,128)S(1)}, f32[512,128]{1,0:T(8,128)}, u32[]{:S(2)}) copy-start(f32[512,128]{1,0:T(8,128)} %feats.6) | copy-start | bytes 786436
  6.6 5.3 %collective-permute-start.2 = (f32[24,128]{1,0:T(8,128)S(1)}, f32[24,128]{1,0:T(8,128)S(1)}, u32[]{:S(2)}, u32[]{:S(2)}) collective-permute-start(f32[24,128]{1,0:T(8,128)S(1)} %get-tuple-element.22.m0.margin.rest_0_), channel_id=1, source_target_pairs={{0,2},{1,3},{2,0},{3,1},{4,6},{5,7},{6,4},{7,5},{8,10},{9,11},{10,... | collective-permute-start | bytes 36872 | tf_op jit(solution)/shard_map/ppermute | solution.py:620
  10.4 2.6 %collective-permute-start.1 = (f32[24,128]{1,0:T(8,128)S(1)}, f32[24,128]{1,0:T(8,128)S(1)}, u32[]{:S(2)}, u32[]{:S(2)}) collective-permute-start(f32[24,128]{1,0:T(8,128)S(1)} %get-tuple-element.22.m0.margin.rest_0_), channel_id=1, source_target_pairs={{0,3},{1,0},{2,1},{3,2},{4,7},{5,4},{6,5},{7,6},{8,11},{9,8},{10,9... | collective-permute-start | bytes 36872 | tf_op jit(solution)/shard_map/ppermute | solution.py:620
  11.2 3.8 %collective-permute-start = (f32[24,128]{1,0:T(8,128)S(1)}, f32[24,128]{1,0:T(8,128)S(1)}, u32[]{:S(2)}, u32[]{:S(2)}) collective-permute-start(f32[24,128]{1,0:T(8,128)S(1)} %get-tuple-element.22.m0.margin.rest_0_), channel_id=1, source_target_pairs={{0,1},{1,2},{2,3},{3,0},{4,5},{5,6},{6,7},{7,4},{8,9},{9,10},{10,1... | collective-permute-start | bytes 36872 | tf_op jit(solution)/shard_map/ppermute | solution.py:620
  17.5 8.1 %collective-permute-start.5 = (f32[72,256]{1,0:T(8,128)S(1)}, f32[72,256]{1,0:T(8,128)S(1)}, u32[]{:S(2)}, u32[]{:S(2)}) collective-permute-start(f32[72,256]{1,0:T(8,128)S(1)} %own_stats.1), channel_id=1, source_target_pairs={{0,24},{4,100},{8,0},{12,108},{16,8},{20,116},{24,16},{28,124},{32... | collective-permute-start | bytes 221192 | tf_op jit(solution)/shard_map/ppermute | solution.py:637
  20.1 5.5 %collective-permute-start.4 = (f32[72,256]{1,0:T(8,128)S(1)}, f32[72,256]{1,0:T(8,128)S(1)}, u32[]{:S(2)}, u32[]{:S(2)}) collective-permute-start(f32[72,256]{1,0:T(8,128)S(1)} %own_stats.1), channel_id=1, source_target_pairs={{0,16},{4,68},{8,24},{12,76},{16,0},{20,84},{24,8},{28,92},{32,48}... | collective-permute-start | bytes 221192 | tf_op jit(solution)/shard_map/ppermute | solution.py:637
  20.6 5.0 %collective-permute-start.3 = (f32[72,256]{1,0:T(8,128)S(1)}, f32[72,256]{1,0:T(8,128)S(1)}, u32[]{:S(2)}, u32[]{:S(2)}) collective-permute-start(f32[72,256]{1,0:T(8,128)S(1)} %own_stats.1), channel_id=1, source_target_pairs={{0,8},{4,36},{8,16},{12,44},{16,24},{20,52},{24,0},{28,60},{32,40}... | collective-permute-start | bytes 221192 | tf_op jit(solution)/shard_map/ppermute | solution.py:637
  25.6 10.9 %collective-permute-start.8 = (f32[288,256]{1,0:T(8,128)S(1)}, f32[288,256]{1,0:T(8,128)S(1)}, u32[]{:S(2)}, u32[]{:S(2)}) collective-permute-start(f32[288,256]{1,0:T(8,128)S(1)} %constant_dynamic-update-slice_fusion.rest_4_.rest_0_), channel_id=1, source_target_pairs={{0,96},{4,28},{8,104},{12,4},{16,112},{20,12},{24,120},{28,20},{32... | collective-permute-start | bytes 884744 | tf_op jit(solution)/shard_map/ppermute | solution.py:639
  29.8 11.0 %collective-permute-start.7 = (f32[288,256]{1,0:T(8,128)S(1)}, f32[288,256]{1,0:T(8,128)S(1)}, u32[]{:S(2)}, u32[]{:S(2)}) collective-permute-start(f32[288,256]{1,0:T(8,128)S(1)} %constant_dynamic-update-slice_fusion.rest_4_.rest_0_), channel_id=1, source_target_pairs={{0,64},{4,20},{8,72},{12,28},{16,80},{20,4},{24,88},{28,12},{32,96... | collective-permute-start | bytes 884744 | tf_op jit(solution)/shard_map/ppermute | solution.py:639
  29.8 11.9 %collective-permute-start.6 = (f32[288,256]{1,0:T(8,128)S(1)}, f32[288,256]{1,0:T(8,128)S(1)}, u32[]{:S(2)}, u32[]{:S(2)}) collective-permute-start(f32[288,256]{1,0:T(8,128)S(1)} %constant_dynamic-update-slice_fusion.rest_4_.rest_0_), channel_id=1, source_target_pairs={{0,32},{4,12},{8,40},{12,20},{16,48},{20,28},{24,56},{28,4},{32,64... | collective-permute-start | bytes 884744 | tf_op jit(solution)/shard_map/ppermute | solution.py:639
  30.4 15.4 %collective-permute-start.9 = (f32[288,256]{1,0:T(8,128)S(1)}, f32[288,256]{1,0:T(8,128)S(1)}, u32[]{:S(2)}, u32[]{:S(2)}) collective-permute-start(f32[288,256]{1,0:T(8,128)S(1)} %constant_dynamic-update-slice_fusion.rest_4_.rest_0_), channel_id=1, source_target_pairs={{0,4},{4,0},{8,12},{12,8},{16,20},{20,16},{24,28},{28,24},{32,36},... | collective-permute-start | bytes 884744 | tf_op jit(solution)/shard_map/ppermute | solution.py:640
  36.6 9.2 %collective-permute-start.12 = (f32[288,256]{1,0:T(8,128)S(1)}, f32[288,256]{1,0:T(8,128)S(1)}, u32[]{:S(2)}, u32[]{:S(2)}) collective-permute-start(f32[288,256]{1,0:T(8,128)S(1)} %collective-permute-done.8.rest_7_.rest_3_), channel_id=1, source_target_pairs={{0,4},{4,0},{8,12},{12,8},{16,20},{20,16},{24,28},{28,24},{32,36},... | collective-permute-start | bytes 884744 | tf_op jit(solution)/shard_map/ppermute | solution.py:640
  40.7 5.1 %collective-permute-start.11 = (f32[288,256]{1,0:T(8,128)S(1)}, f32[288,256]{1,0:T(8,128)S(1)}, u32[]{:S(2)}, u32[]{:S(2)}) collective-permute-start(f32[288,256]{1,0:T(8,128)S(1)} %collective-permute-done.7.rest_6_.rest_2_), channel_id=1, source_target_pairs={{0,4},{4,0},{8,12},{12,8},{16,20},{20,16},{24,28},{28,24},{32,36},... | collective-permute-start | bytes 884744 | tf_op jit(solution)/shard_map/ppermute | solution.py:640
  41.6 4.3 %collective-permute-start.10 = (f32[288,256]{1,0:T(8,128)S(1)}, f32[288,256]{1,0:T(8,128)S(1)}, u32[]{:S(2)}, u32[]{:S(2)}) collective-permute-start(f32[288,256]{1,0:T(8,128)S(1)} %collective-permute-done.6.rest_5_.rest_1_), channel_id=1, source_target_pairs={{0,4},{4,0},{8,12},{12,8},{16,20},{20,16},{24,28},{28,24},{32,36},... | collective-permute-start | bytes 884744 | tf_op jit(solution)/shard_map/ppermute | solution.py:640
  51.6 18.8 %all-to-all-start = ((f32[128,1,1152]{2,1,0:T(1,128)}), f32[128,1,1152]{2,1,0:T(1,128)S(1)}, u32[]{:S(2)}, u32[]{:S(2)}) async-start(f32[128,1,1152]{2,1,0:T(1,128)} %bitcast.4), calls=%async_computation | async-start | bytes 1179648 | tf_op jit(solution)/shard_map/all_to_all | solution.py:644
  55.4 15.0 %copy-start.1 = (f32[32,128]{1,0:T(8,128)S(1)}, f32[32,128]{1,0:T(8,128)}, u32[]{:S(2)}) copy-start(f32[32,128]{1,0:T(8,128)} %coefs.3) | copy-start | bytes 49156
  77.3 14.3 %all-to-all-start.1 = ((f32[128,1,128]{2,1,0:T(1,128)}), f32[128,1,128]{2,1,0:T(1,128)S(1)}, u32[]{:S(2)}, u32[]{:S(2)}) async-start(f32[128,1,128]{2,1,0:T(1,128)} %bitcast.7), calls=%async_computation.1 | async-start | bytes 131072 | tf_op jit(solution)/shard_map/all_to_all | solution.py:644

commit v3 on v2

--- a/solution.py
+++ b/solution.py
@@ -31,6 +31,7 @@
 NOTE = CAP + 1
 MEM = 32
 GROUP = 32
+PIVOTS = 4
 RING = (0, 1, 3, 2)
 
 NN = (((1,), (0,)), ((), ()))
@@ -103,19 +104,29 @@
 
 
 def margin_kernel(
-    ids, members, feats, weights, out, chosen, own, sent, merge, held, row_sems, sems
+    ids, members, feats, weights, out, chosen, held, table, own, sums, small_sems, row_sems, sems
 ):
+    early = [
+        pltpu.make_async_copy(ids, table, small_sems.at[0]),
+        pltpu.make_async_copy(members, own, small_sems.at[1]),
+    ]
+    for copy in early:
+        copy.start()
     copies = fetch(feats, held, sems)
+    early[0].wait()
     picked = [
         pltpu.make_async_copy(
-            weights.at[pl.ds(ids[e % SLOTS, e // SLOTS], 1)], chosen.at[pl.ds(e, 1)], row_sems.at[e]
+            weights.at[pl.ds(table[e % SLOTS, e // SLOTS], 1)],
+            chosen.at[pl.ds(e, 1)],
+            row_sems.at[e],
         )
         for e in range(ENTRIES)
     ]
     for copy in picked:
         copy.start()
-
-    owner = members[...] // MEM
+    early[1].wait()
+
+    owner = own[...] // MEM
     column = owner.astype(F32).T.astype(I32)
     sub, lane = iota((TILE, TILE), 0), iota((TILE, TILE), 1)
     for a in range(4):
@@ -129,6 +140,41 @@
         out[TILES + a : TILES + a + 1, :] = owner[a : a + 1, :].astype(F32) * CAP + rank
     out[TILES + 4 :, :] = jnp.zeros((4, TILE), F32)
 
+    for copy in picked:
+        copy.wait()
+    each = TILES // CHUNKS
+    for c in range(CHUNKS):
+        copies[c].wait()
+        for t in range(c * each, (c + 1) * each):
+            sums[t * TILE : (t + 1) * TILE, :] = tile_margin(held, chosen, t)
+    for t in range(TILES):
+        across = sums[t * TILE : (t + 1) * TILE, :].T
+        out[t : t + 1, :] = jnp.sum(across, axis=0, keepdims=True)
+
+
+def first_margin(ids, members, feats, weights):
+    return pl.pallas_call(
+        margin_kernel,
+        in_specs=[HBM, HBM, HBM, HBM],
+        out_shape=[
+            jax.ShapeDtypeStruct((TILES + 8, TILE), F32),
+            jax.ShapeDtypeStruct((ENTRIES, BLK), F32),
+            pltpu.VMEM(feats.shape, F32),
+        ],
+        scratch_shapes=[
+            pltpu.SMEM(ids.shape, I32),
+            pltpu.VMEM(members.shape, I32),
+            pltpu.VMEM((TILES * TILE, BLK), F32),
+            pltpu.SemaphoreType.DMA((2,)),
+            pltpu.SemaphoreType.DMA((ENTRIES,)),
+            pltpu.SemaphoreType.DMA((CHUNKS,)),
+        ],
+        compiler_params=params(47),
+        name="first_margin",
+    )(ids, members, feats, weights)
+
+
+def table_kernel(ids, limit, own, sent, merge):
     at, of = iota((ENTRIES, 128), 0), iota((ENTRIES, 128), 1) % ENTRIES
     rows = jnp.zeros((ENTRIES, 128), I32)
     line = jnp.zeros((8, 128), I32)
@@ -139,52 +185,32 @@
     same = rows == line[0:1, :]
     repeat = jnp.sum(onehot(same & (at < of)), axis=0, keepdims=True)
     own[...] = rows.astype(F32)
-    kept = jnp.where(repeat > 0.0, weights.shape[0], line[0:1, :]).astype(F32)
+    kept = jnp.where(repeat > 0.0, limit, line[0:1, :]).astype(F32)
     sent[...] = jnp.broadcast_to(jnp.concatenate([kept, kept], axis=1), (8, 256))
     earlier = jnp.sum(onehot(same & (of < at)), axis=1, keepdims=True)
     merge[...] = jnp.where(earlier > 0.0, 0.0, onehot(same))
 
-    for copy in picked:
-        copy.wait()
-    each = TILES // CHUNKS
-    for c in range(CHUNKS):
-        copies[c].wait()
-        for t in range(c * each, (c + 1) * each):
-            out[t : t + 1, :] = jnp.sum(tile_margin(held, chosen, t).T, axis=0, keepdims=True)
-
-
-def first_margin(ids, members, feats, weights):
+
+def block_tables(ids, limit):
+    def kernel(ids, *refs):
+        table_kernel(ids, limit, *refs)
+
     table = jax.ShapeDtypeStruct((ENTRIES, BLK), F32)
     return pl.pallas_call(
-        margin_kernel,
-        in_specs=[SMEM, VMEM, HBM, HBM],
-        out_shape=[
-            jax.ShapeDtypeStruct((TILES + 8, TILE), F32),
-            table,
-            table,
-            jax.ShapeDtypeStruct((8, 2 * BLK), F32),
-            table,
-        ],
-        scratch_shapes=[
-            pltpu.VMEM((TILES * TILE, SLOTS * BLK), F32),
-            pltpu.SemaphoreType.DMA((ENTRIES,)),
-            pltpu.SemaphoreType.DMA((CHUNKS,)),
-        ],
-        compiler_params=params(WIDE),
-        name="first_margin",
-    )(ids, members, feats, weights)
-
-
-def stats_kernel(m0, m1, m2, m3, prior, labels, ids, merge, feats, out, held, raw, sems):
-    copies = fetch(feats, held, sems)
+        kernel,
+        in_specs=[SMEM],
+        out_shape=[table, jax.ShapeDtypeStruct((8, 2 * BLK), F32), table],
+        compiler_params=params(16),
+        name="block_tables",
+    )(ids)
+
+
+def stats_kernel(m0, m1, m2, m3, prior, labels, ids, merge, held, out, raw):
     margin = (m0[0:TILES, :] + m1[0:TILES, :]) + (m2[0:TILES, :] + m3[0:TILES, :])
     probs = jax.nn.sigmoid(margin + prior[...])
     residual = (probs - labels[...]).T
     curvature = (probs * (1.0 - probs)).T
-    each = TILES // CHUNKS
     for t in range(TILES):
-        if t % each == 0:
-            copies[t // each].wait()
         r = jnp.broadcast_to(residual[:, t : t + 1], (TILE, BLK))
         c = jnp.broadcast_to(curvature[:, t : t + 1], (TILE, BLK))
         for k in range(SLOTS):
@@ -199,43 +225,51 @@
 def own_stats(margins, prior, labels, ids, merge, feats):
     return pl.pallas_call(
         stats_kernel,
-        in_specs=[VMEM] * 8 + [HBM],
+        in_specs=[VMEM] * 9,
         out_shape=jax.ShapeDtypeStruct((PACKET, 2 * BLK), F32),
         scratch_shapes=[
-            pltpu.VMEM((TILES * TILE, SLOTS * BLK), F32),
             pltpu.VMEM((ENTRIES, 2 * BLK), F32),
-            pltpu.SemaphoreType.DMA((CHUNKS,)),
         ],
-        compiler_params=params(WIDE),
+        compiler_params=params(16),
         name="own_stats",
     )(*margins, prior, labels, ids, merge, feats)
 
 
-def second_kernel(own_ids, chosen, packed, feats, *rest):
-    margins, pieces, (out, held, sent, slots, sems, piece_sems) = rest[:4], rest[4:12], rest[12:]
-    arrivals = [
-        pltpu.make_async_copy(piece, sent.at[pl.ds(4 * PACKET * i, 4 * PACKET)], piece_sems.at[i])
-        for i, piece in enumerate(pieces)
-    ]
-    for copy in arrivals:
-        copy.start()
-    copies = fetch(feats, held, sems)
+def sum_pieces(own_ids, pieces):
     lane = iota((1, 128), 1)
     acc = None
-    for pair in range(SAMPLES // 2):
-        a, b = 2 * pair, 2 * pair + 1
-        if a % 4 == 0:
-            arrivals[a // 4].wait()
-        a, b = a * PACKET, b * PACKET
-        ids = jnp.where(
-            lane < ENTRIES,
-            sent[a + ENTRIES : a + ENTRIES + 1, 0:128],
-            sent[b + ENTRIES : b + ENTRIES + 1, 0:128],
-        )
-        mask = onehot(own_ids[...] == ids).astype(BF16)
-        both = jnp.concatenate([sent[a : a + ENTRIES, :], sent[b : b + ENTRIES, :]], axis=0)
-        term = dot_right(mask, both, 2)
-        acc = term if acc is None else acc + term
+    for piece in pieces:
+        for a in (0, 2 * PACKET):
+            b = a + PACKET
+            ids = jnp.where(
+                lane < ENTRIES,
+                piece[a + ENTRIES : a + ENTRIES + 1, 0:128],
+                piece[b + ENTRIES : b + ENTRIES + 1, 0:128],
+            )
+            mask = onehot(own_ids[...] == ids).astype(BF16)
+            both = jnp.concatenate([piece[a : a + ENTRIES, :], piece[b : b + ENTRIES, :]], axis=0)
+            term = dot_right(mask, both, 2)
+            acc = term if acc is None else acc + term
+    return acc
+
+
+def near_kernel(own_ids, *rest):
+    pieces, out = rest[:4], rest[4]
+    out[...] = sum_pieces(own_ids, pieces)
+
+
+def near_sums(own_ids, pieces):
+    return pl.pallas_call(
+        near_kernel,
+        out_shape=jax.ShapeDtypeStruct((ENTRIES, 2 * BLK), F32),
+        compiler_params=params(16),
+        name="near_sums",
+    )(own_ids, *pieces)
+
+
+def second_kernel(own_ids, chosen, packed, near, feats, *rest):
+    margins, pieces, (out, slots) = rest[:4], rest[4:8], rest[8:]
+    acc = near[...] + sum_pieces(own_ids, pieces)
     w = chosen[...]
     w = w - STEP_SIZE * (acc[:, :BLK] + FIXED_RIDGE * w) / (acc[:, BLK:] + 1.0)
     ones = jnp.ones((BLK, 128), BF16)
@@ -249,8 +283,7 @@
     result = None
     lanes = (iota((TILE, 128), 1) % 32).astype(F32)
     for t in range(0, TILES, 2):
-        copies[t // 2].wait()
-        both = [tile_margin(held, w, t), tile_margin(held, w, t + 1)]
+        both = [tile_margin(feats, w, t), tile_margin(feats, w, t + 1)]
         margin = dot_left(jnp.concatenate(both, axis=0), ones, 2)
         place = [
             lanes == jnp.broadcast_to(column[:, q : q + 1], (TILE, 128)) for q in (t, t + 1)
@@ -267,21 +300,17 @@
         out[at : at + 1, :] = packed[at : at + 1, :] + result[d : d + 1, :]
 
 
-def second_margin(pieces, own_ids, chosen, margins, packed, feats):
+def second_margin(near, pieces, own_ids, chosen, margins, packed, feats):
     return pl.pallas_call(
         second_kernel,
-        in_specs=[VMEM] * 3 + [HBM] + [VMEM] * 4 + [ANY] * 8,
+        in_specs=[VMEM] * 13,
         out_shape=jax.ShapeDtypeStruct((DEVICES * NOTE, 128), F32),
         scratch_shapes=[
-            pltpu.VMEM((TILES * TILE, SLOTS * BLK), F32),
-            pltpu.VMEM((SAMPLES * PACKET, 2 * BLK), F32),
             pltpu.VMEM((TILES, TILE), F32),
-            pltpu.SemaphoreType.DMA((CHUNKS,)),
-            pltpu.SemaphoreType.DMA((8,)),
         ],
-        compiler_params=params(WIDE),
+        compiler_params=params(16),
         name="second_margin",
-    )(own_ids, chosen, packed, feats, *margins, *pieces)
+    )(own_ids, chosen, packed, near, feats, *margins, *pieces)
 
 
 def gathered_place(source):
@@ -414,7 +443,7 @@
             jax.ShapeDtypeStruct((1, OWN), I32),
         ],
         scratch_shapes=[pltpu.VMEM((OWN, 128), F32)],
-        compiler_params=params(WIDE),
+        compiler_params=params(16),
         name="pack_rows",
     )(margin, members, labels, feats)
 
@@ -491,11 +520,11 @@
     alive = dot(by_rank.astype(BF16), by_member, NT)
     target = jnp.where(mem >= 0, rnk * MEM + mem, -1)
     feats = held[...].T
-    pieces = split(feats, 3)
+    pieces = jnp.concatenate(split(feats, 2), axis=0)
     for b in range(4):
         goal = onehot(iota((256, POS), 0) + 256 * b == target).astype(BF16)
-        moved = dot(pieces[0], goal, NT) + dot(pieces[1], goal, NT) + dot(pieces[2], goal, NT)
-        turned[0, :, 256 * b : 256 * (b + 1)] = moved
+        moved = dot(pieces, goal, NT)
+        turned[0, :, 256 * b : 256 * (b + 1)] = moved[0:128, :] + moved[128:256, :]
     x = turned[0]
     for p in range(1, 4):
         turned[p] = pltpu.roll(x, POS - MEM * p, 1)
@@ -533,13 +562,22 @@
         for i in range(GROUP):
             row = gram[i] * (d * d[i : i + 1, :])
             work[i] = row + onehot(at == i)
-        for k in range(GROUP):
-            row = work[k]
-            inverse = 1.0 / row[k : k + 1, :]
-            scaled = jnp.where(at == k, 1.0 - inverse, row * inverse)
-            b = b - b[k : k + 1, :] * scaled
-            for i in range(k + 1, GROUP):
-                work[i] = work[i] - row[i : i + 1, :] * scaled
+        for k in range(0, GROUP, PIVOTS):
+            panel = [work[k + q] for q in range(PIVOTS)]
+            taken = []
+            for q in range(PIVOTS):
+                row = panel[q]
+                inverse = 1.0 / row[k + q : k + q + 1, :]
+                scaled = jnp.where(at == k + q, 1.0 - inverse, row * inverse)
+                for r in range(q + 1, PIVOTS):
+                    panel[r] = panel[r] - row[k + r : k + r + 1, :] * scaled
+                b = b - b[k + q : k + q + 1, :] * scaled
+                taken.append((row, scaled))
+            for i in range(k + PIVOTS, GROUP):
+                rest = work[i]
+                for row, scaled in taken:
+                    rest = rest - row[i : i + 1, :] * scaled
+                work[i] = rest
         u = error - d * b
         s = s - MEMBER_STEP * (gram_times(gram, u) + MEMBER_RIDGE * s)
         steps_total = u * 0.25 if sweep == 0 else steps_total + u * 0.5
@@ -632,12 +670,29 @@
     return pairs
 
 
-def gather_sample(value):
-    early = jnp.concatenate(
-        [value] + [lax.ppermute(value, "sample", sample_pairs(k, True)) for k in (1, 2, 3)], axis=0
-    )
+def join_kernel(*refs):
+    out = refs[-1]
+    for i, ref in enumerate(refs[:-1]):
+        out[i * PACKET : (i + 1) * PACKET, :] = ref[...]
+
+
+def join(packets):
+    return pl.pallas_call(
+        join_kernel,
+        out_shape=jax.ShapeDtypeStruct((len(packets) * PACKET, 2 * BLK), F32),
+        compiler_params=params(16),
+        name="join",
+    )(*packets)
+
+
+def gather_early(value):
+    return join([value] + [lax.ppermute(value, "sample", sample_pairs(k, True)) for k in (1, 2, 3)])
+
+
+def gather_late(early):
     late = [early] + [lax.ppermute(early, "sample", sample_pairs(k, False)) for k in (1, 2, 3)]
-    return late + [lax.ppermute(v, "sample", [(i, i ^ 1) for i in range(SAMPLES)]) for v in late]
+    other = [lax.ppermute(v, "sample", [(i, i ^ 1) for i in range(SAMPLES)]) for v in late]
+    return late, other
 
 
 def exchange(value):
@@ -657,16 +712,26 @@
     members = member_ids.reshape(4, TILE)
     label_tiles = labels.reshape(TILES, TILE)
     prior_tiles = prior_scores.reshape(TILES, TILE)
-    margin, chosen, own_ids, sent_ids, merge = first_margin(
-        block_ids.T, members, feat_values, fixed_weights
+    ids = block_ids.T
+    margin, chosen, held = first_margin(
+        pltpu.with_memory_space_constraint(ids, pltpu.HBM),
+        pltpu.with_memory_space_constraint(members, pltpu.HBM),
+        feat_values,
+        fixed_weights,
     )
+    margin, ids = lax.optimization_barrier((margin, ids))
+    own_ids, sent_ids, merge = block_tables(ids, fixed_weights.shape[0])
     margins = ring_feature(margin)
-    packet = own_stats(margins, prior_tiles, label_tiles, sent_ids, merge, feat_values)
+    packet = own_stats(margins, prior_tiles, label_tiles, sent_ids, merge, held)
     margin, packet = lax.optimization_barrier((margin, packet))
     packed, slot_row = pack_rows(margin, members, label_tiles, member_feats)
-    pieces = gather_sample(packet)
-    message = second_margin(pieces, own_ids, chosen, margins, packed, feat_values)
+    early = gather_early(packet)
+    early, packed = lax.optimization_barrier((early, packed))
+    late, other = gather_late(early)
+    near = near_sums(own_ids, late)
+    message = second_margin(near, other, own_ids, chosen, margins, packed, held)
     rows = exchange(message.reshape(DEVICES, 1, NOTE * 128)).reshape(DEVICES * NOTE, 128)
+    pieces = late + other
     weights = all_weights(pieces, fixed_weights)
     rows, weights = lax.optimization_barrier((rows, weights))
     back, steps, lines = owner_work(rows, member_coefs)

time: 92.8 us -> 84.4 us (0.909)
  Pallas kernels: 32.3 us -> 26.4 us
  local copies, waits for them, and re-layouts: 1.4 us -> 0.03 us
  waiting for transfers between devices: 23.4 us -> 22.4 us
    pallas_call x3 -> x6, Pallas kernels: 12.9 us -> 8.47 us  [the longest x1 3.68 us: first_margin(): pl.pallas_call(margin_kernel, in_specs=[HBM, HBM, HBM, HBM], out_shape=[j...]
    pallas_call x1, Pallas kernels: 6.94 us -> 5.4 us  [owner_work(): pl.pallas_call(owner_kernel, out_shape=[jax.ShapeDtypeStruct((DEVICES, 12...]
    unnamed x15 -> x12, local copies, waits for them, and re-layouts: 1.4 us -> 0.03 us
  transfers between devices with their start and end apart: 15 -> 15, of which waited for: 6 -> 8; matrix products, arithmetic and copies ran while one was open for 0% -> 0% of each run, Pallas kernels for 13% -> 15%
where the time goes in v3:
time: 84.4 us; the launch traced here: 84.2 us
  starting transfers between devices  34.6 us (41%)
  Pallas kernels  26.4 us (31%)
  waiting for transfers between devices  22.4 us (27%)
    all_to_all x2, waiting for transfers between devices, exchange(): lax.all_to_all(value, ('sample', 'feature'), split_axis=0, concat_axis=0,...  14.3 us
    ppermute x4, starting transfers between devices, gather_late(): lax.ppermute(v, 'sample', [(i, i ^ 1) for i in range(SAMPLES)])  12.6 us
    pallas_call x1, Pallas kernels, all_weights(): pl.pallas_call(weights_kernel, in_specs=[HBM] + [ANY] * 8, out_specs=HBM,...  9.48 us
    all_to_all x2, starting transfers between devices, exchange(): lax.all_to_all(value, ('sample', 'feature'), split_axis=0, concat_axis=0,...  8.25 us
    pallas_call x1, Pallas kernels, owner_work(): pl.pallas_call(owner_kernel, out_shape=[jax.ShapeDtypeStruct((DEVICES, 12...  5.4 us
    ppermute x3, starting transfers between devices, ring_feature(): lax.ppermute(value, 'feature', pairs[k])  5.29 us
    ppermute x3, starting transfers between devices, gather_late(): lax.ppermute(early, 'sample', sample_pairs(k, False))  4.77 us
    pallas_call x1, Pallas kernels, first_margin(): pl.pallas_call(margin_kernel, in_specs=[HBM, HBM, HBM, HBM], out_shape=[j...  3.68 us
  transfers between devices with their start and end apart: 15, of which 8 were waited for; matrix products, arithmetic and copies ran while one was open for 0% of the time, Pallas kernels for 15%

profile of v3, /device:TPU:1, one launch (start us, length us, event | category | flops | bytes accessed | tf_op | source)
XLA Modules:
  0.0 84.2 jit_solution(13633168230298279564)
XLA Ops:
  0.7 3.7 %first_margin.1 = (f32[24,128]{1,0:T(8,128)S(1)}, f32[64,128]{1,0:T(8,128)S(1)}, f32[2048,512]{1,0:T(8,128)S(1)}) custom-call(s32[4,16]{1,0:T(4,128)} %bitcast.19, s32[4,128]{1,0:T(4,128)} %bitcast.17, f32[2048,512]{1,0:T(8,128)} %feats.2, f32[8192,128]{1,0:T(8,128)} %weights.3), custom_call_target="tpu_custom_call" | custom-call | tf_op jit(solution)/shard_map/first_margin/pallas_call | solution.py:156
  4.4 3.8 %collective-permute-start.2 = (f32[24,128]{1,0:T(8,128)S(1)}, f32[24,128]{1,0:T(8,128)S(1)}, u32[]{:S(2)}, u32[]{:S(2)}) collective-permute-start(f32[24,128]{1,0:T(8,128)S(1)} %get-tuple-element.31.m0.margin.rest_0_), channel_id=1, source_target_pairs={{0,2},{1,3},{2,0},{3,1},{4,6},{5,7},{6,4},{7,5},{8,10},{9,11},{10,... | collective-permute-start | bytes 36872 | tf_op jit(solution)/shard_map/ppermute | solution.py:658
  8.2 0.8 collective-permute-start.1
  9.0 0.7 collective-permute-start
  9.7 0.7 block_tables.1
  10.4 0.4 collective-permute-done.1.m2.rest_2_
  10.8 1.9 %collective-permute-done.m1.rest_1_ = f32[24,128]{1,0:T(8,128)S(1)} collective-permute-done((f32[24,128]{1,0:T(8,128)S(1)}, f32[24,128]{1,0:T(8,128)S(1)}, u32[]{:S(2)}, u32[]{:S(2)}) %collective-permute-start) | collective-permute-done | bytes 12320 | tf_op jit(solution)/shard_map/ppermute | solution.py:658
  12.7 1.3 %own_stats.1.refs_0_ = f32[72,256]{1,0:T(8,128)S(1)} custom-call(f32[24,128]{1,0:T(8,128)S(1)} %get-tuple-element.31.m0.margin.rest_0_, f32[24,128]{1,0:T(8,128)S(1)} %collective-permute-done.m1.rest_1_, f32[24,128]{1,0:T(8,128)S(1)} %collective-permute-done.1.m2.rest_2_, f32[24,128]{1,0:T(8,128)S(1)} %collective-permute-done.2.m3.rest_3_, ...), custom_call_target="tpu_custom_call" | custom-call | tf_op jit(solution)/shard_map/own_stats/pallas_call | solution.py:226
  14.0 2.5 %collective-permute-start.5 = (f32[72,256]{1,0:T(8,128)S(1)}, f32[72,256]{1,0:T(8,128)S(1)}, u32[]{:S(2)}, u32[]{:S(2)}) collective-permute-start(f32[72,256]{1,0:T(8,128)S(1)} %own_stats.1.refs_0_), channel_id=1, source_target_pairs={{0,24},{4,100},{8,0},{12,108},{16,8},{20,116},{24,16},{28,124},{32... | collective-permute-start | bytes 221192 | tf_op jit(solution)/shard_map/ppermute | solution.py:689
  16.5 0.5 collective-permute-start.4
  17.1 0.6 collective-permute-start.3
  17.7 1.1 %pack_rows.1 = (f32[1152,128]{1,0:T(8,128)S(1)}, s32[1,512]{1,0:T(1,128)S(1)}) custom-call(f32[24,128]{1,0:T(8,128)S(1)} %get-tuple-element.31.m0.margin.rest_0_, s32[4,128]{1,0:T(4,128)S(1)} %bitcast.18, f32[16,128]{1,0:T(8,128)S(1)} %bitcast.15, f32[512,128]{1,0:T(8,128)S(1)} %copy-done), custom_call_target="tpu_custom_call" | custom-call | tf_op jit(solution)/shard_map/pack_rows/pallas_call | solution.py:439
  18.8 2.5 %collective-permute-done.4.refs_2_ = f32[72,256]{1,0:T(8,128)S(1)} collective-permute-done((f32[72,256]{1,0:T(8,128)S(1)}, f32[72,256]{1,0:T(8,128)S(1)}, u32[]{:S(2)}, u32[]{:S(2)}) %collective-permute-start.4) | collective-permute-done | bytes 73760 | tf_op jit(solution)/shard_map/ppermute | solution.py:689
  21.3 0.7 collective-permute-done.3.refs_1_
  22.1 4.1 %collective-permute-start.8 = (f32[288,256]{1,0:T(8,128)S(1)}, f32[288,256]{1,0:T(8,128)S(1)}, u32[]{:S(2)}, u32[]{:S(2)}) collective-permute-start(f32[288,256]{1,0:T(8,128)S(1)} %join.1.rest_0_), channel_id=1, source_target_pairs={{0,96},{4,28},{8,104},{12,4},{16,112},{20,12},{24,120},{28,20},{32... | collective-permute-start | bytes 884744 | tf_op jit(solution)/shard_map/ppermute | solution.py:693
  26.2 0.7 collective-permute-start.6
  26.8 4.5 %collective-permute-start.9 = (f32[288,256]{1,0:T(8,128)S(1)}, f32[288,256]{1,0:T(8,128)S(1)}, u32[]{:S(2)}, u32[]{:S(2)}) collective-permute-start(f32[288,256]{1,0:T(8,128)S(1)} %join.1.rest_0_), channel_id=1, source_target_pairs={{0,4},{4,0},{8,12},{12,8},{16,20},{20,16},{24,28},{28,24},{32,36},... | collective-permute-start | bytes 884744 | tf_op jit(solution)/shard_map/ppermute | solution.py:694
  31.4 1.6 %collective-permute-done.8.rest_3_ = f32[288,256]{1,0:T(8,128)S(1)} collective-permute-done((f32[288,256]{1,0:T(8,128)S(1)}, f32[288,256]{1,0:T(8,128)S(1)}, u32[]{:S(2)}, u32[]{:S(2)}) %collective-permute-start.8) | collective-permute-done | bytes 294944 | tf_op jit(solution)/shard_map/ppermute | solution.py:693
  33.0 4.1 %collective-permute-start.12 = (f32[288,256]{1,0:T(8,128)S(1)}, f32[288,256]{1,0:T(8,128)S(1)}, u32[]{:S(2)}, u32[]{:S(2)}) collective-permute-start(f32[288,256]{1,0:T(8,128)S(1)} %collective-permute-done.8.rest_3_), channel_id=1, source_target_pairs={{0,4},{4,0},{8,12},{12,8},{16,20},{20,16},{24,28},{28,24},{32,36},... | collective-permute-start | bytes 884744 | tf_op jit(solution)/shard_map/ppermute | solution.py:694
  37.1 0.9 %collective-permute-start.11 = (f32[288,256]{1,0:T(8,128)S(1)}, f32[288,256]{1,0:T(8,128)S(1)}, u32[]{:S(2)}, u32[]{:S(2)}) collective-permute-start(f32[288,256]{1,0:T(8,128)S(1)} %collective-permute-done.7.rest_2_), channel_id=1, source_target_pairs={{0,4},{4,0},{8,12},{12,8},{16,20},{20,16},{24,28},{28,24},{32,36},... | collective-permute-start | bytes 884744 | tf_op jit(solution)/shard_map/ppermute | solution.py:694
  38.0 3.1 %collective-permute-start.10 = (f32[288,256]{1,0:T(8,128)S(1)}, f32[288,256]{1,0:T(8,128)S(1)}, u32[]{:S(2)}, u32[]{:S(2)}) collective-permute-start(f32[288,256]{1,0:T(8,128)S(1)} %collective-permute-done.6.rest_1_), channel_id=1, source_target_pairs={{0,4},{4,0},{8,12},{12,8},{16,20},{20,16},{24,28},{28,24},{32,36},... | collective-permute-start | bytes 884744 | tf_op jit(solution)/shard_map/ppermute | solution.py:694
  41.1 0.3 near_sums.1.near
  41.4 0.9 %collective-permute-done.10.rest_5_ = f32[288,256]{1,0:T(8,128)S(1)} collective-permute-done((f32[288,256]{1,0:T(8,128)S(1)}, f32[288,256]{1,0:T(8,128)S(1)}, u32[]{:S(2)}, u32[]{:S(2)}) %collective-permute-start.10) | collective-permute-done | bytes 294944 | tf_op jit(solution)/shard_map/ppermute | solution.py:694
  42.3 2.5 %second_margin.1 = f32[1152,128]{1,0:T(8,128)} custom-call(f32[64,128]{1,0:T(8,128)S(1)} %get-tuple-element.24.own_ids, f32[64,128]{1,0:T(8,128)S(1)} %get-tuple-element.25.chosen, f32[1152,128]{1,0:T(8,128)S(1)} %get-tuple-element.33.packed, f32[64,256]{1,0:T(8,128)S(1)} %near_sums.1.near, f32[2048,512]{1,0:T(8,128)S(1)} %get-tuple-element.29.held.feats, ...), custom_call_target="tpu_custom_call" | custom-call | tf_op jit(solution)/shard_map/second_margin/pallas_call | solution.py:304
  44.8 3.8 %all-to-all-start = ((f32[128,1,1152]{2,1,0:T(1,128)}), f32[128,1,1152]{2,1,0:T(1,128)S(1)}, u32[]{:S(2)}, u32[]{:S(2)}) async-start(f32[128,1,1152]{2,1,0:T(1,128)} %bitcast.4), calls=%async_computation | async-start | bytes 1179648 | tf_op jit(solution)/shard_map/all_to_all | solution.py:699
  48.6 9.5 %all_weights.1 = f32[8192,128]{1,0:T(8,128)} custom-call(f32[8192,128]{1,0:T(8,128)} %weights.3, f32[288,256]{1,0:T(8,128)S(1)} %join.1.rest_0_, f32[288,256]{1,0:T(8,128)S(1)} %collective-permute-done.6.rest_1_, f32[288,256]{1,0:T(8,128)S(1)} %collective-permute-done.7.rest_2_, f32[288,256]{1,0:T(8,128)S(1)} %collective-permute-done.8.rest_3_, ...), custom_call_target="tpu_custom_call" | custom-call | tf_op jit(solution)/shard_map/all_weights/pallas_call | solution.py:393
  58.1 5.5 %all-to-all-done = f32[128,1,1152]{2,1,0:T(1,128)S(1)} async-done(((f32[128,1,1152]{2,1,0:T(1,128)}), f32[128,1,1152]{2,1,0:T(1,128)S(1)}, u32[]{:S(2)}, u32[]{:S(2)}) %all-to-all-start) | async-done | bytes 589856 | tf_op jit(solution)/shard_map/all_to_all | solution.py:699
  63.6 5.4 %owner_work.1 = (f32[128,128]{1,0:T(8,128)}, f32[32,128]{1,0:T(8,128)S(1)}, s32[16,1024]{1,0:T(8,128)S(1)}) custom-call(f32[1152,128]{1,0:T(8,128)S(1)} %bitcast.11, f32[32,128]{1,0:T(8,128)S(1)} %copy-done.1), custom_call_target="tpu_custom_call" | custom-call | tf_op jit(solution)/shard_map/owner_work/pallas_call | solution.py:595
  69.0 4.5 %all-to-all-start.1 = ((f32[128,1,128]{2,1,0:T(1,128)}), f32[128,1,128]{2,1,0:T(1,128)S(1)}, u32[]{:S(2)}, u32[]{:S(2)}) async-start(f32[128,1,128]{2,1,0:T(1,128)} %bitcast.7), calls=%async_computation.1 | async-start | bytes 131072 | tf_op jit(solution)/shard_map/all_to_all | solution.py:699
  73.4 1.0 %new_coefs.1 = f32[32,128]{1,0:T(8,128)} custom-call(f32[1152,128]{1,0:T(8,128)S(1)} %bitcast.12, f32[32,128]{1,0:T(8,128)S(1)} %copy-done.1, f32[32,128]{1,0:T(8,128)S(1)} %get-tuple-element.37.steps, s32[16,1024]{1,0:T(8,128)S(1)} %get-tuple-element.38.lines), custom_call_target="tpu_custom_call" | custom-call | tf_op jit(solution)/shard_map/new_coefs/pallas_call | solution.py:630
  74.5 8.8 %all-to-all-done.1 = f32[128,1,128]{2,1,0:T(1,128)S(1)} async-done(((f32[128,1,128]{2,1,0:T(1,128)}), f32[128,1,128]{2,1,0:T(1,128)S(1)}, u32[]{:S(2)}, u32[]{:S(2)}) %all-to-all-start.1) | async-done | bytes 65568 | tf_op jit(solution)/shard_map/all_to_all | solution.py:699
  83.3 0.9 %total_rows.1 = f32[1,512]{1,0:T(1,128)} custom-call(f32[128,128]{1,0:T(8,128)S(1)} %bitcast.13, s32[1,512]{1,0:T(1,128)S(1)} %get-tuple-element.40.slots), custom_call_target="tpu_custom_call" | custom-call | tf_op jit(solution)/shard_map/total_rows/pallas_call | solution.py:648
  (21 shorter events, 0.1 us)
Async XLA Ops:
  0.6 9.0 %copy-start.5 = (s32[16,4]{0,1:T(4,128)S(1)}, s32[16,4]{0,1:T(4,128)}, u32[]{:S(2)}) copy-start(s32[16,4]{0,1:T(4,128)} %param.9) | copy-start | bytes 772
  0.6 12.1 %copy-start.2 = (f32[2048]{0:T(1024)S(1)}, f32[2048]{0:T(1024)}, u32[]{:S(2)}) copy-start(f32[2048]{0:T(1024)} %param.11) | copy-start | bytes 24580
  0.7 12.1 %copy-start.3 = (f32[2048]{0:T(1024)S(1)}, f32[2048]{0:T(1024)}, u32[]{:S(2)}) copy-start(f32[2048]{0:T(1024)} %param.12) | copy-start | bytes 24580
  4.3 13.3 %copy-start = (f32[512,128]{1,0:T(8,128)S(1)}, f32[512,128]{1,0:T(8,128)}, u32[]{:S(2)}) copy-start(f32[512,128]{1,0:T(8,128)} %feats.3) | copy-start | bytes 786436
  4.4 13.3 %copy-start.4 = (s32[512]{0:T(512)S(1)}, s32[512]{0:T(512)}, u32[]{:S(2)}) copy-start(s32[512]{0:T(512)} %param.14) | copy-start | bytes 6148
  4.4 6.0 %collective-permute-start.2 = (f32[24,128]{1,0:T(8,128)S(1)}, f32[24,128]{1,0:T(8,128)S(1)}, u32[]{:S(2)}, u32[]{:S(2)}) collective-permute-start(f32[24,128]{1,0:T(8,128)S(1)} %get-tuple-element.31.m0.margin.rest_0_), channel_id=1, source_target_pairs={{0,2},{1,3},{2,0},{3,1},{4,6},{5,7},{6,4},{7,5},{8,10},{9,11},{10,... | collective-permute-start | bytes 36872 | tf_op jit(solution)/shard_map/ppermute | solution.py:658
  8.2 2.6 %collective-permute-start.1 = (f32[24,128]{1,0:T(8,128)S(1)}, f32[24,128]{1,0:T(8,128)S(1)}, u32[]{:S(2)}, u32[]{:S(2)}) collective-permute-start(f32[24,128]{1,0:T(8,128)S(1)} %get-tuple-element.31.m0.margin.rest_0_), channel_id=1, source_target_pairs={{0,3},{1,0},{2,1},{3,2},{4,7},{5,4},{6,5},{7,6},{8,11},{9,8},{10,9... | collective-permute-start | bytes 36872 | tf_op jit(solution)/shard_map/ppermute | solution.py:658
  9.0 3.8 %collective-permute-start = (f32[24,128]{1,0:T(8,128)S(1)}, f32[24,128]{1,0:T(8,128)S(1)}, u32[]{:S(2)}, u32[]{:S(2)}) collective-permute-start(f32[24,128]{1,0:T(8,128)S(1)} %get-tuple-element.31.m0.margin.rest_0_), channel_id=1, source_target_pairs={{0,1},{1,2},{2,3},{3,0},{4,5},{5,6},{6,7},{7,4},{8,9},{9,10},{10,1... | collective-permute-start | bytes 36872 | tf_op jit(solution)/shard_map/ppermute | solution.py:658
  14.0 4.8 %collective-permute-start.5 = (f32[72,256]{1,0:T(8,128)S(1)}, f32[72,256]{1,0:T(8,128)S(1)}, u32[]{:S(2)}, u32[]{:S(2)}) collective-permute-start(f32[72,256]{1,0:T(8,128)S(1)} %own_stats.1.refs_0_), channel_id=1, source_target_pairs={{0,24},{4,100},{8,0},{12,108},{16,8},{20,116},{24,16},{28,124},{32... | collective-permute-start | bytes 221192 | tf_op jit(solution)/shard_map/ppermute | solution.py:689
  16.5 4.8 %collective-permute-start.4 = (f32[72,256]{1,0:T(8,128)S(1)}, f32[72,256]{1,0:T(8,128)S(1)}, u32[]{:S(2)}, u32[]{:S(2)}) collective-permute-start(f32[72,256]{1,0:T(8,128)S(1)} %own_stats.1.refs_0_), channel_id=1, source_target_pairs={{0,16},{4,68},{8,24},{12,76},{16,0},{20,84},{24,8},{28,92},{32,48}... | collective-permute-start | bytes 221192 | tf_op jit(solution)/shard_map/ppermute | solution.py:689
  17.1 5.0 %collective-permute-start.3 = (f32[72,256]{1,0:T(8,128)S(1)}, f32[72,256]{1,0:T(8,128)S(1)}, u32[]{:S(2)}, u32[]{:S(2)}) collective-permute-start(f32[72,256]{1,0:T(8,128)S(1)} %own_stats.1.refs_0_), channel_id=1, source_target_pairs={{0,8},{4,36},{8,16},{12,44},{16,24},{20,52},{24,0},{28,60},{32,40}... | collective-permute-start | bytes 221192 | tf_op jit(solution)/shard_map/ppermute | solution.py:689
  22.1 10.9 %collective-permute-start.8 = (f32[288,256]{1,0:T(8,128)S(1)}, f32[288,256]{1,0:T(8,128)S(1)}, u32[]{:S(2)}, u32[]{:S(2)}) collective-permute-start(f32[288,256]{1,0:T(8,128)S(1)} %join.1.rest_0_), channel_id=1, source_target_pairs={{0,96},{4,28},{8,104},{12,4},{16,112},{20,12},{24,120},{28,20},{32... | collective-permute-start | bytes 884744 | tf_op jit(solution)/shard_map/ppermute | solution.py:693
  26.2 11.0 %collective-permute-start.7 = (f32[288,256]{1,0:T(8,128)S(1)}, f32[288,256]{1,0:T(8,128)S(1)}, u32[]{:S(2)}, u32[]{:S(2)}) collective-permute-start(f32[288,256]{1,0:T(8,128)S(1)} %join.1.rest_0_), channel_id=1, source_target_pairs={{0,64},{4,20},{8,72},{12,28},{16,80},{20,4},{24,88},{28,12},{32,96... | collective-permute-start | bytes 884744 | tf_op jit(solution)/shard_map/ppermute | solution.py:693
  26.2 11.9 %collective-permute-start.6 = (f32[288,256]{1,0:T(8,128)S(1)}, f32[288,256]{1,0:T(8,128)S(1)}, u32[]{:S(2)}, u32[]{:S(2)}) collective-permute-start(f32[288,256]{1,0:T(8,128)S(1)} %join.1.rest_0_), channel_id=1, source_target_pairs={{0,32},{4,12},{8,40},{12,20},{16,48},{20,28},{24,56},{28,4},{32,64... | collective-permute-start | bytes 884744 | tf_op jit(solution)/shard_map/ppermute | solution.py:693
  26.8 14.6 %collective-permute-start.9 = (f32[288,256]{1,0:T(8,128)S(1)}, f32[288,256]{1,0:T(8,128)S(1)}, u32[]{:S(2)}, u32[]{:S(2)}) collective-permute-start(f32[288,256]{1,0:T(8,128)S(1)} %join.1.rest_0_), channel_id=1, source_target_pairs={{0,4},{4,0},{8,12},{12,8},{16,20},{20,16},{24,28},{28,24},{32,36},... | collective-permute-start | bytes 884744 | tf_op jit(solution)/shard_map/ppermute | solution.py:694
  33.0 8.4 %collective-permute-start.12 = (f32[288,256]{1,0:T(8,128)S(1)}, f32[288,256]{1,0:T(8,128)S(1)}, u32[]{:S(2)}, u32[]{:S(2)}) collective-permute-start(f32[288,256]{1,0:T(8,128)S(1)} %collective-permute-done.8.rest_3_), channel_id=1, source_target_pairs={{0,4},{4,0},{8,12},{12,8},{16,20},{20,16},{24,28},{28,24},{32,36},... | collective-permute-start | bytes 884744 | tf_op jit(solution)/shard_map/ppermute | solution.py:694
  37.1 4.3 %collective-permute-start.11 = (f32[288,256]{1,0:T(8,128)S(1)}, f32[288,256]{1,0:T(8,128)S(1)}, u32[]{:S(2)}, u32[]{:S(2)}) collective-permute-start(f32[288,256]{1,0:T(8,128)S(1)} %collective-permute-done.7.rest_2_), channel_id=1, source_target_pairs={{0,4},{4,0},{8,12},{12,8},{16,20},{20,16},{24,28},{28,24},{32,36},... | collective-permute-start | bytes 884744 | tf_op jit(solution)/shard_map/ppermute | solution.py:694
  38.0 4.3 %collective-permute-start.10 = (f32[288,256]{1,0:T(8,128)S(1)}, f32[288,256]{1,0:T(8,128)S(1)}, u32[]{:S(2)}, u32[]{:S(2)}) collective-permute-start(f32[288,256]{1,0:T(8,128)S(1)} %collective-permute-done.6.rest_1_), channel_id=1, source_target_pairs={{0,4},{4,0},{8,12},{12,8},{16,20},{20,16},{24,28},{28,24},{32,36},... | collective-permute-start | bytes 884744 | tf_op jit(solution)/shard_map/ppermute | solution.py:694
  44.8 18.8 %all-to-all-start = ((f32[128,1,1152]{2,1,0:T(1,128)}), f32[128,1,1152]{2,1,0:T(1,128)S(1)}, u32[]{:S(2)}, u32[]{:S(2)}) async-start(f32[128,1,1152]{2,1,0:T(1,128)} %bitcast.4), calls=%async_computation | async-start | bytes 1179648 | tf_op jit(solution)/shard_map/all_to_all | solution.py:699
  48.6 15.0 %copy-start.1 = (f32[32,128]{1,0:T(8,128)S(1)}, f32[32,128]{1,0:T(8,128)}, u32[]{:S(2)}) copy-start(f32[32,128]{1,0:T(8,128)} %coefs.3) | copy-start | bytes 49156
  69.0 14.3 %all-to-all-start.1 = ((f32[128,1,128]{2,1,0:T(1,128)}), f32[128,1,128]{2,1,0:T(1,128)S(1)}, u32[]{:S(2)}, u32[]{:S(2)}) async-start(f32[128,1,128]{2,1,0:T(1,128)} %bitcast.7), calls=%async_computation.1 | async-start | bytes 131072 | tf_op jit(solution)/shard_map/all_to_all | solution.py:699

commit v4 on v3

--- a/solution.py
+++ b/solution.py
@@ -52,12 +52,25 @@
     return lax.dot_general(a, b, dims, preferred_element_type=F32)
 
 
-def dot_right(mask, x, parts, dims=NN):
-    return functools.reduce(jnp.add, [dot(mask, piece, dims) for piece in split(x, parts)])
-
-
-def dot_left(x, mask, parts, dims=NN):
-    return functools.reduce(jnp.add, [dot(piece, mask, dims) for piece in split(x, parts)])
+def dot_right(mask, x, parts):
+    return dot(jnp.concatenate([mask] * parts, axis=1), jnp.concatenate(split(x, parts), axis=0))
+
+
+def dot_left(values, mask, dims=NN):
+    pieces = [piece for x, parts in values for piece in split(x, parts)]
+    out = dot(jnp.concatenate(pieces, axis=0), mask, dims)
+    results, at = [], 0
+    for x, parts in values:
+        rows = x.shape[0]
+        results.append(
+            sum_pieces_of([out[at + p * rows : at + (p + 1) * rows, :] for p in range(parts)])
+        )
+        at += parts * rows
+    return results
+
+
+def sum_pieces_of(pieces):
+    return functools.reduce(jnp.add, pieces)
 
 
 def iota(shape, dim):
@@ -140,10 +153,10 @@
         out[TILES + a : TILES + a + 1, :] = owner[a : a + 1, :].astype(F32) * CAP + rank
     out[TILES + 4 :, :] = jnp.zeros((4, TILE), F32)
 
-    for copy in picked:
-        copy.wait()
     each = TILES // CHUNKS
     for c in range(CHUNKS):
+        for copy in picked[c * each * SLOTS : (c + 1) * each * SLOTS]:
+            copy.wait()
         copies[c].wait()
         for t in range(c * each, (c + 1) * each):
             sums[t * TILE : (t + 1) * TILE, :] = tile_margin(held, chosen, t)
@@ -284,14 +297,14 @@
     lanes = (iota((TILE, 128), 1) % 32).astype(F32)
     for t in range(0, TILES, 2):
         both = [tile_margin(feats, w, t), tile_margin(feats, w, t + 1)]
-        margin = dot_left(jnp.concatenate(both, axis=0), ones, 2)
+        margin = sum_pieces_of([dot(p, ones) for p in split(jnp.concatenate(both, axis=0), 2)])
         place = [
             lanes == jnp.broadcast_to(column[:, q : q + 1], (TILE, 128)) for q in (t, t + 1)
         ]
         placed = jnp.where(jnp.concatenate(place, axis=0), margin, 0.0)
         owners = jnp.concatenate([owner[t : t + 1, :], owner[t + 1 : t + 2, :]], axis=1)
         mask = onehot(iota((DEVICES, 2 * TILE), 0) == owners).astype(BF16)
-        term = dot_right(mask, placed, 2)
+        term = sum_pieces_of([dot(mask, p) for p in split(placed, 2)])
         result = term if result is None else result + term
     out[...] = packed[...]
     result = jnp.where(iota((DEVICES, 128), 1) < 32, result, 0.0)
@@ -515,9 +528,9 @@
     lines[8:16, :] = jnp.broadcast_to(rnk, (8, POS))
     by_rank = onehot((iota((GROUP, POS), 0) == rnk) & (mem >= 0))
     by_member = onehot((iota((128, POS), 0) % MEM) == mem).astype(BF16)
-    y = dot_left(by_rank * lab, by_member, 3, NT)
-    offset = dot_left(by_rank * fixed, by_member, 2, NT)
-    alive = dot(by_rank.astype(BF16), by_member, NT)
+    y, offset, alive = dot_left(
+        [(by_rank * lab, 3), (by_rank * fixed, 2), (by_rank, 1)], by_member, NT
+    )
     target = jnp.where(mem >= 0, rnk * MEM + mem, -1)
     feats = held[...].T
     pieces = jnp.concatenate(split(feats, 2), axis=0)
@@ -536,11 +549,11 @@
         folded = folded + own[:, 128 * b : 128 * (b + 1)]
     folded = folded + pltpu.roll(folded, 64, 1)
     s = folded + pltpu.roll(folded, 32, 1)
-    for delta in range(GROUP // 2 + 1):
-        p, q = delta % 4, delta // 4
-        for b in range(8):
-            o = (b + q) % 8
-            prod = turned[0, :, 128 * b : 128 * (b + 1)] * turned[p, :, 128 * o : 128 * (o + 1)]
+    for b in range(8):
+        block = turned[0, :, 128 * b : 128 * (b + 1)]
+        for delta in range(GROUP // 2 + 1):
+            p, o = delta % 4, (b + delta // 4) % 8
+            prod = block * turned[p, :, 128 * o : 128 * (o + 1)]
             diag[delta : delta + 1, 128 * b : 128 * (b + 1)] = jnp.sum(prod, axis=0, keepdims=True)
     for delta in range(GROUP // 2 + 1, GROUP):
         diag[delta : delta + 1, :] = pltpu.roll(
@@ -559,11 +572,16 @@
         error = (p - y) * alive
         d = jnp.sqrt(p * (1.0 - p) * alive)
         b = d * (gram_times(gram, error) + s)
-        for i in range(GROUP):
+        def formed(i):
             row = gram[i] * (d * d[i : i + 1, :])
-            work[i] = row + onehot(at == i)
+            cut = i // 8 * 8
+            one = row[cut : cut + 8, :] + onehot(iota((8, 128), 0) == i - cut)
+            return jnp.concatenate(
+                [row[r : r + 8, :] if r != cut else one for r in range(0, GROUP, 8)], axis=0
+            )
+
         for k in range(0, GROUP, PIVOTS):
-            panel = [work[k + q] for q in range(PIVOTS)]
+            panel = [work[k + q] if k else formed(q) for q in range(PIVOTS)]
             taken = []
             for q in range(PIVOTS):
                 row = panel[q]
@@ -574,7 +592,7 @@
                 b = b - b[k + q : k + q + 1, :] * scaled
                 taken.append((row, scaled))
             for i in range(k + PIVOTS, GROUP):
-                rest = work[i]
+                rest = work[i] if k else formed(i)
                 for row, scaled in taken:
                     rest = rest - row[i : i + 1, :] * scaled
                 work[i] = rest
@@ -583,7 +601,8 @@
         steps_total = u * 0.25 if sweep == 0 else steps_total + u * 0.5
     steps[...] = steps_total
     final = (s + offset) * 0.25
-    scores = jnp.sum(by_rank * dot_left(final, by_member, 2), axis=0, keepdims=True)
+    (scores,) = dot_left([(final, 2)], by_member)
+    scores = jnp.sum(by_rank * scores, axis=0, keepdims=True)
     for b in range(8):
         line = jnp.broadcast_to(scores[:, 128 * b : 128 * (b + 1)], (16, 128))
         back[16 * b : 16 * (b + 1), :] = jnp.where(
@@ -617,9 +636,8 @@
     mem = lines[0:1, :]
     by_rank = onehot((iota((GROUP, POS), 0) == lines[8:9, :]) & (mem >= 0))
     by_member = onehot((iota((128, POS), 0) % MEM) == mem)
-    line = jnp.sum(
-        by_rank * dot_left(steps[...] * 0.25, by_member.astype(BF16), 2), axis=0, keepdims=True
-    )
+    (line,) = dot_left([(steps[...] * 0.25, 2)], by_member.astype(BF16))
+    line = jnp.sum(by_rank * line, axis=0, keepdims=True)
     weighted = split(by_member[0:MEM, :] * line, 2)
     feats = split(held[...], 2)
     moved = dot(weighted[0], feats[0]) + dot(weighted[0], feats[1]) + dot(weighted[1], feats[0])
@@ -639,7 +657,7 @@
 def total_kernel(back, slots, out):
     slot = slots[...]
     mask = onehot(iota((DEVICES, OWN), 0) == slot // CAP).astype(BF16)
-    moved = dot_left(back[...].T, mask, 2)
+    (moved,) = dot_left([(back[...].T, 2)], mask)
     keep = (iota((128, OWN), 0) % CAP) == slot % CAP
     out[...] = jnp.sum(jnp.where(keep, moved, 0.0), axis=0, keepdims=True)
 

time: 84.4 us -> 83.7 us (level)
  no operation moved by 1% of the time
where the time goes in v4:
time: 83.7 us; the launch traced here: 83.5 us
  starting transfers between devices  34.5 us (41%)
  Pallas kernels  25.8 us (31%)
  waiting for transfers between devices  22.4 us (27%)
    all_to_all x2, waiting for transfers between devices, exchange(): lax.all_to_all(value, ('sample', 'feature'), split_axis=0, concat_axis=0,...  14.3 us
    ppermute x4, starting transfers between devices, gather_late(): lax.ppermute(v, 'sample', [(i, i ^ 1) for i in range(SAMPLES)])  12.6 us
    pallas_call x1, Pallas kernels, all_weights(): pl.pallas_call(weights_kernel, in_specs=[HBM] + [ANY] * 8, out_specs=HBM,...  9.48 us
    all_to_all x2, starting transfers between devices, exchange(): lax.all_to_all(value, ('sample', 'feature'), split_axis=0, concat_axis=0,...  8.24 us
    ppermute x3, starting transfers between devices, ring_feature(): lax.ppermute(value, 'feature', pairs[k])  5.29 us
    pallas_call x1, Pallas kernels, owner_work(): pl.pallas_call(owner_kernel, out_shape=[jax.ShapeDtypeStruct((DEVICES, 12...  5 us
    ppermute x3, starting transfers between devices, gather_late(): lax.ppermute(early, 'sample', sample_pairs(k, False))  4.77 us
    ppermute x3, starting transfers between devices, gather_early(): lax.ppermute(value, 'sample', sample_pairs(k, True))  3.62 us
  transfers between devices with their start and end apart: 15, of which 8 were waited for; matrix products, arithmetic and copies ran while one was open for 0% of the time, Pallas kernels for 15%

profile of v4, /device:TPU:1, one launch (start us, length us, event | category | flops | bytes accessed | tf_op | source)
XLA Modules:
  0.0 83.5 jit_solution(16073404861643216064)
XLA Ops:
  0.7 3.5 %first_margin.1 = (f32[24,128]{1,0:T(8,128)S(1)}, f32[64,128]{1,0:T(8,128)S(1)}, f32[2048,512]{1,0:T(8,128)S(1)}) custom-call(s32[4,16]{1,0:T(4,128)} %bitcast.19, s32[4,128]{1,0:T(4,128)} %bitcast.17, f32[2048,512]{1,0:T(8,128)} %feats.2, f32[8192,128]{1,0:T(8,128)} %weights.3), custom_call_target="tpu_custom_call" | custom-call | tf_op jit(solution)/shard_map/first_margin/pallas_call | solution.py:169
  4.2 3.8 %collective-permute-start.2 = (f32[24,128]{1,0:T(8,128)S(1)}, f32[24,128]{1,0:T(8,128)S(1)}, u32[]{:S(2)}, u32[]{:S(2)}) collective-permute-start(f32[24,128]{1,0:T(8,128)S(1)} %get-tuple-element.31.m0.margin.rest_0_), channel_id=1, source_target_pairs={{0,2},{1,3},{2,0},{3,1},{4,6},{5,7},{6,4},{7,5},{8,10},{9,11},{10,... | collective-permute-start | bytes 36872 | tf_op jit(solution)/shard_map/ppermute | solution.py:676
  8.1 0.8 collective-permute-start.1
  8.8 0.7 collective-permute-start
  9.5 0.7 block_tables.1
  10.2 0.4 collective-permute-done.1.m2.rest_2_
  10.7 1.9 %collective-permute-done.m1.rest_1_ = f32[24,128]{1,0:T(8,128)S(1)} collective-permute-done((f32[24,128]{1,0:T(8,128)S(1)}, f32[24,128]{1,0:T(8,128)S(1)}, u32[]{:S(2)}, u32[]{:S(2)}) %collective-permute-start) | collective-permute-done | bytes 12320 | tf_op jit(solution)/shard_map/ppermute | solution.py:676
  12.6 1.2 %own_stats.1.refs_0_ = f32[72,256]{1,0:T(8,128)S(1)} custom-call(f32[24,128]{1,0:T(8,128)S(1)} %get-tuple-element.31.m0.margin.rest_0_, f32[24,128]{1,0:T(8,128)S(1)} %collective-permute-done.m1.rest_1_, f32[24,128]{1,0:T(8,128)S(1)} %collective-permute-done.1.m2.rest_2_, f32[24,128]{1,0:T(8,128)S(1)} %collective-permute-done.2.m3.rest_3_, ...), custom_call_target="tpu_custom_call" | custom-call | tf_op jit(solution)/shard_map/own_stats/pallas_call | solution.py:239
  13.8 2.5 %collective-permute-start.5 = (f32[72,256]{1,0:T(8,128)S(1)}, f32[72,256]{1,0:T(8,128)S(1)}, u32[]{:S(2)}, u32[]{:S(2)}) collective-permute-start(f32[72,256]{1,0:T(8,128)S(1)} %own_stats.1.refs_0_), channel_id=1, source_target_pairs={{0,24},{4,100},{8,0},{12,108},{16,8},{20,116},{24,16},{28,124},{32... | collective-permute-start | bytes 221192 | tf_op jit(solution)/shard_map/ppermute | solution.py:707
  16.3 0.5 collective-permute-start.4
  16.8 0.6 collective-permute-start.3
  17.4 1.1 %pack_rows.1 = (f32[1152,128]{1,0:T(8,128)S(1)}, s32[1,512]{1,0:T(1,128)S(1)}) custom-call(f32[24,128]{1,0:T(8,128)S(1)} %get-tuple-element.31.m0.margin.rest_0_, s32[4,128]{1,0:T(4,128)S(1)} %bitcast.18, f32[16,128]{1,0:T(8,128)S(1)} %bitcast.15, f32[512,128]{1,0:T(8,128)S(1)} %copy-done), custom_call_target="tpu_custom_call" | custom-call | tf_op jit(solution)/shard_map/pack_rows/pallas_call | solution.py:452
  18.5 2.5 %collective-permute-done.4.refs_2_ = f32[72,256]{1,0:T(8,128)S(1)} collective-permute-done((f32[72,256]{1,0:T(8,128)S(1)}, f32[72,256]{1,0:T(8,128)S(1)}, u32[]{:S(2)}, u32[]{:S(2)}) %collective-permute-start.4) | collective-permute-done | bytes 73760 | tf_op jit(solution)/shard_map/ppermute | solution.py:707
  21.0 0.7 collective-permute-done.3.refs_1_
  21.8 4.1 %collective-permute-start.8 = (f32[288,256]{1,0:T(8,128)S(1)}, f32[288,256]{1,0:T(8,128)S(1)}, u32[]{:S(2)}, u32[]{:S(2)}) collective-permute-start(f32[288,256]{1,0:T(8,128)S(1)} %join.1.rest_0_), channel_id=1, source_target_pairs={{0,96},{4,28},{8,104},{12,4},{16,112},{20,12},{24,120},{28,20},{32... | collective-permute-start | bytes 884744 | tf_op jit(solution)/shard_map/ppermute | solution.py:711
  25.9 0.7 collective-permute-start.6
  26.6 4.5 %collective-permute-start.9 = (f32[288,256]{1,0:T(8,128)S(1)}, f32[288,256]{1,0:T(8,128)S(1)}, u32[]{:S(2)}, u32[]{:S(2)}) collective-permute-start(f32[288,256]{1,0:T(8,128)S(1)} %join.1.rest_0_), channel_id=1, source_target_pairs={{0,4},{4,0},{8,12},{12,8},{16,20},{20,16},{24,28},{28,24},{32,36},... | collective-permute-start | bytes 884744 | tf_op jit(solution)/shard_map/ppermute | solution.py:712
  31.1 1.6 %collective-permute-done.8.rest_3_ = f32[288,256]{1,0:T(8,128)S(1)} collective-permute-done((f32[288,256]{1,0:T(8,128)S(1)}, f32[288,256]{1,0:T(8,128)S(1)}, u32[]{:S(2)}, u32[]{:S(2)}) %collective-permute-start.8) | collective-permute-done | bytes 294944 | tf_op jit(solution)/shard_map/ppermute | solution.py:711
  32.7 4.1 %collective-permute-start.12 = (f32[288,256]{1,0:T(8,128)S(1)}, f32[288,256]{1,0:T(8,128)S(1)}, u32[]{:S(2)}, u32[]{:S(2)}) collective-permute-start(f32[288,256]{1,0:T(8,128)S(1)} %collective-permute-done.8.rest_3_), channel_id=1, source_target_pairs={{0,4},{4,0},{8,12},{12,8},{16,20},{20,16},{24,28},{28,24},{32,36},... | collective-permute-start | bytes 884744 | tf_op jit(solution)/shard_map/ppermute | solution.py:712
  36.9 0.9 %collective-permute-start.11 = (f32[288,256]{1,0:T(8,128)S(1)}, f32[288,256]{1,0:T(8,128)S(1)}, u32[]{:S(2)}, u32[]{:S(2)}) collective-permute-start(f32[288,256]{1,0:T(8,128)S(1)} %collective-permute-done.7.rest_2_), channel_id=1, source_target_pairs={{0,4},{4,0},{8,12},{12,8},{16,20},{20,16},{24,28},{28,24},{32,36},... | collective-permute-start | bytes 884744 | tf_op jit(solution)/shard_map/ppermute | solution.py:712
  37.8 3.1 %collective-permute-start.10 = (f32[288,256]{1,0:T(8,128)S(1)}, f32[288,256]{1,0:T(8,128)S(1)}, u32[]{:S(2)}, u32[]{:S(2)}) collective-permute-start(f32[288,256]{1,0:T(8,128)S(1)} %collective-permute-done.6.rest_1_), channel_id=1, source_target_pairs={{0,4},{4,0},{8,12},{12,8},{16,20},{20,16},{24,28},{28,24},{32,36},... | collective-permute-start | bytes 884744 | tf_op jit(solution)/shard_map/ppermute | solution.py:712
  40.8 0.3 near_sums.1.near
  41.1 0.9 %collective-permute-done.10.rest_5_ = f32[288,256]{1,0:T(8,128)S(1)} collective-permute-done((f32[288,256]{1,0:T(8,128)S(1)}, f32[288,256]{1,0:T(8,128)S(1)}, u32[]{:S(2)}, u32[]{:S(2)}) %collective-permute-start.10) | collective-permute-done | bytes 294944 | tf_op jit(solution)/shard_map/ppermute | solution.py:712
  42.0 2.5 %second_margin.1 = f32[1152,128]{1,0:T(8,128)} custom-call(f32[64,128]{1,0:T(8,128)S(1)} %get-tuple-element.24.own_ids, f32[64,128]{1,0:T(8,128)S(1)} %get-tuple-element.25.chosen, f32[1152,128]{1,0:T(8,128)S(1)} %get-tuple-element.33.packed, f32[64,256]{1,0:T(8,128)S(1)} %near_sums.1.near, f32[2048,512]{1,0:T(8,128)S(1)} %get-tuple-element.29.held.feats, ...), custom_call_target="tpu_custom_call" | custom-call | tf_op jit(solution)/shard_map/second_margin/pallas_call | solution.py:317
  44.6 3.8 %all-to-all-start = ((f32[128,1,1152]{2,1,0:T(1,128)}), f32[128,1,1152]{2,1,0:T(1,128)S(1)}, u32[]{:S(2)}, u32[]{:S(2)}) async-start(f32[128,1,1152]{2,1,0:T(1,128)} %bitcast.4), calls=%async_computation | async-start | bytes 1179648 | tf_op jit(solution)/shard_map/all_to_all | solution.py:717
  48.4 9.5 %all_weights.1 = f32[8192,128]{1,0:T(8,128)} custom-call(f32[8192,128]{1,0:T(8,128)} %weights.3, f32[288,256]{1,0:T(8,128)S(1)} %join.1.rest_0_, f32[288,256]{1,0:T(8,128)S(1)} %collective-permute-done.6.rest_1_, f32[288,256]{1,0:T(8,128)S(1)} %collective-permute-done.7.rest_2_, f32[288,256]{1,0:T(8,128)S(1)} %collective-permute-done.8.rest_3_, ...), custom_call_target="tpu_custom_call" | custom-call | tf_op jit(solution)/shard_map/all_weights/pallas_call | solution.py:406
  57.9 5.5 %all-to-all-done = f32[128,1,1152]{2,1,0:T(1,128)S(1)} async-done(((f32[128,1,1152]{2,1,0:T(1,128)}), f32[128,1,1152]{2,1,0:T(1,128)S(1)}, u32[]{:S(2)}, u32[]{:S(2)}) %all-to-all-start) | async-done | bytes 589856 | tf_op jit(solution)/shard_map/all_to_all | solution.py:717
  63.3 5.0 %owner_work.1 = (f32[128,128]{1,0:T(8,128)}, f32[32,128]{1,0:T(8,128)S(1)}, s32[16,1024]{1,0:T(8,128)S(1)}) custom-call(f32[1152,128]{1,0:T(8,128)S(1)} %bitcast.11, f32[32,128]{1,0:T(8,128)S(1)} %copy-done.1), custom_call_target="tpu_custom_call" | custom-call | tf_op jit(solution)/shard_map/owner_work/pallas_call | solution.py:614
  68.3 4.5 %all-to-all-start.1 = ((f32[128,1,128]{2,1,0:T(1,128)}), f32[128,1,128]{2,1,0:T(1,128)S(1)}, u32[]{:S(2)}, u32[]{:S(2)}) async-start(f32[128,1,128]{2,1,0:T(1,128)} %bitcast.7), calls=%async_computation.1 | async-start | bytes 131072 | tf_op jit(solution)/shard_map/all_to_all | solution.py:717
  72.8 1.0 %new_coefs.1 = f32[32,128]{1,0:T(8,128)} custom-call(f32[1152,128]{1,0:T(8,128)S(1)} %bitcast.12, f32[32,128]{1,0:T(8,128)S(1)} %copy-done.1, f32[32,128]{1,0:T(8,128)S(1)} %get-tuple-element.37.steps, s32[16,1024]{1,0:T(8,128)S(1)} %get-tuple-element.38.lines), custom_call_target="tpu_custom_call" | custom-call | tf_op jit(solution)/shard_map/new_coefs/pallas_call | solution.py:648
  73.8 8.9 %all-to-all-done.1 = f32[128,1,128]{2,1,0:T(1,128)S(1)} async-done(((f32[128,1,128]{2,1,0:T(1,128)}), f32[128,1,128]{2,1,0:T(1,128)S(1)}, u32[]{:S(2)}, u32[]{:S(2)}) %all-to-all-start.1) | async-done | bytes 65568 | tf_op jit(solution)/shard_map/all_to_all | solution.py:717
  82.7 0.9 %total_rows.1 = f32[1,512]{1,0:T(1,128)} custom-call(f32[128,128]{1,0:T(8,128)S(1)} %bitcast.13, s32[1,512]{1,0:T(1,128)S(1)} %get-tuple-element.40.slots), custom_call_target="tpu_custom_call" | custom-call | tf_op jit(solution)/shard_map/total_rows/pallas_call | solution.py:666
  (21 shorter events, 0.1 us)
Async XLA Ops:
  0.6 8.9 %copy-start.5 = (s32[16,4]{0,1:T(4,128)S(1)}, s32[16,4]{0,1:T(4,128)}, u32[]{:S(2)}) copy-start(s32[16,4]{0,1:T(4,128)} %param.9) | copy-start | bytes 772
  0.6 11.9 %copy-start.2 = (f32[2048]{0:T(1024)S(1)}, f32[2048]{0:T(1024)}, u32[]{:S(2)}) copy-start(f32[2048]{0:T(1024)} %param.11) | copy-start | bytes 24580
  0.7 11.9 %copy-start.3 = (f32[2048]{0:T(1024)S(1)}, f32[2048]{0:T(1024)}, u32[]{:S(2)}) copy-start(f32[2048]{0:T(1024)} %param.12) | copy-start | bytes 24580
  4.2 13.2 %copy-start = (f32[512,128]{1,0:T(8,128)S(1)}, f32[512,128]{1,0:T(8,128)}, u32[]{:S(2)}) copy-start(f32[512,128]{1,0:T(8,128)} %feats.3) | copy-start | bytes 786436
  4.2 13.2 %copy-start.4 = (s32[512]{0:T(512)S(1)}, s32[512]{0:T(512)}, u32[]{:S(2)}) copy-start(s32[512]{0:T(512)} %param.14) | copy-start | bytes 6148
  4.2 6.0 %collective-permute-start.2 = (f32[24,128]{1,0:T(8,128)S(1)}, f32[24,128]{1,0:T(8,128)S(1)}, u32[]{:S(2)}, u32[]{:S(2)}) collective-permute-start(f32[24,128]{1,0:T(8,128)S(1)} %get-tuple-element.31.m0.margin.rest_0_), channel_id=1, source_target_pairs={{0,2},{1,3},{2,0},{3,1},{4,6},{5,7},{6,4},{7,5},{8,10},{9,11},{10,... | collective-permute-start | bytes 36872 | tf_op jit(solution)/shard_map/ppermute | solution.py:676
  8.1 2.6 %collective-permute-start.1 = (f32[24,128]{1,0:T(8,128)S(1)}, f32[24,128]{1,0:T(8,128)S(1)}, u32[]{:S(2)}, u32[]{:S(2)}) collective-permute-start(f32[24,128]{1,0:T(8,128)S(1)} %get-tuple-element.31.m0.margin.rest_0_), channel_id=1, source_target_pairs={{0,3},{1,0},{2,1},{3,2},{4,7},{5,4},{6,5},{7,6},{8,11},{9,8},{10,9... | collective-permute-start | bytes 36872 | tf_op jit(solution)/shard_map/ppermute | solution.py:676
  8.8 3.8 %collective-permute-start = (f32[24,128]{1,0:T(8,128)S(1)}, f32[24,128]{1,0:T(8,128)S(1)}, u32[]{:S(2)}, u32[]{:S(2)}) collective-permute-start(f32[24,128]{1,0:T(8,128)S(1)} %get-tuple-element.31.m0.margin.rest_0_), channel_id=1, source_target_pairs={{0,1},{1,2},{2,3},{3,0},{4,5},{5,6},{6,7},{7,4},{8,9},{9,10},{10,1... | collective-permute-start | bytes 36872 | tf_op jit(solution)/shard_map/ppermute | solution.py:676
  13.8 4.8 %collective-permute-start.5 = (f32[72,256]{1,0:T(8,128)S(1)}, f32[72,256]{1,0:T(8,128)S(1)}, u32[]{:S(2)}, u32[]{:S(2)}) collective-permute-start(f32[72,256]{1,0:T(8,128)S(1)} %own_stats.1.refs_0_), channel_id=1, source_target_pairs={{0,24},{4,100},{8,0},{12,108},{16,8},{20,116},{24,16},{28,124},{32... | collective-permute-start | bytes 221192 | tf_op jit(solution)/shard_map/ppermute | solution.py:707
  16.3 4.8 %collective-permute-start.4 = (f32[72,256]{1,0:T(8,128)S(1)}, f32[72,256]{1,0:T(8,128)S(1)}, u32[]{:S(2)}, u32[]{:S(2)}) collective-permute-start(f32[72,256]{1,0:T(8,128)S(1)} %own_stats.1.refs_0_), channel_id=1, source_target_pairs={{0,16},{4,68},{8,24},{12,76},{16,0},{20,84},{24,8},{28,92},{32,48}... | collective-permute-start | bytes 221192 | tf_op jit(solution)/shard_map/ppermute | solution.py:707
  16.8 5.0 %collective-permute-start.3 = (f32[72,256]{1,0:T(8,128)S(1)}, f32[72,256]{1,0:T(8,128)S(1)}, u32[]{:S(2)}, u32[]{:S(2)}) collective-permute-start(f32[72,256]{1,0:T(8,128)S(1)} %own_stats.1.refs_0_), channel_id=1, source_target_pairs={{0,8},{4,36},{8,16},{12,44},{16,24},{20,52},{24,0},{28,60},{32,40}... | collective-permute-start | bytes 221192 | tf_op jit(solution)/shard_map/ppermute | solution.py:707
  21.8 10.9 %collective-permute-start.8 = (f32[288,256]{1,0:T(8,128)S(1)}, f32[288,256]{1,0:T(8,128)S(1)}, u32[]{:S(2)}, u32[]{:S(2)}) collective-permute-start(f32[288,256]{1,0:T(8,128)S(1)} %join.1.rest_0_), channel_id=1, source_target_pairs={{0,96},{4,28},{8,104},{12,4},{16,112},{20,12},{24,120},{28,20},{32... | collective-permute-start | bytes 884744 | tf_op jit(solution)/shard_map/ppermute | solution.py:711
  25.9 11.0 %collective-permute-start.7 = (f32[288,256]{1,0:T(8,128)S(1)}, f32[288,256]{1,0:T(8,128)S(1)}, u32[]{:S(2)}, u32[]{:S(2)}) collective-permute-start(f32[288,256]{1,0:T(8,128)S(1)} %join.1.rest_0_), channel_id=1, source_target_pairs={{0,64},{4,20},{8,72},{12,28},{16,80},{20,4},{24,88},{28,12},{32,96... | collective-permute-start | bytes 884744 | tf_op jit(solution)/shard_map/ppermute | solution.py:711
  25.9 11.9 %collective-permute-start.6 = (f32[288,256]{1,0:T(8,128)S(1)}, f32[288,256]{1,0:T(8,128)S(1)}, u32[]{:S(2)}, u32[]{:S(2)}) collective-permute-start(f32[288,256]{1,0:T(8,128)S(1)} %join.1.rest_0_), channel_id=1, source_target_pairs={{0,32},{4,12},{8,40},{12,20},{16,48},{20,28},{24,56},{28,4},{32,64... | collective-permute-start | bytes 884744 | tf_op jit(solution)/shard_map/ppermute | solution.py:711
  26.6 14.6 %collective-permute-start.9 = (f32[288,256]{1,0:T(8,128)S(1)}, f32[288,256]{1,0:T(8,128)S(1)}, u32[]{:S(2)}, u32[]{:S(2)}) collective-permute-start(f32[288,256]{1,0:T(8,128)S(1)} %join.1.rest_0_), channel_id=1, source_target_pairs={{0,4},{4,0},{8,12},{12,8},{16,20},{20,16},{24,28},{28,24},{32,36},... | collective-permute-start | bytes 884744 | tf_op jit(solution)/shard_map/ppermute | solution.py:712
  32.7 8.4 %collective-permute-start.12 = (f32[288,256]{1,0:T(8,128)S(1)}, f32[288,256]{1,0:T(8,128)S(1)}, u32[]{:S(2)}, u32[]{:S(2)}) collective-permute-start(f32[288,256]{1,0:T(8,128)S(1)} %collective-permute-done.8.rest_3_), channel_id=1, source_target_pairs={{0,4},{4,0},{8,12},{12,8},{16,20},{20,16},{24,28},{28,24},{32,36},... | collective-permute-start | bytes 884744 | tf_op jit(solution)/shard_map/ppermute | solution.py:712
  36.9 4.3 %collective-permute-start.11 = (f32[288,256]{1,0:T(8,128)S(1)}, f32[288,256]{1,0:T(8,128)S(1)}, u32[]{:S(2)}, u32[]{:S(2)}) collective-permute-start(f32[288,256]{1,0:T(8,128)S(1)} %collective-permute-done.7.rest_2_), channel_id=1, source_target_pairs={{0,4},{4,0},{8,12},{12,8},{16,20},{20,16},{24,28},{28,24},{32,36},... | collective-permute-start | bytes 884744 | tf_op jit(solution)/shard_map/ppermute | solution.py:712
  37.8 4.3 %collective-permute-start.10 = (f32[288,256]{1,0:T(8,128)S(1)}, f32[288,256]{1,0:T(8,128)S(1)}, u32[]{:S(2)}, u32[]{:S(2)}) collective-permute-start(f32[288,256]{1,0:T(8,128)S(1)} %collective-permute-done.6.rest_1_), channel_id=1, source_target_pairs={{0,4},{4,0},{8,12},{12,8},{16,20},{20,16},{24,28},{28,24},{32,36},... | collective-permute-start | bytes 884744 | tf_op jit(solution)/shard_map/ppermute | solution.py:712
  44.6 18.8 %all-to-all-start = ((f32[128,1,1152]{2,1,0:T(1,128)}), f32[128,1,1152]{2,1,0:T(1,128)S(1)}, u32[]{:S(2)}, u32[]{:S(2)}) async-start(f32[128,1,1152]{2,1,0:T(1,128)} %bitcast.4), calls=%async_computation | async-start | bytes 1179648 | tf_op jit(solution)/shard_map/all_to_all | solution.py:717
  48.4 15.0 %copy-start.1 = (f32[32,128]{1,0:T(8,128)S(1)}, f32[32,128]{1,0:T(8,128)}, u32[]{:S(2)}) copy-start(f32[32,128]{1,0:T(8,128)} %coefs.3) | copy-start | bytes 49156
  68.3 14.3 %all-to-all-start.1 = ((f32[128,1,128]{2,1,0:T(1,128)}), f32[128,1,128]{2,1,0:T(1,128)S(1)}, u32[]{:S(2)}, u32[]{:S(2)}) async-start(f32[128,1,128]{2,1,0:T(1,128)} %bitcast.7), calls=%async_computation.1 | async-start | bytes 131072 | tf_op jit(solution)/shard_map/all_to_all | solution.py:717
